TPU v7x, 32 devices: a whole 2x2x4 slice. The times are simulated.
32 devices in a mesh: fsdp: 8 (over y, x, core), tp: 4 (over z).
Axes of the slice: x: 2, y: 2, z: 4, core: 2. Of those that a mesh axis runs over, the one named last changes fastest.
Arguments:
- tokens: bfloat16 [512, 5120], P(('fsdp', 'tp')), may hold values from -6 to 6
- tile_values: bfloat16 [128, 840, 128], P('fsdp', 'tp'), may hold values from -0.15625 to 0.15625
- tile_row: int32 [4, 210], P('tp'), may hold values from 0 to 39, as said below
- tile_col: int32 [4, 210], P('tp'), may hold values from 0 to 20, as said below
- grad_act: bfloat16 [512, 10752], P('fsdp', 'tp'), may hold values from -6 to 6
Outputs:
- act: bfloat16 [512, 10752], P('fsdp', 'tp')
- grad_tokens: bfloat16 [512, 5120], P(('fsdp', 'tp'))
- grad_tiles: float32 [128, 840, 128], P('fsdp', 'tp')
Inputs may be any that keep to these rules, and one draw needn't show every extreme that they name: Within each of the 4 shards the pairs (tile_row, tile_col) of its 210 slots are distinct; every shard has one slot at tile row 39 and tile column 20. `tile_col`: the pairs are those of tile_row.
All inputs are finite; a program needn't handle non-finite values.
Results may differ from a plain program's by a relative error of at most 0.0095.
Values may be sent and summed in bfloat16 or wider, within the bound.
No kernel may reach another device: no remote copies, remote signals or barrier semaphores. Data moves between devices by JAX's collectives and lax.ppermute only.
A program may use at most 128 MiB of HBM per device.

v0:
```python
import math

import jax
import jax.numpy as jnp
from jax import lax
from jax.sharding import PartitionSpec as P

SQRT_TWO_PI = 0.7978845608028654
CUBIC_COEF = 0.044715


def gelu_pair(pre_act):
    gelu_inner = SQRT_TWO_PI * (pre_act + CUBIC_COEF * pre_act * pre_act * pre_act)
    tanh_inner = jnp.tanh(gelu_inner)
    act_value = 0.5 * pre_act * (1.0 + tanh_inner)
    act_slope = 0.5 * (1.0 + tanh_inner) + 0.5 * pre_act * (
        1.0 - tanh_inner * tanh_inner
    ) * SQRT_TWO_PI * (1.0 + 3.0 * CUBIC_COEF * pre_act * pre_act)
    return (act_value, act_slope)


def local(tokens, tile_values, tile_row, tile_col, grad_act):
    highest = lax.Precision.HIGHEST
    gathered = lax.all_gather(tokens, "tp", axis=0, tiled=True)
    group_rows = gathered.shape[0]
    tile_width = tile_values.shape[2]
    row_tiles = gathered.shape[1] // tile_width
    col_tiles = grad_act.shape[1] // tile_width
    block_rows = math.gcd(group_rows, 32)
    block_count = group_rows // block_rows
    row_index = tile_row[0]
    col_index = tile_col[0]
    row_onehot = (row_index[:, None] == jnp.arange(row_tiles, dtype=jnp.int32)[None, :]).astype(
        jnp.float32
    )
    col_onehot = (col_index[:, None] == jnp.arange(col_tiles, dtype=jnp.int32)[None, :]).astype(
        jnp.float32
    )
    token_blocks = gathered.reshape(block_count, block_rows, row_tiles, tile_width)

    def forward_block(token_block, tiles_now):
        chosen = jnp.take(token_block, row_index, axis=1)
        product = jnp.einsum("rnk,knj->rnj", chosen, tiles_now, preferred_element_type=jnp.float32)
        return jnp.einsum("rnj,nc->rcj", product, col_onehot, precision=highest)

    whole_tiles = lax.all_gather(tile_values, "fsdp", axis=0, tiled=True)
    hidden = lax.map(lambda token_block: forward_block(token_block, whole_tiles), token_blocks)
    hidden = hidden.reshape(group_rows, col_tiles, tile_width)
    act_value, act_slope = gelu_pair(hidden)
    act = act_value.astype(jnp.bfloat16).reshape(group_rows, col_tiles * tile_width)
    hidden_grad = (
        grad_act.reshape(group_rows, col_tiles, tile_width).astype(jnp.float32) * act_slope
    ).astype(jnp.bfloat16)
    grad_blocks = hidden_grad.reshape(block_count, block_rows, col_tiles, tile_width)
    grad_scale = 1.0 / math.sqrt(group_rows * lax.axis_size("fsdp"))
    slot_count = row_index.shape[0]

    def add_block(total, pair):
        token_block, grad_block = pair
        chosen = jnp.take(token_block, row_index, axis=1)
        grad_chosen = jnp.take(grad_block, col_index, axis=1)
        return (
            total
            + jnp.einsum("rnk,rnj->knj", chosen, grad_chosen, preferred_element_type=jnp.float32),
            None,
        )

    total, _ = lax.scan(
        add_block,
        jnp.zeros(
            (tile_values.shape[0] * lax.axis_size("fsdp"), slot_count, tile_width), jnp.float32
        ),
        (token_blocks, grad_blocks),
    )
    grad_tiles = lax.psum_scatter(total * grad_scale, "fsdp", scatter_dimension=0, tiled=True)

    def backward_block(grad_block, tiles_now):
        grad_chosen = jnp.take(grad_block, col_index, axis=1)
        back_product = jnp.einsum(
            "rnj,knj->rnk", grad_chosen, tiles_now, preferred_element_type=jnp.float32
        )
        return jnp.einsum("rnk,nq->rqk", back_product, row_onehot, precision=highest).astype(
            jnp.bfloat16
        )

    partial_value = lax.map(lambda grad_block: backward_block(grad_block, whole_tiles), grad_blocks)
    partial_value = lax.optimization_barrier(
        partial_value.reshape(group_rows, row_tiles * tile_width)
    )
    summed = lax.psum_scatter(
        partial_value.astype(jnp.float32).astype(jnp.bfloat16),
        "tp",
        scatter_dimension=0,
        tiled=True,
    )
    return (act, summed, grad_tiles)


def solution(mesh):
    in_specs = (
        P(("fsdp", "tp"), None),
        P("fsdp", "tp", None),
        P("tp", None),
        P("tp", None),
        P("fsdp", "tp"),
    )
    out_specs = (P("fsdp", "tp"), P(("fsdp", "tp"), None), P("fsdp", "tp", None))
    return jax.shard_map(local, mesh=mesh, in_specs=in_specs, out_specs=out_specs, check_vma=False)
```

profile of v0, /device:TPU:0, one launch (start us, length us, event | category | flops | bytes accessed | tf_op | source)
XLA Modules:
  0.0 268.4 jit_solution(7332669669897467790)
XLA Ops:
  8.0 20.0 %all_gather.6 = bf16[64,5120]{1,0:T(8,128)(2,1)S(1)} all-gather(bf16[16,5120]{1,0:T(8,128)(2,1)} %param.15), channel_id=1, replica_groups=mesh['fsdp'=8,'tp'=4] {'tp'}, dimensions={0}, use_global_device_ids=true | all-gather | bytes 819200 | tf_op jit(solution)/shard_map/all_gather | solution.py:24
  28.2 1.1 reshape.37
  29.2 32.7 %all-gather.2.cloned.1.call-done = bf16[128,210,128]{2,0,1:T(8,128)(2,1)} async-done(((bf16[16,210,128]{2,0,1:T(8,128)(2,1)}), bf16[128,210,128]{2,0,1:T(8,128)(2,1)}) %all-gather.2.cloned.1.call-update) | async-done | bytes 6881296 | tf_op jit(solution)/shard_map/all_gather | solution.py:46
  61.9 20.3 %while.33 = (s32[]{:T(128)}, f32[2,32,21,128]{3,2,1,0:T(8,128)}, bf16[2,32,40,128]{3,1,2,0:T(8,128)(2,1)S(1)}, s32[210]{0:T(256)S(1)}, bf16[128,210,128]{2,0,1:T(8,128)(2,1)}, /*index=5*/s32[210]{0:T(256)S(1)}, s32[]{:T(128)}) while((s32[]{:T(128)}, f32[2,32,21,128]{3,2,1,0:T(8,128)}, bf16[2,32,40,128]{3,1,2,0:T(8,128)(2,1)S(1)}, ...), condition=%wide.region_1.0_spmd.clone, body=%wide.region_0.2_spmd.clone.sunk | while | flops 437833152 | bytes 25487008 | solution.py:47
  62.0 0.9 gather_fusion
  62.9 4.2 %convolution_bitcast_fusion.4 = f32[32,210,128]{2,0,1:T(8,128)S(1)} fusion(bf16[128,210,128]{2,0,1:T(8,128)(2,1)} %get-tuple-element.362, bf16[210,32,128]{2,1,0:T(8,128)(2,1)S(1)} %gather_fusion, pred[210]{0:T(512)(128)(4,1)S(1)} %compare_and_fusion.7), kind=kOutput, calls=%fused_computation.8.clone.1 | convolution fusion | flops 221061120 | bytes 12042450 | tf_op jit(solution)/shard_map/while/body/eval_jaxpr/rnk,knj->rnj/dot_general | solution.py:43
  67.2 4.0 %fusion.77 = f32[2,32,21,128]{3,2,1,0:T(8,128)S(1)} fusion(f32[2,32,21,128]{3,2,1,0:T(8,128)S(1)} %copy-done, s32[]{:T(128)S(6)} %copy.49, f32[32,210,128]{2,0,1:T(8,128)S(1)} %convolution_bitcast_fusion.4, s32[210]{0:T(256)S(1)} %get-tuple-element.363), kind=kOutput, calls=%fused_computation.13.clone.1 | convolution fusion | flops 216769136 | bytes 3834884 | tf_op jit(solution)/shard_map/while/body/eval_jaxpr/rnj,nc->rcj/dot_general | solution.py:44
  71.1 0.9 copy-done.1
  72.1 0.9 gather_fusion
  73.1 4.2 %convolution_bitcast_fusion.4 = f32[32,210,128]{2,0,1:T(8,128)S(1)} fusion(bf16[128,210,128]{2,0,1:T(8,128)(2,1)} %get-tuple-element.362, bf16[210,32,128]{2,1,0:T(8,128)(2,1)S(1)} %gather_fusion, pred[210]{0:T(512)(128)(4,1)S(1)} %compare_and_fusion.7), kind=kOutput, calls=%fused_computation.8.clone.1 | convolution fusion | flops 221061120 | bytes 12042450 | tf_op jit(solution)/shard_map/while/body/eval_jaxpr/rnk,knj->rnj/dot_general | solution.py:43
  77.3 4.0 %fusion.77 = f32[2,32,21,128]{3,2,1,0:T(8,128)S(1)} fusion(f32[2,32,21,128]{3,2,1,0:T(8,128)S(1)} %copy-done, s32[]{:T(128)S(6)} %copy.49, f32[32,210,128]{2,0,1:T(8,128)S(1)} %convolution_bitcast_fusion.4, s32[210]{0:T(256)S(1)} %get-tuple-element.363), kind=kOutput, calls=%fused_computation.13.clone.1 | convolution fusion | flops 216769136 | bytes 3834884 | tf_op jit(solution)/shard_map/while/body/eval_jaxpr/rnj,nc->rcj/dot_general | solution.py:44
  82.2 1.9 fusion.53
  84.1 24.7 %while.34 = (s32[]{:T(128)}, bf16[2,32,40,128]{3,2,1,0:T(8,128)(2,1)}, bf16[2,32,21,128]{3,1,2,0:T(8,128)(2,1)S(1)}, s32[210]{0:T(256)S(1)}, bf16[128,210,128]{2,0,1:T(8,128)(2,1)}, /*index=5*/s32[210]{0:T(256)S(1)}, s32[]{:T(128)}) while((s32[]{:T(128)}, bf16[2,32,40,128]{3,2,1,0:T(8,128)(2,1)}, ...), condition=%wide.region_3.6_spmd.clone, body=%wide.region_2.5_spmd.clone.sunk | while | flops 634121472 | bytes 24848032 | solution.py:86
  84.4 0.9 gather_fusion.1
  85.3 6.0 %convolution_bitcast_fusion.5 = f32[32,210,128]{2,0,1:T(8,128)S(1)} fusion(bf16[128,210,128]{2,0,1:T(8,128)(2,1)} %get-tuple-element.383, bf16[210,32,128]{2,1,0:T(8,128)(2,1)S(1)} %gather_fusion.1, pred[210]{0:T(512)(128)(4,1)S(1)} %compare_and_fusion.8), kind=kOutput, calls=%fused_computation.26.clone.1 | convolution fusion | flops 221061120 | bytes 12042450 | tf_op jit(solution)/shard_map/while/body/eval_jaxpr/rnj,knj->rnk/dot_general | solution.py:79
  91.3 4.4 %fusion.82 = bf16[2,32,40,128]{3,2,1,0:T(8,128)(2,1)S(1)} fusion(bf16[2,32,40,128]{3,2,1,0:T(8,128)(2,1)S(1)} %copy-done.3, s32[]{:T(128)S(6)} %copy.55, f32[32,210,128]{2,0,1:T(8,128)S(1)} %convolution_bitcast_fusion.5, s32[210]{0:T(256)S(1)} %get-tuple-element.384), kind=kOutput, calls=%fused_computation.32.clone.1 | convolution fusion | flops 413057440 | bytes 3769348 | tf_op jit(solution)/shard_map/while/body/eval_jaxpr/rnk,nq->rqk/dot_general | solution.py:82
  96.6 0.9 gather_fusion.1
  97.6 6.0 %convolution_bitcast_fusion.5 = f32[32,210,128]{2,0,1:T(8,128)S(1)} fusion(bf16[128,210,128]{2,0,1:T(8,128)(2,1)} %get-tuple-element.383, bf16[210,32,128]{2,1,0:T(8,128)(2,1)S(1)} %gather_fusion.1, pred[210]{0:T(512)(128)(4,1)S(1)} %compare_and_fusion.8), kind=kOutput, calls=%fused_computation.26.clone.1 | convolution fusion | flops 221061120 | bytes 12042450 | tf_op jit(solution)/shard_map/while/body/eval_jaxpr/rnj,knj->rnk/dot_general | solution.py:79
  103.5 4.4 %fusion.82 = bf16[2,32,40,128]{3,2,1,0:T(8,128)(2,1)S(1)} fusion(bf16[2,32,40,128]{3,2,1,0:T(8,128)(2,1)S(1)} %copy-done.3, s32[]{:T(128)S(6)} %copy.55, f32[32,210,128]{2,0,1:T(8,128)S(1)} %convolution_bitcast_fusion.5, s32[210]{0:T(256)S(1)} %get-tuple-element.384), kind=kOutput, calls=%fused_computation.32.clone.1 | convolution fusion | flops 413057440 | bytes 3769348 | tf_op jit(solution)/shard_map/while/body/eval_jaxpr/rnk,nq->rqk/dot_general | solution.py:82
  108.8 2.0 copy.40
  111.0 24.3 %while.35 = (s32[]{:T(128)}, f32[128,210,128]{0,2,1:T(8,128)}, bf16[2,32,21,128]{3,1,2,0:T(8,128)(2,1)S(1)}, s32[210]{0:T(256)S(1)}, bf16[2,32,40,128]{3,1,2,0:T...) while((s32[]{:T(128)}, f32[128,210,128]{0,2,1:T(8,128)}, ...), condition=%wide.region_6.9_spmd.clone, body=%wide.region_5.8_spmd.clone.sunk | while | flops 228808384 | bytes 38864004 | solution.py:68
  111.1 0.9 gather_fusion.2
  112.0 2.0 gather_fusion.3
  114.1 7.9 %bitcast_add_fusion.2 = f32[128,210,128]{0,2,1:T(8,128)} fusion(f32[128,210,128]{0,2,1:T(8,128)} %get-tuple-element.395, pred[]{:T(512)S(6)} %compare.3, bf16[210,32,128]{2,1,0:T(8,128)(2,1)S(1)} %gather_fusion.2, bf16[210,32,128]{2,1,0:T(8,128)(2,1)} %gather_fusion.3, pred[210]{0:T(512)(128)(4,1)S(1)} %get-tuple-element.342, ...), kind=kOutput, calls=%fused_computation.43.clone.1 | convolution fusion | flops 228802560 | bytes 30966180 | tf_op jit(solution)/shard_map/while/body/eval_jaxpr/rnk,rnj->knj/dot_general | solution.py:64
  122.1 0.9 gather_fusion.2
  123.0 2.0 gather_fusion.3
  125.0 10.2 %bitcast_add_fusion.2 = f32[128,210,128]{0,2,1:T(8,128)} fusion(f32[128,210,128]{0,2,1:T(8,128)} %get-tuple-element.395, pred[]{:T(512)S(6)} %compare.3, bf16[210,32,128]{2,1,0:T(8,128)(2,1)S(1)} %gather_fusion.2, bf16[210,32,128]{2,1,0:T(8,128)(2,1)} %gather_fusion.3, pred[210]{0:T(512)(128)(4,1)S(1)} %get-tuple-element.342, ...), kind=kOutput, calls=%fused_computation.43.clone.1 | convolution fusion | flops 228802560 | bytes 30966180 | tf_op jit(solution)/shard_map/while/body/eval_jaxpr/rnk,rnj->knj/dot_general | solution.py:64
  135.2 14.6 %copy.20 = f32[128,210,128]{2,0,1:T(8,128)} copy(f32[128,210,128]{0,2,1:T(8,128)} %get-tuple-element.103) | data formatting | bytes 27525120 | tf_op jit(solution)/shard_map/while | solution.py:68
  149.8 13.1 %broadcast_multiply_fusion = f32[128,210,128]{2,0,1:T(8,128)} fusion(f32[128,210,128]{2,0,1:T(8,128)} %copy.20), kind=kLoop, calls=%fused_computation.60 | loop fusion | flops 3440640 | bytes 27525120 | tf_op jit(solution)/shard_map/mul | solution.py:75
  163.0 1.1 copy-done.2
  164.1 1.0 fusion.58
  165.1 96.8 %reduce-scatter.5.cloned.1.call-done = f32[16,210,128]{2,0,1:T(8,128)} async-done(((f32[128,210,128]{2,0,1:T(8,128)}), f32[16,210,128]{2,0,1:T(8,128)}) %reduce-scatter.5.cloned.1.call-update) | async-done | bytes 1720336 | tf_op jit(solution)/shard_map/reduce_scatter | solution.py:75
  (63 shorter events, 4.0 us)
Async XLA Ops:
  7.2 54.7 %all-gather.2.cloned.1.call-start = ((), (), s32[]{:S(2)}) async-start(), calls=%async_computation.2 | async-start | bytes 7741440 | tf_op jit(solution)/shard_map/all_gather | solution.py:46
  7.9 20.2 %copy-start.7 = (bf16[64,2688]{1,0:T(8,128)(2,1)S(1)}, bf16[64,2688]{1,0:T(8,128)(2,1)}, u32[]{:S(2)}) copy-start(bf16[64,2688]{1,0:T(8,128)(2,1)} %param.19) | copy-start | bytes 1032196
  7.9 157.2 %reduce-scatter.3.cloned.1.call-start = ((), (), s32[]{:S(2)}) async-start(), calls=%async_computation.3 | async-start | bytes 819200 | tf_op jit(solution)/shard_map/reduce_scatter | solution.py:90
  27.9 33.9 %copy-start.5 = (s32[1,210]{1,0:T(1,128)S(1)}, s32[1,210]{1,0:T(1,128)}, u32[]{:S(2)}) copy-start(s32[1,210]{1,0:T(1,128)} %param.17) | copy-start | bytes 2524
  27.9 33.9 %copy-start.6 = (s32[1,210]{1,0:T(1,128)S(1)}, s32[1,210]{1,0:T(1,128)}, u32[]{:S(2)}) copy-start(s32[1,210]{1,0:T(1,128)} %param.18) | copy-start | bytes 2524
  62.9 4.3 %copy-start = (f32[2,32,21,128]{3,2,1,0:T(8,128)S(1)}, f32[2,32,21,128]{3,2,1,0:T(8,128)}, u32[]{:S(2)}) copy-start(f32[2,32,21,128]{3,2,1,0:T(8,128)} %get-tuple-element.352) | copy-start | bytes 2064388 | tf_op jit(solution)/shard_map/while
  71.1 0.9 copy-start.1
  73.0 4.3 %copy-start = (f32[2,32,21,128]{3,2,1,0:T(8,128)S(1)}, f32[2,32,21,128]{3,2,1,0:T(8,128)}, u32[]{:S(2)}) copy-start(f32[2,32,21,128]{3,2,1,0:T(8,128)} %get-tuple-element.352) | copy-start | bytes 2064388 | tf_op jit(solution)/shard_map/while
  81.3 0.9 copy-start.1
  85.3 6.0 %copy-start.3 = (bf16[2,32,40,128]{3,2,1,0:T(8,128)(2,1)S(1)}, bf16[2,32,40,128]{3,2,1,0:T(8,128)(2,1)}, u32[]{:S(2)}) copy-start(bf16[2,32,40,128]{3,2,1,0:T(8,128)(2,1)} %get-tuple-element.373) | copy-start | bytes 1966084 | tf_op jit(solution)/shard_map/while
  95.7 0.8 copy-start.4
  97.6 6.0 %copy-start.3 = (bf16[2,32,40,128]{3,2,1,0:T(8,128)(2,1)S(1)}, bf16[2,32,40,128]{3,2,1,0:T(8,128)(2,1)}, u32[]{:S(2)}) copy-start(bf16[2,32,40,128]{3,2,1,0:T(8,128)(2,1)} %get-tuple-element.373) | copy-start | bytes 1966084 | tf_op jit(solution)/shard_map/while
  108.0 0.8 copy-start.4
  110.9 151.0 %reduce-scatter.5.cloned.1.call-start = ((), (), s32[]{:S(2)}) async-start(), calls=%async_computation.4 | async-start | bytes 15482880 | tf_op jit(solution)/shard_map/reduce_scatter | solution.py:75
  163.0 1.1 copy-start.2
Sparse Core Ops, SparseCore 0:
  9.9 51.9 all-gather.1
  111.0 22.1 reduce-scatter.2
  163.1 98.7 reduce-scatter.4
where the time goes:
time: 269 us; the launch traced here: 268 us
  waiting for transfers between devices  130 us (48%)
  matrix products  55.2 us (21%)
  local copies, waits for them, and re-layouts  32.5 us (12%)
  blocking collectives  20 us (7%)
  other arithmetic  16.1 us (6%)
  between operations  13.8 us (5%)
    reduce_scatter x1, waiting for transfers between devices, local(): lax.psum_scatter(total * grad_scale, 'fsdp', scatter_dimension=0, tiled=T...  96.8 us
    all_gather x1, waiting for transfers between devices, local(): whole_tiles = lax.all_gather(tile_values, 'fsdp', axis=0, tiled=True)  32.7 us
    all_gather x1, blocking collectives, local(): gathered = lax.all_gather(tokens, 'tp', axis=0, tiled=True)  20 us
    dot_general x2, matrix products, add_block(): jnp.einsum('rnk,rnj->knj', chosen, grad_chosen, preferred_element_type=jn...  18 us
    while x1, local copies, waits for them, and re-layouts, local(): lax.scan(add_block, jnp.zeros((tile_values.shape[0] * lax.axis_size('fsdp...  14.6 us
    mul x1, other arithmetic, local(): total * grad_scale  13.1 us
    dot_general x2, matrix products, backward_block(): jnp.einsum('rnj,knj->rnk', grad_chosen, tiles_now, preferred_element_type...  11.9 us
    dot_general x2, matrix products, backward_block(): jnp.einsum('rnk,nq->rqk', back_product, row_onehot, precision=highest)  8.87 us
  transfers between devices with their start and end apart: 3, of which 2 were waited for; matrix products, arithmetic and copies ran while one was open for 20% of the time, Pallas kernels for 0%

commit v1 on v0

v1 whole, which is shorter than its diff:
```python
import functools
import math

import jax
import jax.numpy as jnp
from jax import lax
from jax.experimental import pallas as pl
from jax.experimental.pallas import tpu as pltpu
from jax.sharding import PartitionSpec as P

SQRT_TWO_PI = 0.7978845608028654
CUBIC_COEF = 0.044715
BF16 = jnp.bfloat16
F32 = jnp.float32
VMEM = pltpu.VMEM
SMEM = pltpu.SMEM
MIB = 1 << 20


def gelu_pair(pre_act):
    gelu_inner = SQRT_TWO_PI * (pre_act + CUBIC_COEF * pre_act * pre_act * pre_act)
    tanh_inner = jnp.tanh(gelu_inner)
    act_value = 0.5 * pre_act * (1.0 + tanh_inner)
    act_slope = 0.5 * (1.0 + tanh_inner) + 0.5 * pre_act * (
        1.0 - tanh_inner * tanh_inner
    ) * SQRT_TWO_PI * (1.0 + 3.0 * CUBIC_COEF * pre_act * pre_act)
    return (act_value, act_slope)


def spec(space=VMEM):
    return pl.BlockSpec(memory_space=space)


def lane_regroup(chips, tile_width):
    size = chips * tile_width
    part = tile_width // chips
    column = lax.broadcasted_iota(jnp.int32, (1, size), 1)
    chip = column // tile_width
    inner = column % tile_width
    source = (inner // part) * tile_width + chip * part + inner % part
    row = lax.broadcasted_iota(jnp.int32, (size, size), 0)
    return jnp.where(row == source, 1.0, 0.0).astype(BF16)


def split_kernel(chips, tile_width, chip_ref, tokens_ref, out_ref):
    size = chips * tile_width
    onehot = lane_regroup(chips, tile_width)
    me = chip_ref[0]
    for group in range(tokens_ref.shape[1] // size):
        picked = jnp.dot(
            tokens_ref[:, group * size : (group + 1) * size], onehot, preferred_element_type=F32
        ).astype(BF16)
        for chip in range(chips):
            out_ref[me ^ chip, :, group * tile_width : (group + 1) * tile_width] = picked[
                :, chip * tile_width : (chip + 1) * tile_width
            ]


def join_kernel(chips, tile_width, chip_ref, *refs):
    *part_refs, out_ref, held = refs
    size = chips * tile_width
    onehot = lane_regroup(chips, tile_width)
    me = chip_ref[0]
    for step in range(chips):
        held[me ^ step] = part_refs[step][...]
    for group in range(out_ref.shape[1] // size):
        lanes = jnp.concatenate(
            [held[chip, :, group * tile_width : (group + 1) * tile_width] for chip in range(chips)],
            axis=1,
        )
        out_ref[:, group * size : (group + 1) * size] = lax.dot_general(
            lanes, onehot, (((1,), (1,)), ((), ())), preferred_element_type=F32
        ).astype(BF16)


def weight_kernel(core_ref, row_ref, col_ref, own_ref, other_ref, out_ref):
    slots, rows, width = own_ref.shape
    core = core_ref[0]
    out_ref[...] = jnp.zeros_like(out_ref)

    def place(slot, carry):
        top = row_ref[0, slot] * (2 * rows)
        left = pl.multiple_of(col_ref[0, slot] * width, width)
        mine = pl.multiple_of(top + core * rows, rows)
        theirs = pl.multiple_of(top + (1 - core) * rows, rows)
        out_ref[pl.ds(mine, rows), pl.ds(left, width)] = own_ref[slot]
        out_ref[pl.ds(theirs, rows), pl.ds(left, width)] = other_ref[slot]
        return carry

    lax.fori_loop(0, slots, place, 0, unroll=6)


def hidden_kernel(chips, count, *refs):
    x_refs = refs[:count]
    w_ref = refs[count]
    out_refs = refs[count + 1 :]
    rows = x_refs[0].shape[1]
    lhs = jnp.concatenate(
        [x_refs[j][step] for step in range(chips) for j in range(count)], axis=0
    )
    result = jnp.dot(lhs, w_ref[...], preferred_element_type=F32)
    block = rows * count
    for step in range(chips):
        out_refs[step][...] = result[step * block : (step + 1) * block].astype(out_refs[step].dtype)


def back_kernel(chips, count, rows, *refs):
    g_refs = refs[:chips]
    w_ref = refs[chips]
    out_refs = refs[chips + 1 :]
    lhs = jnp.concatenate(
        [g_refs[step][j * rows : (j + 1) * rows] for j in range(count) for step in range(chips)],
        axis=0,
    )
    result = lax.dot_general(lhs, w_ref[...], (((1,), (1,)), ((), ())), preferred_element_type=F32)
    block = rows * chips
    for j in range(count):
        out_refs[j][...] = result[j * block : (j + 1) * block].astype(out_refs[j].dtype)


def tile_grad_kernel(chips, plan, rows, core_ref, row_ref, col_ref, *refs):
    zs = sum(len(chunk) for chunk in plan)
    x_refs = refs[:zs]
    g_refs = refs[zs : zs + chips * len(plan)]
    mine_ref, theirs_ref, x_all, g_all, dense = refs[zs + chips * len(plan) :]
    slots, tile_rows, width = mine_ref.shape
    core = core_ref[0]
    at = 0
    for index, chunk in enumerate(plan):
        for place, j in enumerate(chunk):
            for step in range(chips):
                x_all[at : at + rows] = x_refs[j][step]
                g_all[at : at + rows] = g_refs[index * chips + step][
                    place * rows : (place + 1) * rows
                ]
                at += rows
    x_t = x_all[...].T
    columns = dense.shape[1]
    step_width = columns // 3 if columns % (3 * width) == 0 else width
    for left in range(0, columns, step_width):
        dense[:, left : left + step_width] = jnp.dot(
            x_t, g_all[:, left : left + step_width], preferred_element_type=F32
        )

    def place_tile(slot, carry):
        top = row_ref[0, slot] * (2 * tile_rows)
        left = pl.multiple_of(col_ref[0, slot] * width, width)
        mine = pl.multiple_of(top + core * tile_rows, tile_rows)
        theirs = pl.multiple_of(top + (1 - core) * tile_rows, tile_rows)
        mine_ref[slot] = dense[pl.ds(mine, tile_rows), pl.ds(left, width)]
        theirs_ref[slot] = dense[pl.ds(theirs, tile_rows), pl.ds(left, width)]
        return carry

    lax.fori_loop(0, slots, place_tile, 0, unroll=6)


def params(limit):
    return pltpu.CompilerParams(vmem_limit_bytes=limit * MIB)


def cost(flops, bytes_accessed):
    return pl.CostEstimate(flops=flops, bytes_accessed=bytes_accessed, transcendentals=0)


def local(tokens, tile_values, tile_row, tile_col, grad_act):
    fsdp = lax.axis_size("fsdp")
    n_tp = lax.axis_size("tp")
    chips = fsdp // 2
    rows, width = tokens.shape
    tile_rows, slots, tile_width = tile_values.shape
    row_tiles = width // tile_width
    columns = grad_act.shape[1]
    col_tiles = columns // tile_width
    depth = row_tiles * 2 * tile_rows
    total_tokens = rows * fsdp * n_tp
    grad_scale = 1.0 / math.sqrt(total_tokens)
    place = lax.axis_index("fsdp")
    chip = place // 2
    core = place % 2
    z = lax.axis_index("tp")
    fast = tile_rows % 16 == 0 and rows % 16 == 0 and row_tiles % chips == 0
    plan = [tuple(range(n_tp))]

    def to_core(value):
        return lax.ppermute(value, "fsdp", [(f, f ^ 1) for f in range(fsdp)])

    def to_chip(value, step):
        return lax.ppermute(value, "fsdp", [(f, f ^ (2 * step)) for f in range(fsdp)])

    def to_z(value, step):
        return lax.ppermute(value, "tp", [(i, (i + step) % n_tp) for i in range(n_tp)])

    chip_index = chip.astype(jnp.int32).reshape(1)
    core_index = core.astype(jnp.int32).reshape(1)
    own_tiles = jnp.transpose(tile_values, (1, 0, 2))
    other_tiles = to_core(own_tiles)

    if fast:
        split = pl.pallas_call(
            functools.partial(split_kernel, chips, tile_width),
            out_shape=jax.ShapeDtypeStruct((chips, rows, width // chips), BF16),
            in_specs=[spec(SMEM), spec()],
            out_specs=spec(),
            compiler_params=params(16),
        )(chip_index, tokens)
    else:
        split = jnp.transpose(
            tokens.reshape(rows, row_tiles, chips, tile_width // chips), (2, 0, 1, 3)
        ).reshape(chips, rows, depth)
        split = jnp.take(split, jnp.arange(chips) ^ chip, axis=0)
    pieces = [split[0]] + [to_chip(split[step], step) for step in range(1, chips)]
    x_own = jnp.stack(pieces)
    x_parts = [x_own] + [to_z(x_own, j) for j in range(1, n_tp)]

    if fast:
        weight = pl.pallas_call(
            weight_kernel,
            out_shape=jax.ShapeDtypeStruct((depth, columns), BF16),
            in_specs=[spec(SMEM), spec(SMEM), spec(SMEM), spec(), spec()],
            out_specs=spec(),
            compiler_params=params(24),
            cost_estimate=cost(0, 2 * 2 * depth * columns),
        )(core_index, tile_row, tile_col, own_tiles, other_tiles)
    else:
        both = jnp.where(
            core == 0,
            jnp.concatenate([own_tiles, other_tiles], axis=1),
            jnp.concatenate([other_tiles, own_tiles], axis=1),
        )
        flat = tile_row[0] * col_tiles + tile_col[0]
        weight = jnp.zeros((row_tiles * col_tiles, 2 * tile_rows, tile_width), BF16)
        weight = weight.at[flat].set(both, unique_indices=True)
        weight = jnp.transpose(
            weight.reshape(row_tiles, col_tiles, 2 * tile_rows, tile_width), (0, 2, 1, 3)
        ).reshape(depth, columns)

    acts = [None] * n_tp
    grad_chunks = []
    totals = [None] * n_tp
    for chunk in plan:
        count = len(chunk)
        block = rows * count
        chunk_x = [x_parts[j] for j in chunk]
        if fast:
            hidden_parts = pl.pallas_call(
                functools.partial(hidden_kernel, chips, count),
                out_shape=[jax.ShapeDtypeStruct((block, columns), F32)]
                + [jax.ShapeDtypeStruct((block, columns), BF16)] * (chips - 1),
                in_specs=[spec()] * (count + 1),
                out_specs=[spec()] * chips,
                compiler_params=params(32),
                cost_estimate=cost(2 * chips * block * depth * columns, 2 * depth * columns),
            )(*chunk_x, weight)
        else:
            joined = jnp.concatenate(chunk_x, axis=1).reshape(chips * block, depth)
            product = jnp.dot(joined, weight, preferred_element_type=F32)
            product = product.reshape(chips, block, columns)
            hidden_parts = [product[0]] + [
                product[step].astype(BF16) for step in range(1, chips)
            ]
        hidden = hidden_parts[0]
        for step in range(1, chips):
            hidden = hidden + to_chip(hidden_parts[step], step).astype(F32)
        act_value, act_slope = gelu_pair(hidden)
        act_value = act_value.astype(BF16)
        cotangent = jnp.concatenate(
            [
                lax.dynamic_slice_in_dim(grad_act, ((z - j) % n_tp) * rows, rows, axis=0)
                for j in chunk
            ],
            axis=0,
        )
        hidden_grad = (cotangent.astype(F32) * act_slope).astype(BF16)
        for at, j in enumerate(chunk):
            acts[j] = act_value[at * rows : (at + 1) * rows]
        grads = [hidden_grad] + [to_chip(hidden_grad, step) for step in range(1, chips)]
        grad_chunks.append(grads)
        if fast:
            backs = pl.pallas_call(
                functools.partial(back_kernel, chips, count, rows),
                out_shape=[
                    jax.ShapeDtypeStruct((chips * rows, depth), F32 if j == 0 else BF16)
                    for j in chunk
                ],
                in_specs=[spec()] * (chips + 1),
                out_specs=[spec()] * count,
                compiler_params=params(32),
                cost_estimate=cost(2 * chips * block * depth * columns, 2 * depth * columns),
            )(*grads, weight)
        else:
            joined = jnp.stack(grads).reshape(chips, count, rows, columns)
            product = jnp.einsum(
                "sjrc,kc->jsrk", joined, weight, preferred_element_type=F32
            ).reshape(count, chips * rows, depth)
            backs = [
                product[at] if j == 0 else product[at].astype(BF16)
                for at, j in enumerate(chunk)
            ]
        for at, j in enumerate(chunk):
            totals[j] = backs[at]

    total = totals[0]
    for j in range(1, n_tp):
        total = total + to_z(totals[j], n_tp - j).astype(F32)
    total = total.astype(BF16).reshape(chips, rows, depth)
    parts = [total[0]] + [to_chip(total[step], step) for step in range(1, chips)]

    if fast:
        flat_grads = [grad for grads in grad_chunks for grad in grads]
        mine, theirs = pl.pallas_call(
            functools.partial(tile_grad_kernel, chips, plan, rows),
            out_shape=[jax.ShapeDtypeStruct((slots, tile_rows, tile_width), F32)] * 2,
            in_specs=[spec(SMEM)] * 3 + [spec()] * (n_tp + len(flat_grads)),
            out_specs=[spec()] * 2,
            scratch_shapes=[
                pltpu.VMEM((chips * n_tp * rows, depth), BF16),
                pltpu.VMEM((chips * n_tp * rows, columns), BF16),
                pltpu.VMEM((depth, columns), F32),
            ],
            compiler_params=params(40),
            cost_estimate=cost(
                2 * chips * n_tp * rows * depth * columns, 4 * depth * columns
            ),
        )(core_index, tile_row, tile_col, *x_parts, *flat_grads)
        grad_tokens = pl.pallas_call(
            functools.partial(join_kernel, chips, tile_width),
            out_shape=jax.ShapeDtypeStruct((rows, width), BF16),
            in_specs=[spec(SMEM)] + [spec()] * chips,
            out_specs=spec(),
            scratch_shapes=[pltpu.VMEM((chips, rows, depth), BF16)],
            compiler_params=params(16),
        )(chip_index, *parts)
    else:
        x_all = jnp.concatenate(x_parts, axis=1).reshape(-1, depth)
        g_all = jnp.concatenate(
            [jnp.stack(grads) for grads in grad_chunks], axis=1
        ).reshape(-1, columns)
        dense = jnp.einsum("tk,tn->kn", x_all, g_all, preferred_element_type=F32)
        dense = jnp.transpose(
            dense.reshape(row_tiles, 2, tile_rows, col_tiles, tile_width), (1, 0, 3, 2, 4)
        ).reshape(2, row_tiles * col_tiles, tile_rows, tile_width)
        picked = jnp.take(dense, tile_row[0] * col_tiles + tile_col[0], axis=1)
        mine = jnp.where(core == 0, picked[0], picked[1])
        theirs = jnp.where(core == 0, picked[1], picked[0])
        joined = jnp.take(jnp.stack(parts), jnp.arange(chips) ^ chip, axis=0)
        grad_tokens = jnp.transpose(
            joined.reshape(chips, rows, row_tiles, tile_width // chips), (1, 2, 0, 3)
        ).reshape(rows, width)
    grad_tiles = jnp.transpose((mine + to_core(theirs)) * grad_scale, (1, 0, 2))

    act = jnp.zeros((n_tp * rows, columns), BF16)
    for j in range(n_tp):
        act = lax.dynamic_update_slice_in_dim(act, acts[j], ((z - j) % n_tp) * rows, axis=0)
    return (act, grad_tokens, grad_tiles)


def solution(mesh):
    in_specs = (
        P(("fsdp", "tp"), None),
        P("fsdp", "tp", None),
        P("tp", None),
        P("tp", None),
        P("fsdp", "tp"),
    )
    out_specs = (P("fsdp", "tp"), P(("fsdp", "tp"), None), P("fsdp", "tp", None))
    return jax.shard_map(local, mesh=mesh, in_specs=in_specs, out_specs=out_specs, check_vma=False)
```

time: 269 us -> 94.4 us (0.35)
  waiting for transfers between devices: 130 us -> 50.6 us
  matrix products: 55.2 us -> 0 us
  local copies, waits for them, and re-layouts: 32.5 us -> 2.46 us
  starting transfers between devices: 0.12 us -> 24.8 us
  blocking collectives: 20 us -> 0 us
  other arithmetic: 16.1 us -> 2.16 us
  Pallas kernels: 0 us -> 13.4 us
  between operations: 13.8 us -> 0.79 us
    reduce_scatter x2 -> x0, waiting for transfers between devices: 96.8 us -> none  [the longest x1 96.8 us: local(): lax.psum_scatter(total * grad_scale, 'fsdp', scatter_dimension=0, tiled=T...]
    dot_general x10 -> x0, matrix products: 55.2 us -> none  [the longest x2 18 us: add_block(): jnp.einsum('rnk,rnj->knj', chosen, grad_chosen, preferred_element_type=jn...]
    ppermute x0 -> x20, waiting for transfers between devices: none -> 50.6 us  [the longest x12 33.3 us: to_chip(): return lax.ppermute(value, 'fsdp', [(f, f ^ 2 * step) for f in range(fsdp)])]
    all_gather x1 -> x0, waiting for transfers between devices: 32.7 us -> none  [local(): whole_tiles = lax.all_gather(tile_values, 'fsdp', axis=0, tiled=True)]
    ppermute x0 -> x20, starting transfers between devices: none -> 24.8 us  [the longest x12 14.9 us: to_chip(): return lax.ppermute(value, 'fsdp', [(f, f ^ 2 * step) for f in range(fsdp)])]
    all_gather x1 -> x0, blocking collectives: 20 us -> none  [local(): gathered = lax.all_gather(tokens, 'tp', axis=0, tiled=True)]
    while x17 -> x0, local copies, waits for them, and re-layouts: 18.1 us -> none  [the longest x1 14.6 us: local(): lax.scan(add_block, jnp.zeros((tile_values.shape[0] * lax.axis_size('fsdp...]
    pallas_call x0 -> x6, Pallas kernels: none -> 13.4 us  [the longest x1 4 us: local(): pl.pallas_call(functools.partial(tile_grad_kernel, chips, plan, rows), ou...]
  transfers between devices with their start and end apart: 3 -> 20, of which waited for: 2 -> 13; matrix products, arithmetic and copies ran while one was open for 20% -> 0% of each run, Pallas kernels for 0% -> 10%
where the time goes in v1:
time: 94.4 us; the launch traced here: 94.2 us
  waiting for transfers between devices  50.6 us (54%)
  starting transfers between devices  24.8 us (26%)
  Pallas kernels  13.4 us (14%)
  local copies, waits for them, and re-layouts  2.46 us (3%)
  other arithmetic  2.16 us (2%)
    ppermute x12, waiting for transfers between devices, to_chip(): return lax.ppermute(value, 'fsdp', [(f, f ^ 2 * step) for f in range(fsdp)])  33.3 us
    ppermute x6, waiting for transfers between devices, to_z(): lax.ppermute(value, 'tp', [(i, (i + step) % n_tp) for i in range(n_tp)])  17.3 us
    ppermute x12, starting transfers between devices, to_chip(): return lax.ppermute(value, 'fsdp', [(f, f ^ 2 * step) for f in range(fsdp)])  14.9 us
    ppermute x6, starting transfers between devices, to_z(): lax.ppermute(value, 'tp', [(i, (i + step) % n_tp) for i in range(n_tp)])  9.3 us
    pallas_call x1, Pallas kernels, local(): pl.pallas_call(functools.partial(tile_grad_kernel, chips, plan, rows), ou...  4 us
    pallas_call x1, Pallas kernels, local(): pl.pallas_call(weight_kernel, out_shape=jax.ShapeDtypeStruct((depth, colu...  2.31 us
    unnamed x16, local copies, waits for them, and re-layouts  2.3 us
    pallas_call x1, Pallas kernels, local(): pl.pallas_call(functools.partial(join_kernel, chips, tile_width), out_sha...  2.2 us
  transfers between devices with their start and end apart: 20, of which 13 were waited for; matrix products, arithmetic and copies ran while one was open for 0% of the time, Pallas kernels for 10%

profile of v1, /device:TPU:0, one launch (start us, length us, event | category | flops | bytes accessed | tf_op | source)
XLA Modules:
  0.0 94.2 jit_solution(12004007874845830502)
XLA Ops:
  1.2 0.9 copy-done.1
  2.1 0.8 shard_map.76
  2.9 3.6 %collective-permute-start.2 = (bf16[16,1280]{1,0:T(8,128)(2,1)S(1)}, bf16[16,1280]{1,0:T(8,128)(2,1)S(1)}, u32[]{:S(2)}, u32[]{:S(2)}) collective-permute-start(bf16[16,1280]{1,0:T(8,128)(2,1)S(1)} %get-tuple-element.34), channel_id=1, source_target_pairs={{0,24},{4,28},{8,16},{12,20},{16,8},{20,12},{24,0},{28,4},{1,25},{... | collective-permute-start | bytes 122888 | tf_op jit(solution)/shard_map/ppermute | solution.py:188
  7.1 1.5 %collective-permute-done.2 = bf16[16,1280]{1,0:T(8,128)(2,1)S(1)} collective-permute-done((bf16[16,1280]{1,0:T(8,128)(2,1)S(1)}, bf16[16,1280]{1,0:T(8,128)(2,1)S(1)}, u32[]{:S(2)}, u32[]{:S(2)}) %collective-permute-start.2) | collective-permute-done | bytes 40992 | tf_op jit(solution)/shard_map/ppermute | solution.py:188
  8.7 1.8 %collective-permute-done.1 = bf16[16,1280]{1,0:T(8,128)(2,1)S(1)} collective-permute-done((bf16[16,1280]{1,0:T(8,128)(2,1)S(1)}, bf16[16,1280]{1,0:T(8,128)(2,1)S(1)}, u32[]{:S(2)}, u32[]{:S(2)}) %collective-permute-start.1) | collective-permute-done | bytes 40992 | tf_op jit(solution)/shard_map/ppermute | solution.py:188
  11.0 3.7 %collective-permute-start.5 = (bf16[4,16,1280]{2,1,0:T(8,128)(2,1)S(1)}, bf16[4,16,1280]{2,1,0:T(8,128)(2,1)S(1)}, u32[]{:S(2)}, u32[]{:S(2)}) collective-permute-start(bf16[4,16,1280]{2,1,0:T(8,128)(2,1)S(1)} %pad_maximum_fusion.refs_0_), channel_id=1, source_target_pairs={{0,3},{1,0},{2,1},{3,2},{4,7},{5,4},{6,5},{7,6},{8,11},{9,8},{10,9... | collective-permute-start | bytes 491528 | tf_op jit(solution)/shard_map/ppermute | solution.py:191
  14.7 1.0 %collective-permute-start.3 = (bf16[4,16,1280]{2,1,0:T(8,128)(2,1)S(1)}, bf16[4,16,1280]{2,1,0:T(8,128)(2,1)S(1)}, u32[]{:S(2)}, u32[]{:S(2)}) collective-permute-start(bf16[4,16,1280]{2,1,0:T(8,128)(2,1)S(1)} %pad_maximum_fusion.refs_0_), channel_id=1, source_target_pairs={{0,1},{1,2},{2,3},{3,0},{4,5},{5,6},{6,7},{7,4},{8,9},{9,10},{10,1... | collective-permute-start | bytes 491528 | tf_op jit(solution)/shard_map/ppermute | solution.py:191
  15.7 0.7 copy-done.2
  17.1 2.3 %shard_map.77.refs_4_ = bf16[1280,2688]{1,0:T(8,128)(2,1)S(1)} custom-call(s32[1]{0:T(128)} %bitcast.7.core_ref, s32[1,210]{1,0:T(1,128)S(1)} %copy-done.2, s32[1,210]{1,0:T(1,128)S(1)} %copy-done.4, bf16[210,16,128]{2,1,0:T(8,128)(2,1)S(1)} %bitcast.15, bf16[210,16,128]{2,1,0:T(8,128)(2,1)S(1)} %collective-permute-done.6.other_ref), custom_call_target="tpu_custom_call" | custom-call | bytes 13762560 | tf_op jit(solution)/shard_map/pallas_call | solution.py:216
  19.4 8.5 %collective-permute-done.4.refs_2_ = bf16[4,16,1280]{2,1,0:T(8,128)(2,1)S(1)} collective-permute-done((bf16[4,16,1280]{2,1,0:T(8,128)(2,1)S(1)}, bf16[4,16,1280]{2,1,0:T(8,128)(2,1)S(1)}, u32[]{:S(2)}, u32[]{:S(2)}) %collective-permute-start.4) | collective-permute-done | bytes 163872 | tf_op jit(solution)/shard_map/ppermute | solution.py:191
  28.0 2.0 %shard_map.78 = (f32[64,2688]{1,0:T(8,128)S(1)}, bf16[64,2688]{1,0:T(8,128)(2,1)S(1)}, bf16[64,2688]{1,0:T(8,128)(2,1)S(1)}, bf16[64,2688]{1,0:T(8,128)(2,1)S(1)}) custom-call(bf16[4,16,1280]{2,1,0:T(8,128)(2,1)S(1)} %pad_maximum_fusion.refs_0_, bf16[4,16,1280]{2,1,0:T(8,128)(2,1)S(1)} %collective-permute-done.3.refs_1_, ...), custom_call_target="tpu_custom_call" | custom-call | flops 1761607680 | bytes 6881280 | tf_op jit(solution)/shard_map/pallas_call | solution.py:245
  30.0 0.9 collective-permute-start.7
  30.9 1.2 %collective-permute-start.8 = (bf16[64,2688]{1,0:T(8,128)(2,1)S(1)}, bf16[64,2688]{1,0:T(8,128)(2,1)S(1)}, u32[]{:S(2)}, u32[]{:S(2)}) collective-permute-start(bf16[64,2688]{1,0:T(8,128)(2,1)S(1)} %get-tuple-element.15), channel_id=1, source_target_pairs={{0,16},{4,20},{8,24},{12,28},{16,0},{20,4},{24,8},{28,12},{1,17},{... | collective-permute-start | bytes 1032200 | tf_op jit(solution)/shard_map/ppermute | solution.py:188
  32.1 1.4 %collective-permute-start.9 = (bf16[64,2688]{1,0:T(8,128)(2,1)S(1)}, bf16[64,2688]{1,0:T(8,128)(2,1)S(1)}, u32[]{:S(2)}, u32[]{:S(2)}) collective-permute-start(bf16[64,2688]{1,0:T(8,128)(2,1)S(1)} %get-tuple-element.16), channel_id=1, source_target_pairs={{0,24},{4,28},{8,16},{12,20},{16,8},{20,12},{24,0},{28,4},{1,25},{... | collective-permute-start | bytes 1032200 | tf_op jit(solution)/shard_map/ppermute | solution.py:188
  33.6 7.5 %collective-permute-done.7 = bf16[64,2688]{1,0:T(8,128)(2,1)S(1)} collective-permute-done((bf16[64,2688]{1,0:T(8,128)(2,1)S(1)}, bf16[64,2688]{1,0:T(8,128)(2,1)S(1)}, u32[]{:S(2)}, u32[]{:S(2)}) %collective-permute-start.7) | collective-permute-done | bytes 344096 | tf_op jit(solution)/shard_map/ppermute | solution.py:188
  41.1 5.0 %collective-permute-done.8 = bf16[64,2688]{1,0:T(8,128)(2,1)S(1)} collective-permute-done((bf16[64,2688]{1,0:T(8,128)(2,1)S(1)}, bf16[64,2688]{1,0:T(8,128)(2,1)S(1)}, u32[]{:S(2)}, u32[]{:S(2)}) %collective-permute-start.8) | collective-permute-done | bytes 344096 | tf_op jit(solution)/shard_map/ppermute | solution.py:188
  46.1 1.5 %collective-permute-done.9 = bf16[64,2688]{1,0:T(8,128)(2,1)S(1)} collective-permute-done((bf16[64,2688]{1,0:T(8,128)(2,1)S(1)}, bf16[64,2688]{1,0:T(8,128)(2,1)S(1)}, u32[]{:S(2)}, u32[]{:S(2)}) %collective-permute-start.9) | collective-permute-done | bytes 344096 | tf_op jit(solution)/shard_map/ppermute | solution.py:188
  48.2 1.7 %collective-permute-start.12 = (bf16[64,2688]{1,0:T(8,128)(2,1)S(1)}, bf16[64,2688]{1,0:T(8,128)(2,1)S(1)}, u32[]{:S(2)}, u32[]{:S(2)}) collective-permute-start(bf16[64,2688]{1,0:T(8,128)(2,1)S(1)} %get-tuple-element.23.refs_0_.refs_4_), channel_id=1, source_target_pairs={{0,24},{4,28},{8,16},{12,20},{16,8},{20,12},{24,0},{28,4},{1,25},{... | collective-permute-start | bytes 1032200 | tf_op jit(solution)/shard_map/ppermute | solution.py:188
  50.4 1.4 %collective-permute-start.10 = (bf16[64,2688]{1,0:T(8,128)(2,1)S(1)}, bf16[64,2688]{1,0:T(8,128)(2,1)S(1)}, u32[]{:S(2)}, u32[]{:S(2)}) collective-permute-start(bf16[64,2688]{1,0:T(8,128)(2,1)S(1)} %get-tuple-element.23.refs_0_.refs_4_), channel_id=1, source_target_pairs={{0,8},{4,12},{8,0},{12,4},{16,24},{20,28},{24,16},{28,20},{1,9},{5... | collective-permute-start | bytes 1032200 | tf_op jit(solution)/shard_map/ppermute | solution.py:188
  51.9 8.3 %collective-permute-done.12.refs_3_.refs_7_ = bf16[64,2688]{1,0:T(8,128)(2,1)S(1)} collective-permute-done((bf16[64,2688]{1,0:T(8,128)(2,1)S(1)}, bf16[64,2688]{1,0:T(8,128)(2,1)S(1)}, u32[]{:S(2)}, u32[]{:S(2)}) %collective-permute-start.12) | collective-permute-done | bytes 344096 | tf_op jit(solution)/shard_map/ppermute | solution.py:188
  60.2 4.5 %collective-permute-done.11.refs_2_.refs_6_ = bf16[64,2688]{1,0:T(8,128)(2,1)S(1)} collective-permute-done((bf16[64,2688]{1,0:T(8,128)(2,1)S(1)}, bf16[64,2688]{1,0:T(8,128)(2,1)S(1)}, u32[]{:S(2)}, u32[]{:S(2)}) %collective-permute-start.11) | collective-permute-done | bytes 344096 | tf_op jit(solution)/shard_map/ppermute | solution.py:188
  64.7 2.1 %shard_map.79 = (f32[64,1280]{1,0:T(8,128)S(1)}, bf16[64,1280]{1,0:T(8,128)(2,1)S(1)}, bf16[64,1280]{1,0:T(8,128)(2,1)S(1)}, bf16[64,1280]{1,0:T(8,128)(2,1)S(1)}) custom-call(bf16[64,2688]{1,0:T(8,128)(2,1)S(1)} %get-tuple-element.23.refs_0_.refs_4_, bf16[64,2688]{1,0:T(8,128)(2,1)S(1)} %collective-permute-done.10.refs_1_.refs_5_, ...), custom_call_target="tpu_custom_call" | custom-call | flops 1761607680 | bytes 6881280 | tf_op jit(solution)/shard_map/pallas_call | solution.py:279
  66.8 2.6 %collective-permute-start.14 = (bf16[64,1280]{1,0:T(8,128)(2,1)S(1)}, bf16[64,1280]{1,0:T(8,128)(2,1)S(1)}, u32[]{:S(2)}, u32[]{:S(2)}) collective-permute-start(bf16[64,1280]{1,0:T(8,128)(2,1)S(1)} %get-tuple-element.19), channel_id=1, source_target_pairs={{0,2},{1,3},{2,0},{3,1},{4,6},{5,7},{6,4},{7,5},{8,10},{9,11},{10,... | collective-permute-start | bytes 491528 | tf_op jit(solution)/shard_map/ppermute | solution.py:191
  69.4 1.9 %collective-permute-start.15 = (bf16[64,1280]{1,0:T(8,128)(2,1)S(1)}, bf16[64,1280]{1,0:T(8,128)(2,1)S(1)}, u32[]{:S(2)}, u32[]{:S(2)}) collective-permute-start(bf16[64,1280]{1,0:T(8,128)(2,1)S(1)} %get-tuple-element.20), channel_id=1, source_target_pairs={{0,1},{1,2},{2,3},{3,0},{4,5},{5,6},{6,7},{7,4},{8,9},{9,10},{10,1... | collective-permute-start | bytes 491528 | tf_op jit(solution)/shard_map/ppermute | solution.py:191
  71.4 4.0 %shard_map.81 = (f32[210,16,128]{2,1,0:T(8,128)S(1)}, f32[210,16,128]{2,1,0:T(8,128)S(1)}) custom-call(s32[1]{0:T(128)} %bitcast.7.core_ref, s32[1,210]{1,0:T(1,128)S(1)} %copy-done.3, s32[1,210]{1,0:T(1,128)S(1)} %copy-done.5, bf16[4,16,1280]{2,1,0:T(8,128)(2,1)S(1)} %pad_maximum_fusion.refs_0_, bf16[4,16,1280]{2,1,0:T(8,128)(2,1)S(1)} %collective-permute-done.3.refs_1_, ...), custom_call_target="tpu_custom_call" | custom-call | flops 1761607680 | bytes 13762560 | tf_op jit(solution)/shard_map/pallas_call | solution.py:310
  75.5 8.8 %collective-permute-done.14 = bf16[64,1280]{1,0:T(8,128)(2,1)S(1)} collective-permute-done((bf16[64,1280]{1,0:T(8,128)(2,1)S(1)}, bf16[64,1280]{1,0:T(8,128)(2,1)S(1)}, u32[]{:S(2)}, u32[]{:S(2)}) %collective-permute-start.14) | collective-permute-done | bytes 163872 | tf_op jit(solution)/shard_map/ppermute | solution.py:191
  84.4 1.3 %collective-permute-start.18 = (bf16[16,1280]{1,0:T(8,128)(2,1)S(1)}, bf16[16,1280]{1,0:T(8,128)(2,1)S(1)}, u32[]{:S(2)}, u32[]{:S(2)}) collective-permute-start(bf16[16,1280]{1,0:T(8,128)(2,1)S(1)} %get-tuple-element.29), channel_id=1, source_target_pairs={{0,24},{4,28},{8,16},{12,20},{16,8},{20,12},{24,0},{28,4},{1,25},{... | collective-permute-start | bytes 122888 | tf_op jit(solution)/shard_map/ppermute | solution.py:188
  85.7 0.9 collective-permute-start.17
  86.6 1.3 %collective-permute-start.16 = (bf16[16,1280]{1,0:T(8,128)(2,1)S(1)}, bf16[16,1280]{1,0:T(8,128)(2,1)S(1)}, u32[]{:S(2)}, u32[]{:S(2)}) collective-permute-start(bf16[16,1280]{1,0:T(8,128)(2,1)S(1)} %get-tuple-element.31), channel_id=1, source_target_pairs={{0,8},{4,12},{8,0},{12,4},{16,24},{20,28},{24,16},{28,20},{1,9},{5... | collective-permute-start | bytes 122888 | tf_op jit(solution)/shard_map/ppermute | solution.py:188
  88.0 1.7 %collective-permute-done.18.refs_3_ = bf16[16,1280]{1,0:T(8,128)(2,1)S(1)} collective-permute-done((bf16[16,1280]{1,0:T(8,128)(2,1)S(1)}, bf16[16,1280]{1,0:T(8,128)(2,1)S(1)}, u32[]{:S(2)}, u32[]{:S(2)}) %collective-permute-start.18) | collective-permute-done | bytes 40992 | tf_op jit(solution)/shard_map/ppermute | solution.py:188
  90.6 2.2 %shard_map.80 = bf16[16,5120]{1,0:T(8,128)(2,1)} custom-call(s32[1]{0:T(128)} %bitcast.chip_ref, bf16[16,1280]{1,0:T(8,128)(2,1)S(1)} %get-tuple-element.32.refs_0_, bf16[16,1280]{1,0:T(8,128)(2,1)S(1)} %collective-permute-done.16.refs_1_, bf16[16,1280]{1,0:T(8,128)(2,1)S(1)} %collective-permute-done.17.refs_2_, ...), custom_call_target="tpu_custom_call" | custom-call | tf_op jit(solution)/shard_map/pallas_call | solution.py:325
  92.8 1.4 %multiply_bitcast_fusion = f32[16,210,128]{2,0,1:T(8,128)} fusion(f32[210,16,128]{2,1,0:T(8,128)S(1)} %get-tuple-element.21, f32[210,16,128]{2,1,0:T(8,128)S(1)} %collective-permute-done.19), kind=kLoop, calls=%fused_computation | loop fusion | flops 860160 | bytes 5160960 | tf_op jit(solution)/shard_map/transpose | solution.py:349
  (42 shorter events, 4.8 us)
Async XLA Ops:
  0.6 15.1 %copy-start = (bf16[16,210,128]{2,0,1:T(8,128)(2,1)S(1)}, bf16[16,210,128]{2,0,1:T(8,128)(2,1)}, u32[]{:S(2)}) copy-start(bf16[16,210,128]{2,0,1:T(8,128)(2,1)} %param.6) | copy-start | bytes 2580484
  0.6 15.1 %collective-permute-start.6 = (bf16[210,16,128]{2,1,0:T(8,128)(2,1)}, bf16[210,16,128]{2,1,0:T(8,128)(2,1)S(1)}, u32[]{:S(2)}, u32[]{:S(2)}) collective-permute-start(bf16[210,16,128]{2,1,0:T(8,128)(2,1)} %bitcast.14), channel_id=1, source_target_pairs={{0,4},{4,0},{8,12},{12,8},{16,20},{20,16},{24,28},{28,24},{1,5},{5... | collective-permute-start | bytes 2580488 | tf_op jit(solution)/shard_map/ppermute | solution.py:185
  1.2 0.9 copy-start.1
  2.9 5.7 %collective-permute-start.2 = (bf16[16,1280]{1,0:T(8,128)(2,1)S(1)}, bf16[16,1280]{1,0:T(8,128)(2,1)S(1)}, u32[]{:S(2)}, u32[]{:S(2)}) collective-permute-start(bf16[16,1280]{1,0:T(8,128)(2,1)S(1)} %get-tuple-element.34), channel_id=1, source_target_pairs={{0,24},{4,28},{8,16},{12,20},{16,8},{20,12},{24,0},{28,4},{1,25},{... | collective-permute-start | bytes 122888 | tf_op jit(solution)/shard_map/ppermute | solution.py:188
  6.5 4.0 %collective-permute-start.1 = (bf16[16,1280]{1,0:T(8,128)(2,1)S(1)}, bf16[16,1280]{1,0:T(8,128)(2,1)S(1)}, u32[]{:S(2)}, u32[]{:S(2)}) collective-permute-start(bf16[16,1280]{1,0:T(8,128)(2,1)S(1)} %get-tuple-element.35), channel_id=1, source_target_pairs={{0,16},{4,20},{8,24},{12,28},{16,0},{20,4},{24,8},{28,12},{1,17},{... | collective-permute-start | bytes 122888 | tf_op jit(solution)/shard_map/ppermute | solution.py:188
  7.0 4.0 %collective-permute-start = (bf16[16,1280]{1,0:T(8,128)(2,1)S(1)}, bf16[16,1280]{1,0:T(8,128)(2,1)S(1)}, u32[]{:S(2)}, u32[]{:S(2)}) collective-permute-start(bf16[16,1280]{1,0:T(8,128)(2,1)S(1)} %get-tuple-element.36), channel_id=1, source_target_pairs={{0,8},{4,12},{8,0},{12,4},{16,24},{20,28},{24,16},{28,20},{1,9},{5... | collective-permute-start | bytes 122888 | tf_op jit(solution)/shard_map/ppermute | solution.py:188
  11.0 8.4 %collective-permute-start.5 = (bf16[4,16,1280]{2,1,0:T(8,128)(2,1)S(1)}, bf16[4,16,1280]{2,1,0:T(8,128)(2,1)S(1)}, u32[]{:S(2)}, u32[]{:S(2)}) collective-permute-start(bf16[4,16,1280]{2,1,0:T(8,128)(2,1)S(1)} %pad_maximum_fusion.refs_0_), channel_id=1, source_target_pairs={{0,3},{1,0},{2,1},{3,2},{4,7},{5,4},{6,5},{7,6},{8,11},{9,8},{10,9... | collective-permute-start | bytes 491528 | tf_op jit(solution)/shard_map/ppermute | solution.py:191
  14.7 13.3 %collective-permute-start.4 = (bf16[4,16,1280]{2,1,0:T(8,128)(2,1)S(1)}, bf16[4,16,1280]{2,1,0:T(8,128)(2,1)S(1)}, u32[]{:S(2)}, u32[]{:S(2)}) collective-permute-start(bf16[4,16,1280]{2,1,0:T(8,128)(2,1)S(1)} %pad_maximum_fusion.refs_0_), channel_id=1, source_target_pairs={{0,2},{1,3},{2,0},{3,1},{4,6},{5,7},{6,4},{7,5},{8,10},{9,11},{10,... | collective-permute-start | bytes 491528 | tf_op jit(solution)/shard_map/ppermute | solution.py:191
  14.7 13.3 %collective-permute-start.3 = (bf16[4,16,1280]{2,1,0:T(8,128)(2,1)S(1)}, bf16[4,16,1280]{2,1,0:T(8,128)(2,1)S(1)}, u32[]{:S(2)}, u32[]{:S(2)}) collective-permute-start(bf16[4,16,1280]{2,1,0:T(8,128)(2,1)S(1)} %pad_maximum_fusion.refs_0_), channel_id=1, source_target_pairs={{0,1},{1,2},{2,3},{3,0},{4,5},{5,6},{6,7},{7,4},{8,9},{9,10},{10,1... | collective-permute-start | bytes 491528 | tf_op jit(solution)/shard_map/ppermute | solution.py:191
  15.7 0.7 copy-start.2
  16.4 0.7 copy-start.4
  19.4 14.2 %copy-start.6 = (bf16[64,2688]{1,0:T(8,128)(2,1)S(1)}, bf16[64,2688]{1,0:T(8,128)(2,1)}, u32[]{:S(2)}) copy-start(bf16[64,2688]{1,0:T(8,128)(2,1)} %param.9) | copy-start | bytes 1032196
  30.0 11.1 %collective-permute-start.7 = (bf16[64,2688]{1,0:T(8,128)(2,1)S(1)}, bf16[64,2688]{1,0:T(8,128)(2,1)S(1)}, u32[]{:S(2)}, u32[]{:S(2)}) collective-permute-start(bf16[64,2688]{1,0:T(8,128)(2,1)S(1)} %get-tuple-element.14), channel_id=1, source_target_pairs={{0,8},{4,12},{8,0},{12,4},{16,24},{20,28},{24,16},{28,20},{1,9},{5... | collective-permute-start | bytes 1032200 | tf_op jit(solution)/shard_map/ppermute | solution.py:188
  30.9 15.1 %collective-permute-start.8 = (bf16[64,2688]{1,0:T(8,128)(2,1)S(1)}, bf16[64,2688]{1,0:T(8,128)(2,1)S(1)}, u32[]{:S(2)}, u32[]{:S(2)}) collective-permute-start(bf16[64,2688]{1,0:T(8,128)(2,1)S(1)} %get-tuple-element.15), channel_id=1, source_target_pairs={{0,16},{4,20},{8,24},{12,28},{16,0},{20,4},{24,8},{28,12},{1,17},{... | collective-permute-start | bytes 1032200 | tf_op jit(solution)/shard_map/ppermute | solution.py:188
  32.1 15.5 %collective-permute-start.9 = (bf16[64,2688]{1,0:T(8,128)(2,1)S(1)}, bf16[64,2688]{1,0:T(8,128)(2,1)S(1)}, u32[]{:S(2)}, u32[]{:S(2)}) collective-permute-start(bf16[64,2688]{1,0:T(8,128)(2,1)S(1)} %get-tuple-element.16), channel_id=1, source_target_pairs={{0,24},{4,28},{8,16},{12,20},{16,8},{20,12},{24,0},{28,4},{1,25},{... | collective-permute-start | bytes 1032200 | tf_op jit(solution)/shard_map/ppermute | solution.py:188
  48.2 12.0 %collective-permute-start.12 = (bf16[64,2688]{1,0:T(8,128)(2,1)S(1)}, bf16[64,2688]{1,0:T(8,128)(2,1)S(1)}, u32[]{:S(2)}, u32[]{:S(2)}) collective-permute-start(bf16[64,2688]{1,0:T(8,128)(2,1)S(1)} %get-tuple-element.23.refs_0_.refs_4_), channel_id=1, source_target_pairs={{0,24},{4,28},{8,16},{12,20},{16,8},{20,12},{24,0},{28,4},{1,25},{... | collective-permute-start | bytes 1032200 | tf_op jit(solution)/shard_map/ppermute | solution.py:188
  49.9 14.7 %collective-permute-start.11 = (bf16[64,2688]{1,0:T(8,128)(2,1)S(1)}, bf16[64,2688]{1,0:T(8,128)(2,1)S(1)}, u32[]{:S(2)}, u32[]{:S(2)}) collective-permute-start(bf16[64,2688]{1,0:T(8,128)(2,1)S(1)} %get-tuple-element.23.refs_0_.refs_4_), channel_id=1, source_target_pairs={{0,16},{4,20},{8,24},{12,28},{16,0},{20,4},{24,8},{28,12},{1,17},{... | collective-permute-start | bytes 1032200 | tf_op jit(solution)/shard_map/ppermute | solution.py:188
  50.4 14.3 %collective-permute-start.10 = (bf16[64,2688]{1,0:T(8,128)(2,1)S(1)}, bf16[64,2688]{1,0:T(8,128)(2,1)S(1)}, u32[]{:S(2)}, u32[]{:S(2)}) collective-permute-start(bf16[64,2688]{1,0:T(8,128)(2,1)S(1)} %get-tuple-element.23.refs_0_.refs_4_), channel_id=1, source_target_pairs={{0,8},{4,12},{8,0},{12,4},{16,24},{20,28},{24,16},{28,20},{1,9},{5... | collective-permute-start | bytes 1032200 | tf_op jit(solution)/shard_map/ppermute | solution.py:188
  51.9 19.5 %copy-start.3 = (s32[1,210]{1,0:T(1,128)S(1)}, s32[1,210]{1,0:T(1,128)}, u32[]{:S(2)}) copy-start(s32[1,210]{1,0:T(1,128)} %row_ref.3) | copy-start | bytes 2524
  51.9 19.5 %copy-start.5 = (s32[1,210]{1,0:T(1,128)S(1)}, s32[1,210]{1,0:T(1,128)}, u32[]{:S(2)}) copy-start(s32[1,210]{1,0:T(1,128)} %col_ref.3) | copy-start | bytes 2524
  66.7 8.8 %collective-permute-start.13 = (bf16[64,1280]{1,0:T(8,128)(2,1)S(1)}, bf16[64,1280]{1,0:T(8,128)(2,1)S(1)}, u32[]{:S(2)}, u32[]{:S(2)}) collective-permute-start(bf16[64,1280]{1,0:T(8,128)(2,1)S(1)} %get-tuple-element.18), channel_id=1, source_target_pairs={{0,3},{1,0},{2,1},{3,2},{4,7},{5,4},{6,5},{7,6},{8,11},{9,8},{10,9... | collective-permute-start | bytes 491528 | tf_op jit(solution)/shard_map/ppermute | solution.py:191
  66.8 17.5 %collective-permute-start.14 = (bf16[64,1280]{1,0:T(8,128)(2,1)S(1)}, bf16[64,1280]{1,0:T(8,128)(2,1)S(1)}, u32[]{:S(2)}, u32[]{:S(2)}) collective-permute-start(bf16[64,1280]{1,0:T(8,128)(2,1)S(1)} %get-tuple-element.19), channel_id=1, source_target_pairs={{0,2},{1,3},{2,0},{3,1},{4,6},{5,7},{6,4},{7,5},{8,10},{9,11},{10,... | collective-permute-start | bytes 491528 | tf_op jit(solution)/shard_map/ppermute | solution.py:191
  69.4 14.8 %collective-permute-start.15 = (bf16[64,1280]{1,0:T(8,128)(2,1)S(1)}, bf16[64,1280]{1,0:T(8,128)(2,1)S(1)}, u32[]{:S(2)}, u32[]{:S(2)}) collective-permute-start(bf16[64,1280]{1,0:T(8,128)(2,1)S(1)} %get-tuple-element.20), channel_id=1, source_target_pairs={{0,1},{1,2},{2,3},{3,0},{4,5},{5,6},{6,7},{7,4},{8,9},{9,10},{10,1... | collective-permute-start | bytes 491528 | tf_op jit(solution)/shard_map/ppermute | solution.py:191
  75.4 17.4 %collective-permute-start.19 = (f32[210,16,128]{2,1,0:T(8,128)S(1)}, f32[210,16,128]{2,1,0:T(8,128)S(1)}, u32[]{:S(2)}, u32[]{:S(2)}) collective-permute-start(f32[210,16,128]{2,1,0:T(8,128)S(1)} %get-tuple-element.22), channel_id=1, source_target_pairs={{0,4},{4,0},{8,12},{12,8},{16,20},{20,16},{24,28},{28,24},{1,5},{5... | collective-permute-start | bytes 5160968 | tf_op jit(solution)/shard_map/ppermute | solution.py:185
  84.4 5.3 %collective-permute-start.18 = (bf16[16,1280]{1,0:T(8,128)(2,1)S(1)}, bf16[16,1280]{1,0:T(8,128)(2,1)S(1)}, u32[]{:S(2)}, u32[]{:S(2)}) collective-permute-start(bf16[16,1280]{1,0:T(8,128)(2,1)S(1)} %get-tuple-element.29), channel_id=1, source_target_pairs={{0,24},{4,28},{8,16},{12,20},{16,8},{20,12},{24,0},{28,4},{1,25},{... | collective-permute-start | bytes 122888 | tf_op jit(solution)/shard_map/ppermute | solution.py:188
  85.7 4.3 %collective-permute-start.17 = (bf16[16,1280]{1,0:T(8,128)(2,1)S(1)}, bf16[16,1280]{1,0:T(8,128)(2,1)S(1)}, u32[]{:S(2)}, u32[]{:S(2)}) collective-permute-start(bf16[16,1280]{1,0:T(8,128)(2,1)S(1)} %get-tuple-element.30), channel_id=1, source_target_pairs={{0,16},{4,20},{8,24},{12,28},{16,0},{20,4},{24,8},{28,12},{1,17},{... | collective-permute-start | bytes 122888 | tf_op jit(solution)/shard_map/ppermute | solution.py:188
  86.6 4.0 %collective-permute-start.16 = (bf16[16,1280]{1,0:T(8,128)(2,1)S(1)}, bf16[16,1280]{1,0:T(8,128)(2,1)S(1)}, u32[]{:S(2)}, u32[]{:S(2)}) collective-permute-start(bf16[16,1280]{1,0:T(8,128)(2,1)S(1)} %get-tuple-element.31), channel_id=1, source_target_pairs={{0,8},{4,12},{8,0},{12,4},{16,24},{20,28},{24,16},{28,20},{1,9},{5... | collective-permute-start | bytes 122888 | tf_op jit(solution)/shard_map/ppermute | solution.py:188
  87.9 6.3 %copy-start.7 = (bf16[64,2688]{1,0:T(8,128)(2,1)}, bf16[64,2688]{1,0:T(8,128)(2,1)S(1)}, u32[]{:S(2)}) copy-start(bf16[64,2688]{1,0:T(8,128)(2,1)S(1)} %slice_dynamic-update-slice_fusion) | copy-start | bytes 1032196

commit v2 on v0

v2 whole, which is shorter than its diff:
```python
import functools
import math

import jax
import jax.numpy as jnp
from jax import lax
from jax.experimental import pallas as pl
from jax.experimental.pallas import tpu as pltpu
from jax.sharding import PartitionSpec as P

SQRT_TWO_PI = 0.7978845608028654
CUBIC_COEF = 0.044715
BF16 = jnp.bfloat16
F32 = jnp.float32
VMEM = pltpu.VMEM
SMEM = pltpu.SMEM
MIB = 1 << 20


def gelu_pair(pre_act):
    gelu_inner = SQRT_TWO_PI * (pre_act + CUBIC_COEF * pre_act * pre_act * pre_act)
    tanh_inner = jnp.tanh(gelu_inner)
    act_value = 0.5 * pre_act * (1.0 + tanh_inner)
    act_slope = 0.5 * (1.0 + tanh_inner) + 0.5 * pre_act * (
        1.0 - tanh_inner * tanh_inner
    ) * SQRT_TWO_PI * (1.0 + 3.0 * CUBIC_COEF * pre_act * pre_act)
    return (act_value, act_slope)


def spec(space=VMEM):
    return pl.BlockSpec(memory_space=space)


def lane_regroup(chips, tile_width):
    size = chips * tile_width
    part = tile_width // chips
    column = lax.broadcasted_iota(jnp.int32, (1, size), 1)
    chip = column // tile_width
    inner = column % tile_width
    source = (inner // part) * tile_width + chip * part + inner % part
    row = lax.broadcasted_iota(jnp.int32, (size, size), 0)
    return jnp.where(row == source, 1.0, 0.0).astype(BF16)


def split_kernel(parts, tile_width, place_ref, tokens_ref, out_ref, onehot_ref):
    size = parts * tile_width
    rows = tokens_ref.shape[0]
    onehot_ref[...] = lane_regroup(parts, tile_width)
    me = place_ref[0]
    groups = tokens_ref.shape[1] // size
    lanes = jnp.concatenate(
        [tokens_ref[:, group * size : (group + 1) * size] for group in range(groups)], axis=0
    )
    picked = jnp.dot(lanes, onehot_ref[...], preferred_element_type=F32).astype(BF16)
    for part in range(parts):
        for group in range(groups):
            out_ref[me ^ part, :, group * tile_width : (group + 1) * tile_width] = picked[
                group * rows : (group + 1) * rows, part * tile_width : (part + 1) * tile_width
            ]


def join_kernel(parts, tile_width, groups_of, place_ref, onehot_ref, *refs):
    *part_refs, out_ref, held = refs
    size = parts * tile_width
    rows = out_ref.shape[0]
    me = place_ref[0]
    groups = out_ref.shape[1] // size
    first = 0
    for index, count in enumerate(groups_of):
        for step in range(count):
            own_ref, near_ref, far_ref = part_refs[3 * index : 3 * index + 3]
            total = own_ref[step] + near_ref[0, step].astype(F32) + far_ref[step].astype(F32)
            total = total.astype(BF16)
            for half in range(2):
                for group in range(groups):
                    at = (half * groups + group) * tile_width
                    held[me ^ (2 * (first + step) + half), group * rows : (group + 1) * rows] = (
                        total[:, at : at + tile_width]
                    )
        first += count
    lanes = jnp.concatenate([held[part] for part in range(parts)], axis=1)
    result = jnp.dot(lanes, onehot_ref[...], preferred_element_type=F32).astype(BF16)
    for group in range(groups):
        out_ref[:, group * size : (group + 1) * size] = result[group * rows : (group + 1) * rows]


def place_tiles(half, row_ref, col_ref, tiles_ref, out_ref, first=0):
    slots, rows, width = tiles_ref.shape
    start = half * (out_ref.shape[0] // 2)

    def place(slot, carry):
        top = pl.multiple_of(row_ref[0, first + slot] * rows + start, rows)
        left = pl.multiple_of(col_ref[0, first + slot] * width, width)
        out_ref[pl.ds(top, rows), pl.ds(left, width)] = tiles_ref[slot]
        return carry

    lax.fori_loop(0, slots, place, 0, unroll=15)


def weight_kernel(order_ref, row_ref, col_ref, own_ref, other_ref, w_ref):
    w_ref[...] = jnp.zeros_like(w_ref)
    place_tiles(0, row_ref, col_ref, own_ref, w_ref)
    place_tiles(1, row_ref, col_ref, other_ref, w_ref)


def early_kernel(n_tp, step, w_ref, *refs):
    x_refs = refs[:n_tp]
    *early_refs, sum_ref = refs[n_tp:]
    product = jnp.dot(slice_rows(x_refs, step), w_ref[...], preferred_element_type=F32)
    sum_ref[...] = product + early_refs[0][...] if early_refs else product


def halves_kernel(first_ref, second_ref, lower_ref, upper_ref):
    lower_ref[...] = first_ref[: lower_ref.shape[0]]
    upper_ref[...] = second_ref[lower_ref.shape[0] :]


def half_weight_kernel(order_ref, row_ref, col_ref, lower_ref, upper_ref, out_ref):
    out_ref[...] = jnp.zeros_like(out_ref)
    place_tiles(0, row_ref, col_ref, lower_ref, out_ref)
    place_tiles(0, row_ref, col_ref, upper_ref, out_ref, lower_ref.shape[0])


def gather_kernel(chips, n_tp, *refs):
    x_refs = refs[:n_tp]
    out_refs = refs[n_tp:]
    for step in range(chips):
        out_refs[step][...] = slice_rows(x_refs, step)


def transpose_kernel(order_ref, *refs):
    *part_refs, out_ref = refs
    out_ref[...] = jnp.concatenate([part_ref[...] for part_ref in part_refs], axis=0).T


def slice_rows(x_refs, step):
    return jnp.concatenate(
        [jnp.concatenate([x_ref[2 * step], x_ref[2 * step + 1]], axis=1) for x_ref in x_refs],
        axis=0,
    )


def hidden_kernel(n_tp, step, order_ref, z_ref, row_ref, col_ref, lower_ref, upper_ref, early_ref, cotangent_ref, half_ref, *refs):
    x_refs = refs[:n_tp]
    w_ref, act_ref, grad_ref = refs[n_tp:]
    rows = x_refs[0].shape[1]
    place_tiles(1, row_ref, col_ref, lower_ref, w_ref)
    place_tiles(1, row_ref, col_ref, upper_ref, w_ref, lower_ref.shape[0])
    lhs = slice_rows(x_refs, step)
    for left, right in column_blocks(w_ref.shape[1]):
        hidden = early_ref[:, left:right] + jnp.dot(
            lhs, w_ref[:, left:right], preferred_element_type=F32
        )
        act_value, act_slope = gelu_pair(hidden)
        act_value = act_value.astype(BF16)
        for j in range(n_tp):
            at = pl.ds(pl.multiple_of((z_ref[0] ^ j) * rows, rows), rows)
            act_ref[at, left:right] = act_value[j * rows : (j + 1) * rows]
            slope = act_slope[j * rows : (j + 1) * rows]
            grad_ref[j * rows : (j + 1) * rows, left:right] = (
                cotangent_ref[at, left:right].astype(F32) * slope
            ).astype(BF16)


def column_blocks(columns, block=512):
    return [(left, min(left + block, columns)) for left in range(0, columns, block)]


def back_kernel(n_tp, first, count, g_ref, *refs):
    w_refs = refs[:count]
    own_ref, near_ref, far_ref = refs[-3:]
    rows = g_ref.shape[0] // n_tp
    for step in range(count):
        result = lax.dot_general(
            g_ref[...], w_refs[step][...], (((1,), (1,)), ((), ())), preferred_element_type=F32
        )
        own_ref[first + step] = result[:rows]
        near_ref[0, first + step] = result[rows : 2 * rows].astype(BF16)
        near_ref[1, first + step] = result[3 * rows :].astype(BF16)
        far_ref[first + step] = result[2 * rows : 3 * rows]


def tile_grad_kernel(chips, scale, core_ref, row_ref, col_ref, x_ref, *refs):
    g_refs = refs[:chips]
    mine_ref, theirs_ref, dense = refs[chips:]
    slots, tile_rows, width = mine_ref.shape
    half = dense.shape[0] // 2
    for left, right in column_blocks(dense.shape[1]):
        g_all = jnp.concatenate([g_ref[:, left:right] for g_ref in g_refs], axis=0)
        dense[:, left:right] = jnp.dot(x_ref[...], g_all, preferred_element_type=F32)

    def place_tile(slot, carry):
        top = pl.multiple_of(row_ref[0, slot] * tile_rows, tile_rows)
        left = pl.multiple_of(col_ref[0, slot] * width, width)
        low = pl.multiple_of(top + half, tile_rows)
        mine_ref[slot] = dense[pl.ds(top, tile_rows), pl.ds(left, width)] * scale
        theirs_ref[slot] = (dense[pl.ds(low, tile_rows), pl.ds(left, width)] * scale).astype(
            theirs_ref.dtype
        )
        return carry

    lax.fori_loop(0, slots, place_tile, 0, unroll=15)


def params(limit):
    return pltpu.CompilerParams(vmem_limit_bytes=limit * MIB)


def cost(flops, bytes_accessed):
    return pl.CostEstimate(flops=flops >> 12, bytes_accessed=bytes_accessed >> 12, transcendentals=0)


def local(tokens, tile_values, tile_row, tile_col, grad_act):
    fsdp = lax.axis_size("fsdp")
    n_tp = lax.axis_size("tp")
    chips = fsdp // 2
    rows, width = tokens.shape
    tile_rows, slots, tile_width = tile_values.shape
    row_tiles = width // tile_width
    columns = grad_act.shape[1]
    col_tiles = columns // tile_width
    depth = row_tiles * 2 * tile_rows
    total_tokens = rows * fsdp * n_tp
    grad_scale = 1.0 / math.sqrt(total_tokens)
    place = lax.axis_index("fsdp")
    chip = place // 2
    core = place % 2
    z = lax.axis_index("tp")
    paired = n_tp & (n_tp - 1) == 0
    fast = (
        tile_rows % 16 == 0 and rows % 16 == 0 and row_tiles % fsdp == 0 and n_tp == 4 and chips == 4
    )

    def to_core(value):
        return lax.ppermute(value, "fsdp", [(f, f ^ 1) for f in range(fsdp)])

    def to_chip(value, step):
        return lax.ppermute(value, "fsdp", [(f, f ^ (2 * step)) for f in range(fsdp)])

    def to_z(value, step):
        if paired:
            return lax.ppermute(value, "tp", [(i, i ^ step) for i in range(n_tp)])
        return lax.ppermute(value, "tp", [(i, (i + step) % n_tp) for i in range(n_tp)])

    def from_z(value, step):
        return to_z(value, step if paired else n_tp - step)

    def z_rows(step):
        return (z ^ step if paired else (z - step) % n_tp) * rows

    def after(value, *earlier):
        return lax.optimization_barrier((value, *earlier))[0]

    def along_z(value):
        parts = [value]
        for j in range(1, n_tp):
            parts.append(to_z(parts[2], 1) if paired and j == 3 else to_z(value, j))
        return parts

    z_index = z.astype(jnp.int32).reshape(1)

    place_index = place.astype(jnp.int32).reshape(1)
    tiles = [jnp.transpose(tile_values, (1, 0, 2))]
    block = rows * n_tp
    if fast:
        def make_weight(step, order):
            return pl.pallas_call(
                weight_kernel,
                out_shape=jax.ShapeDtypeStruct((depth, columns), BF16),
                in_specs=[spec(SMEM)] * 3 + [spec()] * 2,
                out_specs=spec(),
                compiler_params=params(10),
                cost_estimate=cost(0, 2 * 2 * depth * columns),
            )(order, tile_row, tile_col, tiles[step], others[step])

        def add_hidden(step, *early):
            return pl.pallas_call(
                functools.partial(early_kernel, n_tp, step),
                out_shape=jax.ShapeDtypeStruct((block, columns), F32),
                in_specs=[spec()] * (1 + n_tp + len(early)),
                out_specs=spec(),
                compiler_params=params(14),
                cost_estimate=cost(2 * block * depth * columns, 2 * depth * columns),
            )(weights[step], *token_parts, *early)

        others = [to_core(tiles[0])]
        split, onehot = pl.pallas_call(
            functools.partial(split_kernel, fsdp, tile_width),
            out_shape=[
                jax.ShapeDtypeStruct((fsdp, rows, depth // 2), BF16),
                jax.ShapeDtypeStruct((fsdp * tile_width, fsdp * tile_width), BF16),
            ],
            in_specs=[spec(SMEM), spec()],
            out_specs=[spec()] * 2,
            compiler_params=params(8),
        )(place_index, tokens)
        token_parts = along_z(split)
        tiles += [to_chip(tiles[0], 1), to_chip(tiles[0], 2)]
        weights = [make_weight(0, z_index)]
        tiles[1], tiles[2], *_ = lax.optimization_barrier(
            (tiles[1], tiles[2], *token_parts[1:], weights[0])
        )
        half = slots // 2
        relay = pl.pallas_call(
            halves_kernel,
            out_shape=[
                jax.ShapeDtypeStruct((half, tile_rows, tile_width), BF16),
                jax.ShapeDtypeStruct((slots - half, tile_rows, tile_width), BF16),
            ],
            in_specs=[spec()] * 2,
            out_specs=[spec()] * 2,
            compiler_params=params(8),
        )(tiles[1], tiles[2])
        relayed = [to_chip(relay[0], 2), to_chip(relay[1], 1)]
        others += [to_core(part) for part in tiles[1:]]
        for step in range(1, chips - 1):
            weights.append(make_weight(step, after(z_index, weights[-1], *relay)))
        mine = pl.pallas_call(
            functools.partial(gather_kernel, chips, n_tp),
            out_shape=[jax.ShapeDtypeStruct((block, depth), BF16)] * chips,
            in_specs=[spec()] * n_tp,
            out_specs=[spec()] * chips,
            compiler_params=params(8),
        )(after(token_parts[0], weights[1]), *token_parts[1:])
        early = add_hidden(0)
        for step in range(1, chips - 1):
            early = add_hidden(step, early)
        *relayed, _ = lax.optimization_barrier((*relayed, early))
        last_others = [to_core(part) for part in relayed]
    else:
        tiles += [to_chip(tiles[0], step) for step in range(1, chips)]
        others = [to_core(part) for part in tiles]
        split = jnp.transpose(
            tokens.reshape(rows, row_tiles, chips, tile_width // chips), (2, 0, 1, 3)
        ).reshape(chips, rows, depth)
        split = jnp.take(split, jnp.arange(chips) ^ chip, axis=0)
        token_parts = along_z(split)
        pieces = [split[0]] + [to_chip(split[step], step) for step in range(1, chips)]
        slice_parts = along_z(jnp.stack(pieces))

    if fast:
        half_weight = pl.pallas_call(
            half_weight_kernel,
            out_shape=jax.ShapeDtypeStruct((depth, columns), BF16),
            in_specs=[spec(SMEM)] * 3 + [spec()] * 2,
            out_specs=spec(),
            compiler_params=params(10),
            cost_estimate=cost(0, 2 * 2 * depth * columns),
        )(z_index, tile_row, tile_col, *relayed)
        slices = pl.pallas_call(
            transpose_kernel,
            out_shape=jax.ShapeDtypeStruct((depth, chips * block), BF16),
            in_specs=[spec(SMEM)] + [spec()] * chips,
            out_specs=spec(),
            compiler_params=params(8),
        )(
            z_index,
            mine[0],
            *[to_chip(mine[step], step) for step in range(1, chips)],
        )
        last_weight, act, hidden_grad = pl.pallas_call(
            functools.partial(hidden_kernel, n_tp, chips - 1),
            out_shape=[
                jax.ShapeDtypeStruct((depth, columns), BF16),
                jax.ShapeDtypeStruct((block, columns), BF16),
                jax.ShapeDtypeStruct((block, columns), BF16),
            ],
            in_specs=[spec(SMEM)] * 4 + [spec()] * (5 + n_tp),
            out_specs=[spec()] * 3,
            input_output_aliases={8: 0},
            compiler_params=params(20),
            cost_estimate=cost(2 * block * depth * columns, 2 * depth * columns),
        )(
            after(z_index, slices), z_index, tile_row, tile_col, *last_others, early, grad_act, half_weight,
            *token_parts,
        )
        weights.append(last_weight)
    else:
        mine = jnp.stack(tiles, axis=1)
        theirs = jnp.stack(others, axis=1)
        both = jnp.where(
            core == 0,
            jnp.concatenate([mine, theirs], axis=2),
            jnp.concatenate([theirs, mine], axis=2),
        )
        flat = tile_row[0] * col_tiles + tile_col[0]
        weight = jnp.zeros((row_tiles * col_tiles, chips, 2 * tile_rows, tile_width), BF16)
        weight = weight.at[flat].set(both, unique_indices=True)
        weight = jnp.transpose(
            weight.reshape(row_tiles, col_tiles, chips, 2 * tile_rows, tile_width),
            (2, 0, 3, 1, 4),
        ).reshape(chips, depth, columns)
        hidden = jnp.einsum(
            "jqrk,qkc->jrc", jnp.stack(token_parts), weight, preferred_element_type=F32
        )
        act_value, act_slope = gelu_pair(hidden)
        act_value = act_value.astype(BF16)
        cotangent = jnp.stack(
            [lax.dynamic_slice_in_dim(grad_act, z_rows(j), rows, axis=0) for j in range(n_tp)]
        )
        hidden_grad = (cotangent.astype(F32) * act_slope).astype(BF16).reshape(block, columns)
        act = jnp.zeros((block, columns), BF16)
        for j in range(n_tp):
            act = lax.dynamic_update_slice_in_dim(act, act_value[j], z_rows(j), axis=0)

    grads = [hidden_grad] + [to_chip(hidden_grad, step) for step in range(1, chips)]

    if fast:
        group_sizes = (chips,)
        backs = []
        for first in range(0, chips, 2):
            backs = pl.pallas_call(
                functools.partial(back_kernel, n_tp, first, 2),
                out_shape=[
                    jax.ShapeDtypeStruct((chips, rows, depth), F32),
                    jax.ShapeDtypeStruct((2, chips, rows, depth), BF16),
                    jax.ShapeDtypeStruct((chips, rows, depth), F32),
                ],
                in_specs=[spec()] * (3 + len(backs)),
                out_specs=[spec()] * 3,
                input_output_aliases={3: 0, 4: 1, 5: 2} if backs else {},
                compiler_params=params(18),
                cost_estimate=cost(4 * block * depth * columns, 4 * depth * columns),
            )(hidden_grad, *weights[first : first + 2], *backs)
        near = to_z(backs[1], 1)
        far = to_z((backs[2] + near[1].astype(F32)).astype(BF16), 2)
        returned = [[backs[0], near, far]]
        grad_tokens = pl.pallas_call(
            functools.partial(join_kernel, fsdp, tile_width, group_sizes),
            out_shape=jax.ShapeDtypeStruct((rows, width), BF16),
            in_specs=[spec(SMEM)] + [spec()] * (1 + 3 * len(group_sizes)),
            out_specs=spec(),
            scratch_shapes=[pltpu.VMEM((fsdp, rows * row_tiles // fsdp, tile_width), BF16)],
            compiler_params=params(8),
        )(place_index, onehot, *[part for group in returned for part in group])
        mine, theirs = pl.pallas_call(
            functools.partial(tile_grad_kernel, chips, grad_scale),
            out_shape=[
                jax.ShapeDtypeStruct((slots, tile_rows, tile_width), F32),
                jax.ShapeDtypeStruct((slots, tile_rows, tile_width), BF16),
            ],
            in_specs=[spec(SMEM)] * 3 + [spec()] * (1 + chips),
            out_specs=[spec()] * 2,
            scratch_shapes=[pltpu.VMEM((depth, columns), F32)],
            compiler_params=params(26),
            cost_estimate=cost(2 * chips * block * depth * columns, 4 * depth * columns),
        )(z_index, tile_row, tile_col, slices, *grads)
        grad_tiles = mine + to_core(theirs).astype(F32)
    else:
        backs = jnp.einsum(
            "jrc,qkc->jqrk",
            hidden_grad.reshape(n_tp, rows, columns),
            weight,
            preferred_element_type=F32,
        )
        total = backs[0]
        for j in range(1, n_tp):
            total = total + from_z(backs[j].astype(BF16), j).astype(F32)
        joined = jnp.take(total.astype(BF16), jnp.arange(chips) ^ chip, axis=0)
        grad_tokens = jnp.transpose(
            joined.reshape(chips, rows, row_tiles, tile_width // chips), (1, 2, 0, 3)
        ).reshape(rows, width)
        x_all = jnp.stack(slice_parts, axis=1).reshape(-1, depth)
        g_all = jnp.stack(grads).reshape(-1, columns)
        dense = jnp.einsum("tk,tn->kn", x_all, g_all, preferred_element_type=F32) * grad_scale
        dense = jnp.transpose(
            dense.reshape(row_tiles, 2, tile_rows, col_tiles, tile_width), (1, 0, 3, 2, 4)
        ).reshape(2, row_tiles * col_tiles, tile_rows, tile_width)
        picked = jnp.take(dense, tile_row[0] * col_tiles + tile_col[0], axis=1)
        mine = jnp.where(core == 0, picked[0], picked[1])
        theirs = jnp.where(core == 0, picked[1], picked[0])
        grad_tiles = mine + to_core(theirs)
    grad_tiles = jnp.transpose(grad_tiles, (1, 0, 2))
    return (act, grad_tokens, grad_tiles)


def solution(mesh):
    in_specs = (
        P(("fsdp", "tp"), None),
        P("fsdp", "tp", None),
        P("tp", None),
        P("tp", None),
        P("fsdp", "tp"),
    )
    out_specs = (P("fsdp", "tp"), P(("fsdp", "tp"), None), P("fsdp", "tp", None))
    return jax.shard_map(local, mesh=mesh, in_specs=in_specs, out_specs=out_specs, check_vma=False)
```

time: 269 us -> 88.3 us (0.33)
  waiting for transfers between devices: 130 us -> 25.8 us
  matrix products: 55.2 us -> 0 us
  Pallas kernels: 0 us -> 31.3 us
  local copies, waits for them, and re-layouts: 32.5 us -> 4.78 us
  starting transfers between devices: 0.12 us -> 23.9 us
  blocking collectives: 20 us -> 0 us
  other arithmetic: 16.1 us -> 1.5 us
  between operations: 13.8 us -> 0.87 us
    reduce_scatter x2 -> x0, waiting for transfers between devices: 96.8 us -> none  [the longest x1 96.8 us: local(): lax.psum_scatter(total * grad_scale, 'fsdp', scatter_dimension=0, tiled=T...]
    dot_general x10 -> x0, matrix products: 55.2 us -> none  [the longest x2 18 us: add_block(): jnp.einsum('rnk,rnj->knj', chosen, grad_chosen, preferred_element_type=jn...]
    all_gather x1 -> x0, waiting for transfers between devices: 32.7 us -> none  [local(): whole_tiles = lax.all_gather(tile_values, 'fsdp', axis=0, tiled=True)]
    pallas_call x0 -> x16, Pallas kernels: none -> 31.3 us  [the longest x2 8.57 us: local(): pl.pallas_call(functools.partial(back_kernel, n_tp, first, 2), out_shape=...]
    ppermute x0 -> x21, waiting for transfers between devices: none -> 25.8 us  [the longest x5 14.7 us: to_z(): return lax.ppermute(value, 'tp', [(i, i ^ step) for i in range(n_tp)])]
    ppermute x0 -> x21, starting transfers between devices: none -> 23.9 us  [the longest x10 13.2 us: to_chip(): return lax.ppermute(value, 'fsdp', [(f, f ^ 2 * step) for f in range(fsdp)])]
    all_gather x1 -> x0, blocking collectives: 20 us -> none  [local(): gathered = lax.all_gather(tokens, 'tp', axis=0, tiled=True)]
    while x17 -> x0, local copies, waits for them, and re-layouts: 18.1 us -> none  [the longest x1 14.6 us: local(): lax.scan(add_block, jnp.zeros((tile_values.shape[0] * lax.axis_size('fsdp...]
  transfers between devices with their start and end apart: 3 -> 21, of which waited for: 2 -> 8; matrix products, arithmetic and copies ran while one was open for 20% -> 0% of each run, Pallas kernels for 0% -> 31%
where the time goes in v2:
time: 88.3 us; the launch traced here: 88.1 us
  Pallas kernels  31.3 us (35%)
  waiting for transfers between devices  25.8 us (29%)
  starting transfers between devices  23.9 us (27%)
  local copies, waits for them, and re-layouts  4.78 us (5%)
  other arithmetic  1.5 us (2%)
    ppermute x5, waiting for transfers between devices, to_z(): return lax.ppermute(value, 'tp', [(i, i ^ step) for i in range(n_tp)])  14.7 us
    ppermute x10, starting transfers between devices, to_chip(): return lax.ppermute(value, 'fsdp', [(f, f ^ 2 * step) for f in range(fsdp)])  13.2 us
    ppermute x10, waiting for transfers between devices, to_chip(): return lax.ppermute(value, 'fsdp', [(f, f ^ 2 * step) for f in range(fsdp)])  11 us
    ppermute x5, starting transfers between devices, to_z(): return lax.ppermute(value, 'tp', [(i, i ^ step) for i in range(n_tp)])  9.06 us
    pallas_call x2, Pallas kernels, local(): pl.pallas_call(functools.partial(back_kernel, n_tp, first, 2), out_shape=...  8.57 us
    pallas_call x3, Pallas kernels, make_weight(): pl.pallas_call(weight_kernel, out_shape=jax.ShapeDtypeStruct((depth, colu...  7.44 us
    unnamed x18, local copies, waits for them, and re-layouts  4.78 us
    pallas_call x3, Pallas kernels, add_hidden(): pl.pallas_call(functools.partial(early_kernel, n_tp, step), out_shape=jax...  3.91 us
  transfers between devices with their start and end apart: 21, of which 8 were waited for; matrix products, arithmetic and copies ran while one was open for 0% of the time, Pallas kernels for 31%

profile of v2, /device:TPU:0, one launch (start us, length us, event | category | flops | bytes accessed | tf_op | source)
XLA Modules:
  0.0 88.1 jit_solution(2175217328535327763)
XLA Ops:
  1.1 2.6 %collective-permute-start.2 = (bf16[210,16,128]{2,1,0:T(8,128)(2,1)}, bf16[210,16,128]{2,1,0:T(8,128)(2,1)S(1)}, u32[]{:S(2)}, u32[]{:S(2)}) collective-permute-start(bf16[210,16,128]{2,1,0:T(8,128)(2,1)} %bitcast.11), channel_id=1, source_target_pairs={{0,16},{4,20},{8,24},{12,28},{16,0},{20,4},{24,8},{28,12},{1,17},{... | collective-permute-start | bytes 2580488 | tf_op jit(solution)/shard_map/ppermute | solution.py:238
  3.7 1.5 %collective-permute-start.1 = (bf16[210,16,128]{2,1,0:T(8,128)(2,1)}, bf16[210,16,128]{2,1,0:T(8,128)(2,1)S(1)}, u32[]{:S(2)}, u32[]{:S(2)}) collective-permute-start(bf16[210,16,128]{2,1,0:T(8,128)(2,1)} %bitcast.12), channel_id=1, source_target_pairs={{0,8},{4,12},{8,0},{12,4},{16,24},{20,28},{24,16},{28,20},{1,9},{5... | collective-permute-start | bytes 2580488 | tf_op jit(solution)/shard_map/ppermute | solution.py:238
  5.2 0.9 %copy-done.4 = bf16[16,5120]{1,0:T(8,128)(2,1)S(1)} copy-done((bf16[16,5120]{1,0:T(8,128)(2,1)S(1)}, bf16[16,5120]{1,0:T(8,128)(2,1)}, u32[]{:S(2)}) %copy-start.4) | copy-done | bytes 163864
  6.8 1.3 %copy-done = bf16[1024,1024]{1,0:T(8,128)(2,1)} copy-done((bf16[1024,1024]{1,0:T(8,128)(2,1)}, bf16[1024,1024]{1,0:T(8,128)(2,1)S(1)}, u32[]{:S(2)}) %copy-start) | copy-done | bytes 2097176
  8.2 2.6 %collective-permute-start.4 = (bf16[8,16,640]{2,1,0:T(8,128)(2,1)S(1)}, bf16[8,16,640]{2,1,0:T(8,128)(2,1)S(1)}, u32[]{:S(2)}, u32[]{:S(2)}) collective-permute-start(bf16[8,16,640]{2,1,0:T(8,128)(2,1)S(1)} %get-tuple-element.36.refs_0_), channel_id=1, source_target_pairs={{0,2},{1,3},{2,0},{3,1},{4,6},{5,7},{6,4},{7,5},{8,10},{9,11},{10,... | collective-permute-start | bytes 491528 | tf_op jit(solution)/shard_map/ppermute | solution.py:242
  10.8 1.6 %collective-permute-start.3 = (bf16[8,16,640]{2,1,0:T(8,128)(2,1)S(1)}, bf16[8,16,640]{2,1,0:T(8,128)(2,1)S(1)}, u32[]{:S(2)}, u32[]{:S(2)}) collective-permute-start(bf16[8,16,640]{2,1,0:T(8,128)(2,1)S(1)} %get-tuple-element.36.refs_0_), channel_id=1, source_target_pairs={{0,1},{1,0},{2,3},{3,2},{4,5},{5,4},{6,7},{7,6},{8,9},{9,8},{10,11... | collective-permute-start | bytes 491528 | tf_op jit(solution)/shard_map/ppermute | solution.py:242
  12.3 6.3 %collective-permute-done.4.refs_2_ = bf16[8,16,640]{2,1,0:T(8,128)(2,1)S(1)} collective-permute-done((bf16[8,16,640]{2,1,0:T(8,128)(2,1)S(1)}, bf16[8,16,640]{2,1,0:T(8,128)(2,1)S(1)}, u32[]{:S(2)}, u32[]{:S(2)}) %collective-permute-start.4) | collective-permute-done | bytes 163872 | tf_op jit(solution)/shard_map/ppermute | solution.py:242
  19.3 1.2 %copy-done.2 = bf16[16,210,128]{2,0,1:T(8,128)(2,1)S(1)} copy-done((bf16[16,210,128]{2,0,1:T(8,128)(2,1)S(1)}, bf16[16,210,128]{2,0,1:T(8,128)(2,1)}, u32[]{:S(2)}) %copy-start.2) | copy-done | bytes 860184
  21.8 2.5 %shard_map.77.w_ref.refs_0_ = bf16[1280,2688]{1,0:T(8,128)(2,1)S(1)} custom-call(s32[1]{0:T(128)} %bitcast.order_ref.z_ref.core_ref, s32[1,210]{1,0:T(1,128)S(1)} %copy-done.5, s32[1,210]{1,0:T(1,128)S(1)} %copy-done.7, bf16[210,16,128]{2,1,0:T(8,128)(2,1)S(1)} %bitcast.13, bf16[210,16,128]{2,1,0:T(8,128)(2,1)S(1)} %collective-permute-done.other_ref), custom_call_target="tpu_custom_call" | custom-call | bytes 3360 | tf_op jit(solution)/shard_map/pallas_call | solution.py:267
  26.1 1.7 %collective-permute-start.11 = (bf16[105,16,128]{2,1,0:T(8,128)(2,1)S(1)}, bf16[105,16,128]{2,1,0:T(8,128)(2,1)S(1)}, u32[]{:S(2)}, u32[]{:S(2)}) collective-permute-start(bf16[105,16,128]{2,1,0:T(8,128)(2,1)S(1)} %get-tuple-element.34), channel_id=1, source_target_pairs={{0,8},{4,12},{8,0},{12,4},{16,24},{20,28},{24,16},{28,20},{1,9},{5... | collective-permute-start | bytes 1290248 | tf_op jit(solution)/shard_map/ppermute | solution.py:238
  27.8 1.3 %shard_map.83.refs_4_ = f32[64,2688]{1,0:T(8,128)S(1)} custom-call(bf16[1280,2688]{1,0:T(8,128)(2,1)S(1)} %shard_map.77.w_ref.refs_0_, bf16[8,16,640]{2,1,0:T(8,128)(2,1)S(1)} %get-tuple-element.36.refs_0_, bf16[8,16,640]{2,1,0:T(8,128)(2,1)S(1)} %collective-permute-done.3.refs_1_, bf16[8,16,640]{2,1,0:T(8,128)(2,1)S(1)} %collective-permute-done.4.refs_2_, ...), custom_call_target="tpu_custom_call" | custom-call | flops 107520 | bytes 1680 | tf_op jit(solution)/shard_map/pallas_call | solution.py:277
  29.1 2.5 %shard_map.79.w_ref.refs_1_ = bf16[1280,2688]{1,0:T(8,128)(2,1)S(1)} custom-call(s32[1]{0:T(128)} %bitcast.order_ref.z_ref.core_ref, s32[1,210]{1,0:T(1,128)S(1)} %copy-done.6, s32[1,210]{1,0:T(1,128)S(1)} %copy-done.8, bf16[210,16,128]{2,1,0:T(8,128)(2,1)S(1)} %collective-permute-done.1.first_ref.own_ref, ...), custom_call_target="tpu_custom_call" | custom-call | bytes 3360 | tf_op jit(solution)/shard_map/pallas_call | solution.py:267
  31.6 1.3 %shard_map.84.refs_4_ = f32[64,2688]{1,0:T(8,128)S(1)} custom-call(bf16[1280,2688]{1,0:T(8,128)(2,1)S(1)} %shard_map.79.w_ref.refs_1_, bf16[8,16,640]{2,1,0:T(8,128)(2,1)S(1)} %get-tuple-element.36.refs_0_, bf16[8,16,640]{2,1,0:T(8,128)(2,1)S(1)} %collective-permute-done.3.refs_1_, bf16[8,16,640]{2,1,0:T(8,128)(2,1)S(1)} %collective-permute-done.4.refs_2_, ...), custom_call_target="tpu_custom_call" | custom-call | flops 107520 | bytes 1680 | tf_op jit(solution)/shard_map/pallas_call | solution.py:277
  32.9 2.5 %shard_map.82.w_ref.refs_0_ = bf16[1280,2688]{1,0:T(8,128)(2,1)S(1)} custom-call(s32[1]{0:T(128)} %bitcast.order_ref.z_ref.core_ref, s32[1,210]{1,0:T(1,128)S(1)} %copy-done.6, s32[1,210]{1,0:T(1,128)S(1)} %copy-done.8, bf16[210,16,128]{2,1,0:T(8,128)(2,1)S(1)} %collective-permute-done.2.second_ref.own_ref, ...), custom_call_target="tpu_custom_call" | custom-call | bytes 3360 | tf_op jit(solution)/shard_map/pallas_call | solution.py:267
  35.4 1.3 %shard_map.85.early_ref = f32[64,2688]{1,0:T(8,128)S(1)} custom-call(bf16[1280,2688]{1,0:T(8,128)(2,1)S(1)} %shard_map.82.w_ref.refs_0_, bf16[8,16,640]{2,1,0:T(8,128)(2,1)S(1)} %get-tuple-element.36.refs_0_, bf16[8,16,640]{2,1,0:T(8,128)(2,1)S(1)} %collective-permute-done.3.refs_1_, bf16[8,16,640]{2,1,0:T(8,128)(2,1)S(1)} %collective-permute-done.4.refs_2_, ...), custom_call_target="tpu_custom_call" | custom-call | flops 107520 | bytes 1680 | tf_op jit(solution)/shard_map/pallas_call | solution.py:277
  38.3 1.7 %collective-permute-start.7 = (bf16[64,1280]{1,0:T(8,128)(2,1)S(1)}, bf16[64,1280]{1,0:T(8,128)(2,1)S(1)}, u32[]{:S(2)}, u32[]{:S(2)}) collective-permute-start(bf16[64,1280]{1,0:T(8,128)(2,1)S(1)} %get-tuple-element.38), channel_id=1, source_target_pairs={{0,8},{4,12},{8,0},{12,4},{16,24},{20,28},{24,16},{28,20},{1,9},{5... | collective-permute-start | bytes 491528 | tf_op jit(solution)/shard_map/ppermute | solution.py:238
  39.9 1.5 %collective-permute-start.8 = (bf16[64,1280]{1,0:T(8,128)(2,1)S(1)}, bf16[64,1280]{1,0:T(8,128)(2,1)S(1)}, u32[]{:S(2)}, u32[]{:S(2)}) collective-permute-start(bf16[64,1280]{1,0:T(8,128)(2,1)S(1)} %get-tuple-element.39), channel_id=1, source_target_pairs={{0,16},{4,20},{8,24},{12,28},{16,0},{20,4},{24,8},{28,12},{1,17},{... | collective-permute-start | bytes 491528 | tf_op jit(solution)/shard_map/ppermute | solution.py:238
  41.8 1.7 %shard_map.86.half_ref = bf16[1280,2688]{1,0:T(8,128)(2,1)S(1)} custom-call(s32[1]{0:T(128)} %bitcast.order_ref.z_ref.core_ref, s32[1,210]{1,0:T(1,128)S(1)} %copy-done.6, s32[1,210]{1,0:T(1,128)S(1)} %copy-done.8, bf16[105,16,128]{2,1,0:T(8,128)(2,1)S(1)} %collective-permute-done.10.lower_ref, bf16[105,16,128]{2,1,0:T(8,128)(2,1)S(1)} %collective-permute-done.11.upper_ref), custom_call_target="tpu_custom_call" | custom-call | bytes 3360 | tf_op jit(solution)/shard_map/pallas_call | solution.py:342
  43.6 1.8 %collective-permute-done.7.refs_1_ = bf16[64,1280]{1,0:T(8,128)(2,1)S(1)} collective-permute-done((bf16[64,1280]{1,0:T(8,128)(2,1)S(1)}, bf16[64,1280]{1,0:T(8,128)(2,1)S(1)}, u32[]{:S(2)}, u32[]{:S(2)}) %collective-permute-start.7) | collective-permute-done | bytes 163872 | tf_op jit(solution)/shard_map/ppermute | solution.py:238
  45.4 3.9 %collective-permute-done.8.refs_2_ = bf16[64,1280]{1,0:T(8,128)(2,1)S(1)} collective-permute-done((bf16[64,1280]{1,0:T(8,128)(2,1)S(1)}, bf16[64,1280]{1,0:T(8,128)(2,1)S(1)}, u32[]{:S(2)}, u32[]{:S(2)}) %collective-permute-start.8) | collective-permute-done | bytes 163872 | tf_op jit(solution)/shard_map/ppermute | solution.py:238
  49.5 3.7 %shard_map.87 = (bf16[1280,2688]{1,0:T(8,128)(2,1)S(1)}, bf16[64,2688]{1,0:T(8,128)(2,1)}, bf16[64,2688]{1,0:T(8,128)(2,1)S(1)}) custom-call(s32[1]{0:T(128)} %bitcast.order_ref.z_ref.core_ref, s32[1]{0:T(128)} %bitcast.order_ref.z_ref.core_ref, s32[1,210]{1,0:T(1,128)S(1)} %copy-done.6, s32[1,210]{1,0:T(1,128)S(1)} %copy-done.8, ...), custom_call_target="tpu_custom_call", output_to_operand_aliasing={{0}: (8, {})} | custom-call | flops 107520 | bytes 1680 | tf_op jit(solution)/shard_map/pallas_call | solution.py:361
  53.3 1.5 %collective-permute-start.19 = (bf16[64,2688]{1,0:T(8,128)(2,1)S(1)}, bf16[64,2688]{1,0:T(8,128)(2,1)S(1)}, u32[]{:S(2)}, u32[]{:S(2)}) collective-permute-start(bf16[64,2688]{1,0:T(8,128)(2,1)S(1)} %get-tuple-element.47.g_ref.refs_0_), channel_id=1, source_target_pairs={{0,24},{4,28},{8,16},{12,20},{16,8},{20,12},{24,0},{28,4},{1,25},{... | collective-permute-start | bytes 1032200 | tf_op jit(solution)/shard_map/ppermute | solution.py:238
  54.8 1.2 %collective-permute-start.18 = (bf16[64,2688]{1,0:T(8,128)(2,1)S(1)}, bf16[64,2688]{1,0:T(8,128)(2,1)S(1)}, u32[]{:S(2)}, u32[]{:S(2)}) collective-permute-start(bf16[64,2688]{1,0:T(8,128)(2,1)S(1)} %get-tuple-element.47.g_ref.refs_0_), channel_id=1, source_target_pairs={{0,16},{4,20},{8,24},{12,28},{16,0},{20,4},{24,8},{28,12},{1,17},{... | collective-permute-start | bytes 1032200 | tf_op jit(solution)/shard_map/ppermute | solution.py:238
  56.8 4.3 %shard_map.88 = (f32[4,16,1280]{2,1,0:T(8,128)S(1)}, bf16[2,4,16,1280]{3,2,1,0:T(8,128)(2,1)S(1)}, f32[4,16,1280]{2,1,0:T(8,128)S(1)}) custom-call(bf16[64,2688]{1,0:T(8,128)(2,1)S(1)} %get-tuple-element.47.g_ref.refs_0_, bf16[1280,2688]{1,0:T(8,128)(2,1)S(1)} %shard_map.77.w_ref.refs_0_, bf16[1280,2688]{1,0:T(8,128)(2,1)S(1)} %shard_map.79.w_ref.refs_1_), custom_call_target="tpu_custom_call" | custom-call | flops 215040 | bytes 3360 | tf_op jit(solution)/shard_map/pallas_call | solution.py:412
  61.0 4.3 %shard_map.89 = (f32[4,16,1280]{2,1,0:T(8,128)S(1)}, bf16[2,4,16,1280]{3,2,1,0:T(8,128)(2,1)S(1)}, f32[4,16,1280]{2,1,0:T(8,128)S(1)}) custom-call(bf16[64,2688]{1,0:T(8,128)(2,1)S(1)} %get-tuple-element.47.g_ref.refs_0_, bf16[1280,2688]{1,0:T(8,128)(2,1)S(1)} %shard_map.82.w_ref.refs_0_, ...), custom_call_target="tpu_custom_call", output_to_operand_aliasing={{0}: (3, {}), {1}: (4, {}), {2}: (5, {})} | custom-call | flops 215040 | bytes 3360 | tf_op jit(solution)/shard_map/pallas_call | solution.py:412
  65.3 1.6 %collective-permute-start.15 = (bf16[2,4,16,1280]{3,2,1,0:T(8,128)(2,1)S(1)}, bf16[2,4,16,1280]{3,2,1,0:T(8,128)(2,1)S(1)}, u32[]{:S(2)}, u32[]{:S(2)}) collective-permute-start(bf16[2,4,16,1280]{3,2,1,0:T(8,128)(2,1)S(1)} %get-tuple-element.53), channel_id=1, source_target_pairs={{0,1},{1,0},{2,3},{3,2},{4,5},{5,4},{6,7},{7,6},{8,9},{9,8},{10,11... | collective-permute-start | bytes 983048 | tf_op jit(solution)/shard_map/ppermute | solution.py:242
  67.0 3.5 %collective-permute-done.18.refs_2_ = bf16[64,2688]{1,0:T(8,128)(2,1)S(1)} collective-permute-done((bf16[64,2688]{1,0:T(8,128)(2,1)S(1)}, bf16[64,2688]{1,0:T(8,128)(2,1)S(1)}, u32[]{:S(2)}, u32[]{:S(2)}) %collective-permute-start.18) | collective-permute-done | bytes 344096 | tf_op jit(solution)/shard_map/ppermute | solution.py:238
  70.5 3.7 %shard_map.91 = (f32[210,16,128]{2,1,0:T(8,128)S(1)}, bf16[210,16,128]{2,1,0:T(8,128)(2,1)S(1)}) custom-call(s32[1]{0:T(128)} %bitcast.order_ref.z_ref.core_ref, s32[1,210]{1,0:T(1,128)S(1)} %copy-done.6, s32[1,210]{1,0:T(1,128)S(1)} %copy-done.8, bf16[1280,256]{1,0:T(8,128)(2,1)S(1)} %shard_map.81.x_ref, ...), custom_call_target="tpu_custom_call" | custom-call | flops 430080 | bytes 3360 | tf_op jit(solution)/shard_map/pallas_call | solution.py:436
  74.3 2.7 %collective-permute-start.16 = (bf16[4,16,1280]{2,1,0:T(8,128)(2,1)S(1)}, bf16[4,16,1280]{2,1,0:T(8,128)(2,1)S(1)}, u32[]{:S(2)}, u32[]{:S(2)}) collective-permute-start(bf16[4,16,1280]{2,1,0:T(8,128)(2,1)S(1)} %fusion), channel_id=1, source_target_pairs={{0,2},{1,3},{2,0},{3,1},{4,6},{5,7},{6,4},{7,5},{8,10},{9,11},{10,... | collective-permute-start | bytes 491528 | tf_op jit(solution)/shard_map/ppermute | solution.py:242
  77.0 8.4 %collective-permute-done.16.refs_2_ = bf16[4,16,1280]{2,1,0:T(8,128)(2,1)S(1)} collective-permute-done((bf16[4,16,1280]{2,1,0:T(8,128)(2,1)S(1)}, bf16[4,16,1280]{2,1,0:T(8,128)(2,1)S(1)}, u32[]{:S(2)}, u32[]{:S(2)}) %collective-permute-start.16) | collective-permute-done | bytes 163872 | tf_op jit(solution)/shard_map/ppermute | solution.py:242
  85.4 1.2 %shard_map.90 = bf16[16,5120]{1,0:T(8,128)(2,1)} custom-call(s32[1]{0:T(128)} %bitcast.1.place_ref, bf16[1024,1024]{1,0:T(8,128)(2,1)S(1)} %copy-done.1, f32[4,16,1280]{2,1,0:T(8,128)S(1)} %get-tuple-element.52.refs_0_, bf16[2,4,16,1280]{3,2,1,0:T(8,128)(2,1)S(1)} %collective-permute-done.15.refs_1_, bf16[4,16,1280]{2,1,0:T(8,128)(2,1)S(1)} %collective-permute-done.16.refs_2_), custom_call_target="tpu_custom_call" | custom-call | tf_op jit(solution)/shard_map/pallas_call | solution.py:428
  86.6 1.5 %add_bitcast_fusion = f32[16,210,128]{2,0,1:T(8,128)} fusion(f32[210,16,128]{2,1,0:T(8,128)S(1)} %get-tuple-element.55, bf16[210,16,128]{2,1,0:T(8,128)(2,1)S(1)} %collective-permute-done.20), kind=kLoop, calls=%fused_computation | loop fusion | flops 860160 | bytes 4300800 | tf_op jit(solution)/shard_map/transpose | solution.py:473
  (46 shorter events, 8.0 us)
Async XLA Ops:
  0.6 18.6 %collective-permute-start = (bf16[210,16,128]{2,1,0:T(8,128)(2,1)}, bf16[210,16,128]{2,1,0:T(8,128)(2,1)S(1)}, u32[]{:S(2)}, u32[]{:S(2)}) collective-permute-start(bf16[210,16,128]{2,1,0:T(8,128)(2,1)} %bitcast.10), channel_id=1, source_target_pairs={{0,4},{4,0},{8,12},{12,8},{16,20},{20,16},{24,28},{28,24},{1,5},{5... | collective-permute-start | bytes 2580488 | tf_op jit(solution)/shard_map/ppermute | solution.py:235
  1.1 23.1 %collective-permute-start.2 = (bf16[210,16,128]{2,1,0:T(8,128)(2,1)}, bf16[210,16,128]{2,1,0:T(8,128)(2,1)S(1)}, u32[]{:S(2)}, u32[]{:S(2)}) collective-permute-start(bf16[210,16,128]{2,1,0:T(8,128)(2,1)} %bitcast.11), channel_id=1, source_target_pairs={{0,16},{4,20},{8,24},{12,28},{16,0},{20,4},{24,8},{28,12},{1,17},{... | collective-permute-start | bytes 2580488 | tf_op jit(solution)/shard_map/ppermute | solution.py:238
  3.7 21.4 %collective-permute-start.1 = (bf16[210,16,128]{2,1,0:T(8,128)(2,1)}, bf16[210,16,128]{2,1,0:T(8,128)(2,1)S(1)}, u32[]{:S(2)}, u32[]{:S(2)}) collective-permute-start(bf16[210,16,128]{2,1,0:T(8,128)(2,1)} %bitcast.12), channel_id=1, source_target_pairs={{0,8},{4,12},{8,0},{12,4},{16,24},{20,28},{24,16},{28,20},{1,9},{5... | collective-permute-start | bytes 2580488 | tf_op jit(solution)/shard_map/ppermute | solution.py:238
  5.2 0.9 %copy-start.4 = (bf16[16,5120]{1,0:T(8,128)(2,1)S(1)}, bf16[16,5120]{1,0:T(8,128)(2,1)}, u32[]{:S(2)}) copy-start(bf16[16,5120]{1,0:T(8,128)(2,1)} %tokens_ref.1) | copy-start | bytes 491524
  6.8 1.3 %copy-start = (bf16[1024,1024]{1,0:T(8,128)(2,1)}, bf16[1024,1024]{1,0:T(8,128)(2,1)S(1)}, u32[]{:S(2)}) copy-start(bf16[1024,1024]{1,0:T(8,128)(2,1)S(1)} %get-tuple-element.46.onehot_ref) | copy-start | bytes 6291460
  8.2 10.5 %collective-permute-start.4 = (bf16[8,16,640]{2,1,0:T(8,128)(2,1)S(1)}, bf16[8,16,640]{2,1,0:T(8,128)(2,1)S(1)}, u32[]{:S(2)}, u32[]{:S(2)}) collective-permute-start(bf16[8,16,640]{2,1,0:T(8,128)(2,1)S(1)} %get-tuple-element.36.refs_0_), channel_id=1, source_target_pairs={{0,2},{1,3},{2,0},{3,1},{4,6},{5,7},{6,4},{7,5},{8,10},{9,11},{10,... | collective-permute-start | bytes 491528 | tf_op jit(solution)/shard_map/ppermute | solution.py:242
  10.8 13.5 %collective-permute-start.3 = (bf16[8,16,640]{2,1,0:T(8,128)(2,1)S(1)}, bf16[8,16,640]{2,1,0:T(8,128)(2,1)S(1)}, u32[]{:S(2)}, u32[]{:S(2)}) collective-permute-start(bf16[8,16,640]{2,1,0:T(8,128)(2,1)S(1)} %get-tuple-element.36.refs_0_), channel_id=1, source_target_pairs={{0,1},{1,0},{2,3},{3,2},{4,5},{5,4},{6,7},{7,6},{8,9},{9,8},{10,11... | collective-permute-start | bytes 491528 | tf_op jit(solution)/shard_map/ppermute | solution.py:242
  18.7 5.6 %collective-permute-start.5 = (bf16[8,16,640]{2,1,0:T(8,128)(2,1)S(1)}, bf16[8,16,640]{2,1,0:T(8,128)(2,1)S(1)}, u32[]{:S(2)}, u32[]{:S(2)}) collective-permute-start(bf16[8,16,640]{2,1,0:T(8,128)(2,1)S(1)} %collective-permute-done.4.refs_2_), channel_id=1, source_target_pairs={{0,1},{1,0},{2,3},{3,2},{4,5},{5,4},{6,7},{7,6},{8,9},{9,8},{10,11... | collective-permute-start | bytes 491528 | tf_op jit(solution)/shard_map/ppermute | solution.py:242
  19.2 1.2 %copy-start.2 = (bf16[16,210,128]{2,0,1:T(8,128)(2,1)S(1)}, bf16[16,210,128]{2,0,1:T(8,128)(2,1)}, u32[]{:S(2)}) copy-start(bf16[16,210,128]{2,0,1:T(8,128)(2,1)} %param.6) | copy-start | bytes 2580484
  20.4 0.7 copy-start.5
  21.1 0.7 copy-start.7
  25.1 4.0 %collective-permute-start.6 = (bf16[210,16,128]{2,1,0:T(8,128)(2,1)S(1)}, bf16[210,16,128]{2,1,0:T(8,128)(2,1)S(1)}, u32[]{:S(2)}, u32[]{:S(2)}) collective-permute-start(bf16[210,16,128]{2,1,0:T(8,128)(2,1)S(1)} %collective-permute-done.1.first_ref.own_ref), channel_id=1, source_target_pairs={{0,4},{4,0},{8,12},{12,8},{16,20},{20,16},{24,28},{28,24},{1,5},{5... | collective-permute-start | bytes 2580488 | tf_op jit(solution)/shard_map/ppermute | solution.py:235
  25.1 7.8 %collective-permute-start.12 = (bf16[210,16,128]{2,1,0:T(8,128)(2,1)S(1)}, bf16[210,16,128]{2,1,0:T(8,128)(2,1)S(1)}, u32[]{:S(2)}, u32[]{:S(2)}) collective-permute-start(bf16[210,16,128]{2,1,0:T(8,128)(2,1)S(1)} %collective-permute-done.2.second_ref.own_ref), channel_id=1, source_target_pairs={{0,4},{4,0},{8,12},{12,8},{16,20},{20,16},{24,28},{28,24},{1,5},{5... | collective-permute-start | bytes 2580488 | tf_op jit(solution)/shard_map/ppermute | solution.py:235
  25.7 11.9 %collective-permute-start.10 = (bf16[105,16,128]{2,1,0:T(8,128)(2,1)S(1)}, bf16[105,16,128]{2,1,0:T(8,128)(2,1)S(1)}, u32[]{:S(2)}, u32[]{:S(2)}) collective-permute-start(bf16[105,16,128]{2,1,0:T(8,128)(2,1)S(1)} %get-tuple-element.33), channel_id=1, source_target_pairs={{0,16},{4,20},{8,24},{12,28},{16,0},{20,4},{24,8},{28,12},{1,17},{... | collective-permute-start | bytes 1290248 | tf_op jit(solution)/shard_map/ppermute | solution.py:238
  26.1 3.0 %copy-start.6 = (s32[1,210]{1,0:T(1,128)S(1)}, s32[1,210]{1,0:T(1,128)}, u32[]{:S(2)}) copy-start(s32[1,210]{1,0:T(1,128)} %row_ref.11) | copy-start | bytes 2524
  26.1 3.0 %copy-start.8 = (s32[1,210]{1,0:T(1,128)S(1)}, s32[1,210]{1,0:T(1,128)}, u32[]{:S(2)}) copy-start(s32[1,210]{1,0:T(1,128)} %col_ref.11) | copy-start | bytes 2524
  26.1 11.6 %collective-permute-start.11 = (bf16[105,16,128]{2,1,0:T(8,128)(2,1)S(1)}, bf16[105,16,128]{2,1,0:T(8,128)(2,1)S(1)}, u32[]{:S(2)}, u32[]{:S(2)}) collective-permute-start(bf16[105,16,128]{2,1,0:T(8,128)(2,1)S(1)} %get-tuple-element.34), channel_id=1, source_target_pairs={{0,8},{4,12},{8,0},{12,4},{16,24},{20,28},{24,16},{28,20},{1,9},{5... | collective-permute-start | bytes 1290248 | tf_op jit(solution)/shard_map/ppermute | solution.py:238
  37.7 11.8 %collective-permute-start.13 = (bf16[105,16,128]{2,1,0:T(8,128)(2,1)S(1)}, bf16[105,16,128]{2,1,0:T(8,128)(2,1)S(1)}, u32[]{:S(2)}, u32[]{:S(2)}) collective-permute-start(bf16[105,16,128]{2,1,0:T(8,128)(2,1)S(1)} %collective-permute-done.10.lower_ref), channel_id=1, source_target_pairs={{0,4},{4,0},{8,12},{12,8},{16,20},{20,16},{24,28},{28,24},{1,5},{5... | collective-permute-start | bytes 1290248 | tf_op jit(solution)/shard_map/ppermute | solution.py:235
  37.7 11.8 %collective-permute-start.14 = (bf16[105,16,128]{2,1,0:T(8,128)(2,1)S(1)}, bf16[105,16,128]{2,1,0:T(8,128)(2,1)S(1)}, u32[]{:S(2)}, u32[]{:S(2)}) collective-permute-start(bf16[105,16,128]{2,1,0:T(8,128)(2,1)S(1)} %collective-permute-done.11.upper_ref), channel_id=1, source_target_pairs={{0,4},{4,0},{8,12},{12,8},{16,20},{20,16},{24,28},{28,24},{1,5},{5... | collective-permute-start | bytes 1290248 | tf_op jit(solution)/shard_map/ppermute | solution.py:235
  38.3 7.1 %collective-permute-start.7 = (bf16[64,1280]{1,0:T(8,128)(2,1)S(1)}, bf16[64,1280]{1,0:T(8,128)(2,1)S(1)}, u32[]{:S(2)}, u32[]{:S(2)}) collective-permute-start(bf16[64,1280]{1,0:T(8,128)(2,1)S(1)} %get-tuple-element.38), channel_id=1, source_target_pairs={{0,8},{4,12},{8,0},{12,4},{16,24},{20,28},{24,16},{28,20},{1,9},{5... | collective-permute-start | bytes 491528 | tf_op jit(solution)/shard_map/ppermute | solution.py:238
  39.9 9.3 %collective-permute-start.8 = (bf16[64,1280]{1,0:T(8,128)(2,1)S(1)}, bf16[64,1280]{1,0:T(8,128)(2,1)S(1)}, u32[]{:S(2)}, u32[]{:S(2)}) collective-permute-start(bf16[64,1280]{1,0:T(8,128)(2,1)S(1)} %get-tuple-element.39), channel_id=1, source_target_pairs={{0,16},{4,20},{8,24},{12,28},{16,0},{20,4},{24,8},{28,12},{1,17},{... | collective-permute-start | bytes 491528 | tf_op jit(solution)/shard_map/ppermute | solution.py:238
  41.5 8.1 %copy-start.3 = (bf16[64,2688]{1,0:T(8,128)(2,1)S(1)}, bf16[64,2688]{1,0:T(8,128)(2,1)}, u32[]{:S(2)}) copy-start(bf16[64,2688]{1,0:T(8,128)(2,1)} %cotangent_ref.1) | copy-start | bytes 1032196
  41.5 7.8 %collective-permute-start.9 = (bf16[64,1280]{1,0:T(8,128)(2,1)S(1)}, bf16[64,1280]{1,0:T(8,128)(2,1)S(1)}, u32[]{:S(2)}, u32[]{:S(2)}) collective-permute-start(bf16[64,1280]{1,0:T(8,128)(2,1)S(1)} %get-tuple-element.40), channel_id=1, source_target_pairs={{0,24},{4,28},{8,16},{12,20},{16,8},{20,12},{24,0},{28,4},{1,25},{... | collective-permute-start | bytes 491528 | tf_op jit(solution)/shard_map/ppermute | solution.py:238
  53.3 13.7 %collective-permute-start.19 = (bf16[64,2688]{1,0:T(8,128)(2,1)S(1)}, bf16[64,2688]{1,0:T(8,128)(2,1)S(1)}, u32[]{:S(2)}, u32[]{:S(2)}) collective-permute-start(bf16[64,2688]{1,0:T(8,128)(2,1)S(1)} %get-tuple-element.47.g_ref.refs_0_), channel_id=1, source_target_pairs={{0,24},{4,28},{8,16},{12,20},{16,8},{20,12},{24,0},{28,4},{1,25},{... | collective-permute-start | bytes 1032200 | tf_op jit(solution)/shard_map/ppermute | solution.py:238
  54.8 15.7 %collective-permute-start.18 = (bf16[64,2688]{1,0:T(8,128)(2,1)S(1)}, bf16[64,2688]{1,0:T(8,128)(2,1)S(1)}, u32[]{:S(2)}, u32[]{:S(2)}) collective-permute-start(bf16[64,2688]{1,0:T(8,128)(2,1)S(1)} %get-tuple-element.47.g_ref.refs_0_), channel_id=1, source_target_pairs={{0,16},{4,20},{8,24},{12,28},{16,0},{20,4},{24,8},{28,12},{1,17},{... | collective-permute-start | bytes 1032200 | tf_op jit(solution)/shard_map/ppermute | solution.py:238
  56.0 14.5 %collective-permute-start.17 = (bf16[64,2688]{1,0:T(8,128)(2,1)S(1)}, bf16[64,2688]{1,0:T(8,128)(2,1)S(1)}, u32[]{:S(2)}, u32[]{:S(2)}) collective-permute-start(bf16[64,2688]{1,0:T(8,128)(2,1)S(1)} %get-tuple-element.47.g_ref.refs_0_), channel_id=1, source_target_pairs={{0,8},{4,12},{8,0},{12,4},{16,24},{20,28},{24,16},{28,20},{1,9},{5... | collective-permute-start | bytes 1032200 | tf_op jit(solution)/shard_map/ppermute | solution.py:238
  65.3 20.1 %copy-start.1 = (bf16[1024,1024]{1,0:T(8,128)(2,1)S(1)}, bf16[1024,1024]{1,0:T(8,128)(2,1)}, u32[]{:S(2)}) copy-start(bf16[1024,1024]{1,0:T(8,128)(2,1)} %copy-done) | copy-start | bytes 6291460
  65.3 9.0 %collective-permute-start.15 = (bf16[2,4,16,1280]{3,2,1,0:T(8,128)(2,1)S(1)}, bf16[2,4,16,1280]{3,2,1,0:T(8,128)(2,1)S(1)}, u32[]{:S(2)}, u32[]{:S(2)}) collective-permute-start(bf16[2,4,16,1280]{3,2,1,0:T(8,128)(2,1)S(1)} %get-tuple-element.53), channel_id=1, source_target_pairs={{0,1},{1,0},{2,3},{3,2},{4,5},{5,4},{6,7},{7,6},{8,9},{9,8},{10,11... | collective-permute-start | bytes 983048 | tf_op jit(solution)/shard_map/ppermute | solution.py:242
  74.2 12.4 %collective-permute-start.20 = (bf16[210,16,128]{2,1,0:T(8,128)(2,1)S(1)}, bf16[210,16,128]{2,1,0:T(8,128)(2,1)S(1)}, u32[]{:S(2)}, u32[]{:S(2)}) collective-permute-start(bf16[210,16,128]{2,1,0:T(8,128)(2,1)S(1)} %get-tuple-element.56), channel_id=1, source_target_pairs={{0,4},{4,0},{8,12},{12,8},{16,20},{20,16},{24,28},{28,24},{1,5},{5... | collective-permute-start | bytes 2580488 | tf_op jit(solution)/shard_map/ppermute | solution.py:235
  74.3 11.1 %collective-permute-start.16 = (bf16[4,16,1280]{2,1,0:T(8,128)(2,1)S(1)}, bf16[4,16,1280]{2,1,0:T(8,128)(2,1)S(1)}, u32[]{:S(2)}, u32[]{:S(2)}) collective-permute-start(bf16[4,16,1280]{2,1,0:T(8,128)(2,1)S(1)} %fusion), channel_id=1, source_target_pairs={{0,2},{1,3},{2,0},{3,1},{4,6},{5,7},{6,4},{7,5},{8,10},{9,11},{10,... | collective-permute-start | bytes 491528 | tf_op jit(solution)/shard_map/ppermute | solution.py:242

commit v3 on v2

--- a/solution.py
+++ b/solution.py
@@ -59,33 +59,32 @@
             ]
 
 
-def join_kernel(parts, tile_width, groups_of, place_ref, onehot_ref, *refs):
+def join_kernel(parts, tile_width, place_ref, onehot_ref, *refs):
     *part_refs, out_ref, held = refs
     size = parts * tile_width
     rows = out_ref.shape[0]
     me = place_ref[0]
     groups = out_ref.shape[1] // size
-    first = 0
-    for index, count in enumerate(groups_of):
-        for step in range(count):
-            own_ref, near_ref, far_ref = part_refs[3 * index : 3 * index + 3]
-            total = own_ref[step] + near_ref[0, step].astype(F32) + far_ref[step].astype(F32)
-            total = total.astype(BF16)
-            for half in range(2):
-                for group in range(groups):
-                    at = (half * groups + group) * tile_width
-                    held[me ^ (2 * (first + step) + half), group * rows : (group + 1) * rows] = (
-                        total[:, at : at + tile_width]
-                    )
-        first += count
+    for step in range(parts // 2):
+        total = part_refs[0][step]
+        for part_ref in part_refs[1:]:
+            total = total + part_ref[step].astype(F32)
+        total = total.astype(BF16)
+        for half in range(2):
+            for group in range(groups):
+                at = (half * groups + group) * tile_width
+                held[me ^ (2 * step + half), group * rows : (group + 1) * rows] = total[
+                    :, at : at + tile_width
+                ]
     lanes = jnp.concatenate([held[part] for part in range(parts)], axis=1)
     result = jnp.dot(lanes, onehot_ref[...], preferred_element_type=F32).astype(BF16)
     for group in range(groups):
         out_ref[:, group * size : (group + 1) * size] = result[group * rows : (group + 1) * rows]
 
 
-def place_tiles(half, row_ref, col_ref, tiles_ref, out_ref, first=0):
+def place_tiles(half, row_ref, col_ref, tiles_ref, out_ref, first=0, count=None):
     slots, rows, width = tiles_ref.shape
+    slots = slots if count is None else count
     start = half * (out_ref.shape[0] // 2)
 
     def place(slot, carry):
@@ -110,27 +109,16 @@
     sum_ref[...] = product + early_refs[0][...] if early_refs else product
 
 
-def halves_kernel(first_ref, second_ref, lower_ref, upper_ref):
+def relay_kernel(first_ref, second_ref, lower_ref, upper_ref):
     lower_ref[...] = first_ref[: lower_ref.shape[0]]
     upper_ref[...] = second_ref[lower_ref.shape[0] :]
 
 
-def half_weight_kernel(order_ref, row_ref, col_ref, lower_ref, upper_ref, out_ref):
+def half_weight_kernel(half, order_ref, row_ref, col_ref, lower_ref, upper_ref, out_ref):
+    slots = row_ref.shape[1]
     out_ref[...] = jnp.zeros_like(out_ref)
-    place_tiles(0, row_ref, col_ref, lower_ref, out_ref)
-    place_tiles(0, row_ref, col_ref, upper_ref, out_ref, lower_ref.shape[0])
-
-
-def gather_kernel(chips, n_tp, *refs):
-    x_refs = refs[:n_tp]
-    out_refs = refs[n_tp:]
-    for step in range(chips):
-        out_refs[step][...] = slice_rows(x_refs, step)
-
-
-def transpose_kernel(order_ref, *refs):
-    *part_refs, out_ref = refs
-    out_ref[...] = jnp.concatenate([part_ref[...] for part_ref in part_refs], axis=0).T
+    place_tiles(0, row_ref, col_ref, lower_ref, out_ref, 0, half)
+    place_tiles(0, row_ref, col_ref, upper_ref, out_ref, half, slots - half)
 
 
 def slice_rows(x_refs, step):
@@ -140,12 +128,12 @@
     )
 
 
-def hidden_kernel(n_tp, step, order_ref, z_ref, row_ref, col_ref, lower_ref, upper_ref, early_ref, cotangent_ref, half_ref, *refs):
+def hidden_kernel(n_tp, step, half, order_ref, z_ref, row_ref, col_ref, lower_ref, upper_ref, early_ref, cotangent_ref, half_ref, *refs):
     x_refs = refs[:n_tp]
-    w_ref, act_ref, grad_ref = refs[n_tp:]
+    w_ref, act_ref, grad_ref, *pack_refs = refs[n_tp:]
     rows = x_refs[0].shape[1]
-    place_tiles(1, row_ref, col_ref, lower_ref, w_ref)
-    place_tiles(1, row_ref, col_ref, upper_ref, w_ref, lower_ref.shape[0])
+    place_tiles(1, row_ref, col_ref, lower_ref, w_ref, 0, half)
+    place_tiles(1, row_ref, col_ref, upper_ref, w_ref, half, row_ref.shape[1] - half)
     lhs = slice_rows(x_refs, step)
     for left, right in column_blocks(w_ref.shape[1]):
         hidden = early_ref[:, left:right] + jnp.dot(
@@ -157,9 +145,11 @@
             at = pl.ds(pl.multiple_of((z_ref[0] ^ j) * rows, rows), rows)
             act_ref[at, left:right] = act_value[j * rows : (j + 1) * rows]
             slope = act_slope[j * rows : (j + 1) * rows]
-            grad_ref[j * rows : (j + 1) * rows, left:right] = (
-                cotangent_ref[at, left:right].astype(F32) * slope
-            ).astype(BF16)
+            grad = (cotangent_ref[at, left:right].astype(F32) * slope).astype(BF16)
+            for out_ref in (grad_ref, *pack_refs):
+                out_ref[j * rows : (j + 1) * rows, left:right] = grad
+    for chip, pack_ref in enumerate(pack_refs):
+        pack_ref[:, w_ref.shape[1] :] = slice_rows(x_refs, chip)
 
 
 def column_blocks(columns, block=512):
@@ -168,26 +158,26 @@
 
 def back_kernel(n_tp, first, count, g_ref, *refs):
     w_refs = refs[:count]
-    own_ref, near_ref, far_ref = refs[-3:]
+    out_refs = refs[-n_tp:]
     rows = g_ref.shape[0] // n_tp
     for step in range(count):
         result = lax.dot_general(
-            g_ref[...], w_refs[step][...], (((1,), (1,)), ((), ())), preferred_element_type=F32
-        )
-        own_ref[first + step] = result[:rows]
-        near_ref[0, first + step] = result[rows : 2 * rows].astype(BF16)
-        near_ref[1, first + step] = result[3 * rows :].astype(BF16)
-        far_ref[first + step] = result[2 * rows : 3 * rows]
-
-
-def tile_grad_kernel(chips, scale, core_ref, row_ref, col_ref, x_ref, *refs):
-    g_refs = refs[:chips]
+            w_refs[step][...], g_ref[...], (((1,), (1,)), ((), ())), preferred_element_type=F32
+        ).T
+        for j in range(n_tp):
+            out_refs[j][first + step] = result[j * rows : (j + 1) * rows].astype(out_refs[j].dtype)
+
+
+def tile_grad_kernel(chips, scale, order_ref, row_ref, col_ref, *refs):
+    pack_refs = refs[:chips]
     mine_ref, theirs_ref, dense = refs[chips:]
     slots, tile_rows, width = mine_ref.shape
+    columns = dense.shape[1]
     half = dense.shape[0] // 2
-    for left, right in column_blocks(dense.shape[1]):
-        g_all = jnp.concatenate([g_ref[:, left:right] for g_ref in g_refs], axis=0)
-        dense[:, left:right] = jnp.dot(x_ref[...], g_all, preferred_element_type=F32)
+    x_t = jnp.concatenate([pack_ref[:, columns:] for pack_ref in pack_refs], axis=0).T
+    for left, right in column_blocks(columns):
+        g_all = jnp.concatenate([pack_ref[:, left:right] for pack_ref in pack_refs], axis=0)
+        dense[:, left:right] = jnp.dot(x_t, g_all, preferred_element_type=F32)
 
     def place_tile(slot, carry):
         top = pl.multiple_of(row_ref[0, slot] * tile_rows, tile_rows)
@@ -302,7 +292,7 @@
         )
         half = slots // 2
         relay = pl.pallas_call(
-            halves_kernel,
+            relay_kernel,
             out_shape=[
                 jax.ShapeDtypeStruct((half, tile_rows, tile_width), BF16),
                 jax.ShapeDtypeStruct((slots - half, tile_rows, tile_width), BF16),
@@ -315,13 +305,6 @@
         others += [to_core(part) for part in tiles[1:]]
         for step in range(1, chips - 1):
             weights.append(make_weight(step, after(z_index, weights[-1], *relay)))
-        mine = pl.pallas_call(
-            functools.partial(gather_kernel, chips, n_tp),
-            out_shape=[jax.ShapeDtypeStruct((block, depth), BF16)] * chips,
-            in_specs=[spec()] * n_tp,
-            out_specs=[spec()] * chips,
-            compiler_params=params(8),
-        )(after(token_parts[0], weights[1]), *token_parts[1:])
         early = add_hidden(0)
         for step in range(1, chips - 1):
             early = add_hidden(step, early)
@@ -340,38 +323,28 @@
 
     if fast:
         half_weight = pl.pallas_call(
-            half_weight_kernel,
+            functools.partial(half_weight_kernel, half),
             out_shape=jax.ShapeDtypeStruct((depth, columns), BF16),
             in_specs=[spec(SMEM)] * 3 + [spec()] * 2,
             out_specs=spec(),
             compiler_params=params(10),
             cost_estimate=cost(0, 2 * 2 * depth * columns),
         )(z_index, tile_row, tile_col, *relayed)
-        slices = pl.pallas_call(
-            transpose_kernel,
-            out_shape=jax.ShapeDtypeStruct((depth, chips * block), BF16),
-            in_specs=[spec(SMEM)] + [spec()] * chips,
-            out_specs=spec(),
-            compiler_params=params(8),
-        )(
-            z_index,
-            mine[0],
-            *[to_chip(mine[step], step) for step in range(1, chips)],
-        )
-        last_weight, act, hidden_grad = pl.pallas_call(
-            functools.partial(hidden_kernel, n_tp, chips - 1),
+        last_weight, act, hidden_grad, *packs = pl.pallas_call(
+            functools.partial(hidden_kernel, n_tp, chips - 1, half),
             out_shape=[
                 jax.ShapeDtypeStruct((depth, columns), BF16),
                 jax.ShapeDtypeStruct((block, columns), BF16),
                 jax.ShapeDtypeStruct((block, columns), BF16),
-            ],
+            ]
+            + [jax.ShapeDtypeStruct((block, columns + depth), BF16)] * chips,
             in_specs=[spec(SMEM)] * 4 + [spec()] * (5 + n_tp),
-            out_specs=[spec()] * 3,
+            out_specs=[spec()] * (3 + chips),
             input_output_aliases={8: 0},
-            compiler_params=params(20),
+            compiler_params=params(24),
             cost_estimate=cost(2 * block * depth * columns, 2 * depth * columns),
         )(
-            after(z_index, slices), z_index, tile_row, tile_col, *last_others, early, grad_act, half_weight,
+            z_index, z_index, tile_row, tile_col, *last_others, early, grad_act, half_weight,
             *token_parts,
         )
         weights.append(last_weight)
@@ -403,50 +376,47 @@
         for j in range(n_tp):
             act = lax.dynamic_update_slice_in_dim(act, act_value[j], z_rows(j), axis=0)
 
-    grads = [hidden_grad] + [to_chip(hidden_grad, step) for step in range(1, chips)]
 
     if fast:
-        group_sizes = (chips,)
+        packs = [packs[0]] + [to_chip(packs[step], step) for step in range(1, chips)]
         backs = []
         for first in range(0, chips, 2):
             backs = pl.pallas_call(
                 functools.partial(back_kernel, n_tp, first, 2),
                 out_shape=[
-                    jax.ShapeDtypeStruct((chips, rows, depth), F32),
-                    jax.ShapeDtypeStruct((2, chips, rows, depth), BF16),
-                    jax.ShapeDtypeStruct((chips, rows, depth), F32),
+                    jax.ShapeDtypeStruct((chips, rows, depth), F32 if j == 0 else BF16)
+                    for j in range(n_tp)
                 ],
                 in_specs=[spec()] * (3 + len(backs)),
-                out_specs=[spec()] * 3,
-                input_output_aliases={3: 0, 4: 1, 5: 2} if backs else {},
+                out_specs=[spec()] * n_tp,
+                input_output_aliases={3 + j: j for j in range(n_tp)} if backs else {},
                 compiler_params=params(18),
                 cost_estimate=cost(4 * block * depth * columns, 4 * depth * columns),
             )(hidden_grad, *weights[first : first + 2], *backs)
-        near = to_z(backs[1], 1)
-        far = to_z((backs[2] + near[1].astype(F32)).astype(BF16), 2)
-        returned = [[backs[0], near, far]]
-        grad_tokens = pl.pallas_call(
-            functools.partial(join_kernel, fsdp, tile_width, group_sizes),
-            out_shape=jax.ShapeDtypeStruct((rows, width), BF16),
-            in_specs=[spec(SMEM)] + [spec()] * (1 + 3 * len(group_sizes)),
-            out_specs=spec(),
-            scratch_shapes=[pltpu.VMEM((fsdp, rows * row_tiles // fsdp, tile_width), BF16)],
-            compiler_params=params(8),
-        )(place_index, onehot, *[part for group in returned for part in group])
+        returned = [backs[0]] + [to_z(backs[j], j) for j in range(1, n_tp)]
         mine, theirs = pl.pallas_call(
             functools.partial(tile_grad_kernel, chips, grad_scale),
             out_shape=[
                 jax.ShapeDtypeStruct((slots, tile_rows, tile_width), F32),
                 jax.ShapeDtypeStruct((slots, tile_rows, tile_width), BF16),
             ],
-            in_specs=[spec(SMEM)] * 3 + [spec()] * (1 + chips),
+            in_specs=[spec(SMEM)] * 3 + [spec()] * chips,
             out_specs=[spec()] * 2,
             scratch_shapes=[pltpu.VMEM((depth, columns), F32)],
-            compiler_params=params(26),
+            compiler_params=params(28),
             cost_estimate=cost(2 * chips * block * depth * columns, 4 * depth * columns),
-        )(z_index, tile_row, tile_col, slices, *grads)
+        )(after(z_index, *returned[1:]), tile_row, tile_col, *packs)
         grad_tiles = mine + to_core(theirs).astype(F32)
+        grad_tokens = pl.pallas_call(
+            functools.partial(join_kernel, fsdp, tile_width),
+            out_shape=jax.ShapeDtypeStruct((rows, width), BF16),
+            in_specs=[spec(SMEM)] + [spec()] * (1 + n_tp),
+            out_specs=spec(),
+            scratch_shapes=[pltpu.VMEM((fsdp, rows * row_tiles // fsdp, tile_width), BF16)],
+            compiler_params=params(8),
+        )(place_index, onehot, *returned)
     else:
+        grads = [hidden_grad] + [to_chip(hidden_grad, step) for step in range(1, chips)]
         backs = jnp.einsum(
             "jrc,qkc->jqrk",
             hidden_grad.reshape(n_tp, rows, columns),

time: 88.3 us -> 79.1 us (0.90)
  waiting for transfers between devices: 25.8 us -> 17.4 us
  Pallas kernels: 31.3 us -> 30.3 us
    ppermute x10 -> x7, waiting for transfers between devices: 11 us -> 1.75 us  [to_chip(): return lax.ppermute(value, 'fsdp', [(f, f ^ 2 * step) for f in range(fsdp)])]
    ppermute x10 -> x7, starting transfers between devices: 13.2 us -> 9.64 us  [to_chip(): return lax.ppermute(value, 'fsdp', [(f, f ^ 2 * step) for f in range(fsdp)])]
    ppermute x5 -> x6, starting transfers between devices: 9.06 us -> 12.2 us  [to_z(): return lax.ppermute(value, 'tp', [(i, i ^ step) for i in range(n_tp)])]
    ppermute x6, waiting for transfers between devices: 0.02 us -> 1.26 us  [to_core(): return lax.ppermute(value, 'fsdp', [(f, f ^ 1) for f in range(fsdp)])]
    ppermute x5 -> x6, waiting for transfers between devices: 14.7 us -> 14.4 us  [to_z(): return lax.ppermute(value, 'tp', [(i, i ^ step) for i in range(n_tp)])]
    pallas_call x6 -> x4, Pallas kernels: 7.01 us -> 6.79 us  [the longest x1 3.76 us: local(): pl.pallas_call(functools.partial(hidden_kernel, n_tp, chips - 1, half), o...]
  transfers between devices with their start and end apart: 21 -> 19, of which waited for: 8 -> 8; matrix products, arithmetic and copies ran while one was open for 0% -> 0% of each run, Pallas kernels for 31% -> 29%
where the time goes in v3:
time: 79.1 us; the launch traced here: 78.2 us
  Pallas kernels  30.3 us (38%)
  starting transfers between devices  23.5 us (30%)
  waiting for transfers between devices  17.4 us (22%)
  local copies, waits for them, and re-layouts  4.8 us (6%)
  other arithmetic  1.36 us (2%)
  between operations  0.85 us (1%)
    ppermute x6, waiting for transfers between devices, to_z(): return lax.ppermute(value, 'tp', [(i, i ^ step) for i in range(n_tp)])  14.4 us
    ppermute x6, starting transfers between devices, to_z(): return lax.ppermute(value, 'tp', [(i, i ^ step) for i in range(n_tp)])  12.2 us
    ppermute x7, starting transfers between devices, to_chip(): return lax.ppermute(value, 'fsdp', [(f, f ^ 2 * step) for f in range(fsdp)])  9.64 us
    pallas_call x2, Pallas kernels, local(): pl.pallas_call(functools.partial(back_kernel, n_tp, first, 2), out_shape=...  7.69 us
    pallas_call x3, Pallas kernels, make_weight(): pl.pallas_call(weight_kernel, out_shape=jax.ShapeDtypeStruct((depth, colu...  7.44 us
    unnamed x18, local copies, waits for them, and re-layouts  4.8 us
    pallas_call x3, Pallas kernels, add_hidden(): pl.pallas_call(functools.partial(early_kernel, n_tp, step), out_shape=jax...  3.96 us
    pallas_call x1, Pallas kernels, local(): pl.pallas_call(functools.partial(hidden_kernel, n_tp, chips - 1, half), o...  3.76 us
  transfers between devices with their start and end apart: 19, of which 8 were waited for; matrix products, arithmetic and copies ran while one was open for 0% of the time, Pallas kernels for 29%

profile of v3, /device:TPU:0, one launch (start us, length us, event | category | flops | bytes accessed | tf_op | source)
XLA Modules:
  0.0 78.2 jit_solution(16716336821144873091)
XLA Ops:
  1.1 2.6 %collective-permute-start.1 = (bf16[210,16,128]{2,1,0:T(8,128)(2,1)}, bf16[210,16,128]{2,1,0:T(8,128)(2,1)S(1)}, u32[]{:S(2)}, u32[]{:S(2)}) collective-permute-start(bf16[210,16,128]{2,1,0:T(8,128)(2,1)} %bitcast.6), channel_id=1, source_target_pairs={{0,16},{4,20},{8,24},{12,28},{16,0},{20,4},{24,8},{28,12},{1,17},{... | collective-permute-start | bytes 2580488 | tf_op jit(solution)/shard_map/ppermute | solution.py:228
  3.7 1.5 %collective-permute-start = (bf16[210,16,128]{2,1,0:T(8,128)(2,1)}, bf16[210,16,128]{2,1,0:T(8,128)(2,1)S(1)}, u32[]{:S(2)}, u32[]{:S(2)}) collective-permute-start(bf16[210,16,128]{2,1,0:T(8,128)(2,1)} %bitcast.7), channel_id=1, source_target_pairs={{0,8},{4,12},{8,0},{12,4},{16,24},{20,28},{24,16},{28,20},{1,9},{5... | collective-permute-start | bytes 2580488 | tf_op jit(solution)/shard_map/ppermute | solution.py:228
  5.2 0.9 %copy-done.4 = bf16[16,5120]{1,0:T(8,128)(2,1)S(1)} copy-done((bf16[16,5120]{1,0:T(8,128)(2,1)S(1)}, bf16[16,5120]{1,0:T(8,128)(2,1)}, u32[]{:S(2)}) %copy-start.4) | copy-done | bytes 163864
  6.8 1.3 %copy-done = bf16[1024,1024]{1,0:T(8,128)(2,1)} copy-done((bf16[1024,1024]{1,0:T(8,128)(2,1)}, bf16[1024,1024]{1,0:T(8,128)(2,1)S(1)}, u32[]{:S(2)}) %copy-start) | copy-done | bytes 2097176
  8.2 2.6 %collective-permute-start.3 = (bf16[8,16,640]{2,1,0:T(8,128)(2,1)S(1)}, bf16[8,16,640]{2,1,0:T(8,128)(2,1)S(1)}, u32[]{:S(2)}, u32[]{:S(2)}) collective-permute-start(bf16[8,16,640]{2,1,0:T(8,128)(2,1)S(1)} %get-tuple-element.31.refs_0_), channel_id=1, source_target_pairs={{0,2},{1,3},{2,0},{3,1},{4,6},{5,7},{6,4},{7,5},{8,10},{9,11},{10,... | collective-permute-start | bytes 491528 | tf_op jit(solution)/shard_map/ppermute | solution.py:232
  10.8 1.6 %collective-permute-start.2 = (bf16[8,16,640]{2,1,0:T(8,128)(2,1)S(1)}, bf16[8,16,640]{2,1,0:T(8,128)(2,1)S(1)}, u32[]{:S(2)}, u32[]{:S(2)}) collective-permute-start(bf16[8,16,640]{2,1,0:T(8,128)(2,1)S(1)} %get-tuple-element.31.refs_0_), channel_id=1, source_target_pairs={{0,1},{1,0},{2,3},{3,2},{4,5},{5,4},{6,7},{7,6},{8,9},{9,8},{10,11... | collective-permute-start | bytes 491528 | tf_op jit(solution)/shard_map/ppermute | solution.py:232
  12.4 6.3 %collective-permute-done.3.refs_2_ = bf16[8,16,640]{2,1,0:T(8,128)(2,1)S(1)} collective-permute-done((bf16[8,16,640]{2,1,0:T(8,128)(2,1)S(1)}, bf16[8,16,640]{2,1,0:T(8,128)(2,1)S(1)}, u32[]{:S(2)}, u32[]{:S(2)}) %collective-permute-start.3) | collective-permute-done | bytes 163872 | tf_op jit(solution)/shard_map/ppermute | solution.py:232
  19.3 1.2 %copy-done.2 = bf16[16,210,128]{2,0,1:T(8,128)(2,1)S(1)} copy-done((bf16[16,210,128]{2,0,1:T(8,128)(2,1)S(1)}, bf16[16,210,128]{2,0,1:T(8,128)(2,1)}, u32[]{:S(2)}) %copy-start.2) | copy-done | bytes 860184
  21.8 2.5 %shard_map.77.w_ref.refs_0_ = bf16[1280,2688]{1,0:T(8,128)(2,1)S(1)} custom-call(s32[1]{0:T(128)} %bitcast.order_ref.z_ref, s32[1,210]{1,0:T(1,128)S(1)} %copy-done.5, s32[1,210]{1,0:T(1,128)S(1)} %copy-done.7, bf16[210,16,128]{2,1,0:T(8,128)(2,1)S(1)} %bitcast.8, bf16[210,16,128]{2,1,0:T(8,128)(2,1)S(1)} %collective-permute-done.5.other_ref), custom_call_target="tpu_custom_call" | custom-call | bytes 3360 | tf_op jit(solution)/shard_map/pallas_call | solution.py:257
  24.3 0.8 %collective-permute-done.first_ref.own_ref = bf16[210,16,128]{2,1,0:T(8,128)(2,1)S(1)} collective-permute-done((bf16[210,16,128]{2,1,0:T(8,128)(2,1)}, bf16[210,16,128]{2,1,0:T(8,128)(2,1)S(1)}, u32[]{:S(2)}, u32[]{:S(2)}) %collective-permute-start) | collective-permute-done | bytes 860192 | tf_op jit(solution)/shard_map/ppermute | solution.py:228
  26.1 1.7 %collective-permute-start.7 = (bf16[105,16,128]{2,1,0:T(8,128)(2,1)S(1)}, bf16[105,16,128]{2,1,0:T(8,128)(2,1)S(1)}, u32[]{:S(2)}, u32[]{:S(2)}) collective-permute-start(bf16[105,16,128]{2,1,0:T(8,128)(2,1)S(1)} %get-tuple-element.35), channel_id=1, source_target_pairs={{0,8},{4,12},{8,0},{12,4},{16,24},{20,28},{24,16},{28,20},{1,9},{5... | collective-permute-start | bytes 1290248 | tf_op jit(solution)/shard_map/ppermute | solution.py:228
  27.8 1.3 %shard_map.81.refs_4_ = f32[64,2688]{1,0:T(8,128)S(1)} custom-call(bf16[1280,2688]{1,0:T(8,128)(2,1)S(1)} %shard_map.77.w_ref.refs_0_, bf16[8,16,640]{2,1,0:T(8,128)(2,1)S(1)} %get-tuple-element.31.refs_0_, bf16[8,16,640]{2,1,0:T(8,128)(2,1)S(1)} %collective-permute-done.2.refs_1_, bf16[8,16,640]{2,1,0:T(8,128)(2,1)S(1)} %collective-permute-done.3.refs_2_, ...), custom_call_target="tpu_custom_call" | custom-call | flops 107520 | bytes 1680 | tf_op jit(solution)/shard_map/pallas_call | solution.py:267
  29.1 2.5 %shard_map.79.w_ref.refs_1_ = bf16[1280,2688]{1,0:T(8,128)(2,1)S(1)} custom-call(s32[1]{0:T(128)} %bitcast.order_ref.z_ref, s32[1,210]{1,0:T(1,128)S(1)} %copy-done.6, s32[1,210]{1,0:T(1,128)S(1)} %copy-done.8, bf16[210,16,128]{2,1,0:T(8,128)(2,1)S(1)} %collective-permute-done.first_ref.own_ref, bf16[210,16,128]{2,1,0:T(8,128)(2,1)S(1)} %collective-permute-done.8.other_ref), custom_call_target="tpu_custom_call" | custom-call | bytes 3360 | tf_op jit(solution)/shard_map/pallas_call | solution.py:257
  31.6 1.3 %shard_map.82.refs_4_ = f32[64,2688]{1,0:T(8,128)S(1)} custom-call(bf16[1280,2688]{1,0:T(8,128)(2,1)S(1)} %shard_map.79.w_ref.refs_1_, bf16[8,16,640]{2,1,0:T(8,128)(2,1)S(1)} %get-tuple-element.31.refs_0_, bf16[8,16,640]{2,1,0:T(8,128)(2,1)S(1)} %collective-permute-done.2.refs_1_, bf16[8,16,640]{2,1,0:T(8,128)(2,1)S(1)} %collective-permute-done.3.refs_2_, ...), custom_call_target="tpu_custom_call" | custom-call | flops 107520 | bytes 1680 | tf_op jit(solution)/shard_map/pallas_call | solution.py:267
  33.0 2.5 %shard_map.80.w_ref.refs_0_ = bf16[1280,2688]{1,0:T(8,128)(2,1)S(1)} custom-call(s32[1]{0:T(128)} %bitcast.order_ref.z_ref, s32[1,210]{1,0:T(1,128)S(1)} %copy-done.6, s32[1,210]{1,0:T(1,128)S(1)} %copy-done.8, bf16[210,16,128]{2,1,0:T(8,128)(2,1)S(1)} %collective-permute-done.1.second_ref.own_ref, bf16[210,16,128]{2,1,0:T(8,128)(2,1)S(1)} %collective-permute-done.9.other_ref), custom_call_target="tpu_custom_call" | custom-call | bytes 3360 | tf_op jit(solution)/shard_map/pallas_call | solution.py:257
  35.5 1.3 %shard_map.83.early_ref = f32[64,2688]{1,0:T(8,128)S(1)} custom-call(bf16[1280,2688]{1,0:T(8,128)(2,1)S(1)} %shard_map.80.w_ref.refs_0_, bf16[8,16,640]{2,1,0:T(8,128)(2,1)S(1)} %get-tuple-element.31.refs_0_, bf16[8,16,640]{2,1,0:T(8,128)(2,1)S(1)} %collective-permute-done.2.refs_1_, bf16[8,16,640]{2,1,0:T(8,128)(2,1)S(1)} %collective-permute-done.3.refs_2_, ...), custom_call_target="tpu_custom_call" | custom-call | flops 107520 | bytes 1680 | tf_op jit(solution)/shard_map/pallas_call | solution.py:267
  36.8 0.8 %collective-permute-done.6.lower_ref = bf16[105,16,128]{2,1,0:T(8,128)(2,1)S(1)} collective-permute-done((bf16[105,16,128]{2,1,0:T(8,128)(2,1)S(1)}, bf16[105,16,128]{2,1,0:T(8,128)(2,1)S(1)}, u32[]{:S(2)}, u32[]{:S(2)}) %collective-permute-start.6) | collective-permute-done | bytes 430112 | tf_op jit(solution)/shard_map/ppermute | solution.py:228
  38.2 1.7 %shard_map.84.half_ref = bf16[1280,2688]{1,0:T(8,128)(2,1)S(1)} custom-call(s32[1]{0:T(128)} %bitcast.order_ref.z_ref, s32[1,210]{1,0:T(1,128)S(1)} %copy-done.6, s32[1,210]{1,0:T(1,128)S(1)} %copy-done.8, bf16[105,16,128]{2,1,0:T(8,128)(2,1)S(1)} %collective-permute-done.6.lower_ref, bf16[105,16,128]{2,1,0:T(8,128)(2,1)S(1)} %collective-permute-done.7.upper_ref), custom_call_target="tpu_custom_call" | custom-call | bytes 3360 | tf_op jit(solution)/shard_map/pallas_call | solution.py:325
  40.1 3.8 %shard_map.85 = (bf16[1280,2688]{1,0:T(8,128)(2,1)S(1)}, bf16[64,2688]{1,0:T(8,128)(2,1)}, bf16[64,2688]{1,0:T(8,128)(2,1)S(1)}, bf16[64,3968]{1,0:T(8,128)(2,1)...) custom-call(s32[1]{0:T(128)} %bitcast.order_ref.z_ref, ...), custom_call_target="tpu_custom_call", output_to_operand_aliasing={{0}: (8, {})} | custom-call | flops 107520 | bytes 1680 | tf_op jit(solution)/shard_map/pallas_call | solution.py:333
  43.9 1.6 %collective-permute-start.15 = (bf16[64,3968]{1,0:T(8,128)(2,1)S(1)}, bf16[64,3968]{1,0:T(8,128)(2,1)S(1)}, u32[]{:S(2)}, u32[]{:S(2)}) collective-permute-start(bf16[64,3968]{1,0:T(8,128)(2,1)S(1)} %get-tuple-element.54), channel_id=1, source_target_pairs={{0,8},{4,12},{8,0},{12,4},{16,24},{20,28},{24,16},{28,20},{1,9},{5... | collective-permute-start | bytes 1523720 | tf_op jit(solution)/shard_map/ppermute | solution.py:228
  45.5 1.5 %collective-permute-start.16 = (bf16[64,3968]{1,0:T(8,128)(2,1)S(1)}, bf16[64,3968]{1,0:T(8,128)(2,1)S(1)}, u32[]{:S(2)}, u32[]{:S(2)}) collective-permute-start(bf16[64,3968]{1,0:T(8,128)(2,1)S(1)} %get-tuple-element.55), channel_id=1, source_target_pairs={{0,16},{4,20},{8,24},{12,28},{16,0},{20,4},{24,8},{28,12},{1,17},{... | collective-permute-start | bytes 1523720 | tf_op jit(solution)/shard_map/ppermute | solution.py:228
  47.3 3.8 %shard_map.86 = (f32[4,16,1280]{2,1,0:T(8,128)S(1)}, bf16[4,16,1280]{2,1,0:T(8,128)(2,1)S(1)}, bf16[4,16,1280]{2,1,0:T(8,128)(2,1)S(1)}, bf16[4,16,1280]{2,1,0:T(8,128)(2,1)S(1)}) custom-call(bf16[64,2688]{1,0:T(8,128)(2,1)S(1)} %get-tuple-element.42.g_ref, bf16[1280,2688]{1,0:T(8,128)(2,1)S(1)} %shard_map.77.w_ref.refs_0_, ...), custom_call_target="tpu_custom_call" | custom-call | flops 215040 | bytes 3360 | tf_op jit(solution)/shard_map/pallas_call | solution.py:384
  51.2 3.8 %shard_map.87 = (f32[4,16,1280]{2,1,0:T(8,128)S(1)}, bf16[4,16,1280]{2,1,0:T(8,128)(2,1)S(1)}, bf16[4,16,1280]{2,1,0:T(8,128)(2,1)S(1)}, bf16[4,16,1280]{2,1,0:T(8,128)(2,1)S(1)}) custom-call(bf16[64,2688]{1,0:T(8,128)(2,1)S(1)} %get-tuple-element.42.g_ref, ...), custom_call_target="tpu_custom_call", output_to_operand_aliasing={{0}: (3, {}), {1}: (4, {}), {2}: (5, {}), {3}: (6, {})} | custom-call | flops 215040 | bytes 3360 | tf_op jit(solution)/shard_map/pallas_call | solution.py:384
  55.1 1.8 %collective-permute-start.12 = (bf16[4,16,1280]{2,1,0:T(8,128)(2,1)S(1)}, bf16[4,16,1280]{2,1,0:T(8,128)(2,1)S(1)}, u32[]{:S(2)}, u32[]{:S(2)}) collective-permute-start(bf16[4,16,1280]{2,1,0:T(8,128)(2,1)S(1)} %get-tuple-element.49), channel_id=1, source_target_pairs={{0,1},{1,0},{2,3},{3,2},{4,5},{5,4},{6,7},{7,6},{8,9},{9,8},{10,11... | collective-permute-start | bytes 491528 | tf_op jit(solution)/shard_map/ppermute | solution.py:232
  56.8 2.6 %collective-permute-start.13 = (bf16[4,16,1280]{2,1,0:T(8,128)(2,1)S(1)}, bf16[4,16,1280]{2,1,0:T(8,128)(2,1)S(1)}, u32[]{:S(2)}, u32[]{:S(2)}) collective-permute-start(bf16[4,16,1280]{2,1,0:T(8,128)(2,1)S(1)} %get-tuple-element.50), channel_id=1, source_target_pairs={{0,2},{1,3},{2,0},{3,1},{4,6},{5,7},{6,4},{7,5},{8,10},{9,11},{10,... | collective-permute-start | bytes 491528 | tf_op jit(solution)/shard_map/ppermute | solution.py:232
  59.4 3.8 %collective-permute-done.12.refs_1_ = bf16[4,16,1280]{2,1,0:T(8,128)(2,1)S(1)} collective-permute-done((bf16[4,16,1280]{2,1,0:T(8,128)(2,1)S(1)}, bf16[4,16,1280]{2,1,0:T(8,128)(2,1)S(1)}, u32[]{:S(2)}, u32[]{:S(2)}) %collective-permute-start.12) | collective-permute-done | bytes 163872 | tf_op jit(solution)/shard_map/ppermute | solution.py:232
  63.3 3.1 %collective-permute-start.14 = (bf16[4,16,1280]{2,1,0:T(8,128)(2,1)S(1)}, bf16[4,16,1280]{2,1,0:T(8,128)(2,1)S(1)}, u32[]{:S(2)}, u32[]{:S(2)}) collective-permute-start(bf16[4,16,1280]{2,1,0:T(8,128)(2,1)S(1)} %get-tuple-element.51), channel_id=1, source_target_pairs={{0,3},{1,2},{2,1},{3,0},{4,7},{5,6},{6,5},{7,4},{8,11},{9,10},{10,... | collective-permute-start | bytes 491528 | tf_op jit(solution)/shard_map/ppermute | solution.py:232
  66.4 4.2 %collective-permute-done.13.refs_2_ = bf16[4,16,1280]{2,1,0:T(8,128)(2,1)S(1)} collective-permute-done((bf16[4,16,1280]{2,1,0:T(8,128)(2,1)S(1)}, bf16[4,16,1280]{2,1,0:T(8,128)(2,1)S(1)}, u32[]{:S(2)}, u32[]{:S(2)}) %collective-permute-start.13) | collective-permute-done | bytes 163872 | tf_op jit(solution)/shard_map/ppermute | solution.py:232
  70.6 3.8 %shard_map.89 = (f32[210,16,128]{2,1,0:T(8,128)S(1)}, bf16[210,16,128]{2,1,0:T(8,128)(2,1)S(1)}) custom-call(s32[1]{0:T(128)} %bitcast.order_ref.z_ref, s32[1,210]{1,0:T(1,128)S(1)} %copy-done.6, s32[1,210]{1,0:T(1,128)S(1)} %copy-done.8, bf16[64,3968]{1,0:T(8,128)(2,1)S(1)} %get-tuple-element.53.refs_0_, ...), custom_call_target="tpu_custom_call" | custom-call | flops 430080 | bytes 3360 | tf_op jit(solution)/shard_map/pallas_call | solution.py:397
  74.5 1.2 %shard_map.88 = bf16[16,5120]{1,0:T(8,128)(2,1)} custom-call(s32[1]{0:T(128)} %bitcast.2.place_ref, bf16[1024,1024]{1,0:T(8,128)(2,1)S(1)} %copy-done.1, f32[4,16,1280]{2,1,0:T(8,128)S(1)} %get-tuple-element.48.refs_0_, bf16[4,16,1280]{2,1,0:T(8,128)(2,1)S(1)} %collective-permute-done.12.refs_1_, bf16[4,16,1280]{2,1,0:T(8,128)(2,1)S(1)} %collective-permute-done.13.refs_2_, ...), custom_call_target="tpu_custom_call" | custom-call | tf_op jit(solution)/shard_map/pallas_call | solution.py:410
  75.7 1.1 %collective-permute-done.18 = bf16[210,16,128]{2,1,0:T(8,128)(2,1)S(1)} collective-permute-done((bf16[210,16,128]{2,1,0:T(8,128)(2,1)S(1)}, bf16[210,16,128]{2,1,0:T(8,128)(2,1)S(1)}, u32[]{:S(2)}, u32[]{:S(2)}) %collective-permute-start.18) | collective-permute-done | bytes 860192 | tf_op jit(solution)/shard_map/ppermute | solution.py:225
  76.8 1.4 %add_bitcast_fusion = f32[16,210,128]{2,0,1:T(8,128)} fusion(f32[210,16,128]{2,1,0:T(8,128)S(1)} %get-tuple-element.57, bf16[210,16,128]{2,1,0:T(8,128)(2,1)S(1)} %collective-permute-done.18), kind=kLoop, calls=%fused_computation | loop fusion | flops 860160 | bytes 4300800 | tf_op jit(solution)/shard_map/transpose | solution.py:443
  (39 shorter events, 5.2 us)
Async XLA Ops:
  0.6 18.6 %collective-permute-start.5 = (bf16[210,16,128]{2,1,0:T(8,128)(2,1)}, bf16[210,16,128]{2,1,0:T(8,128)(2,1)S(1)}, u32[]{:S(2)}, u32[]{:S(2)}) collective-permute-start(bf16[210,16,128]{2,1,0:T(8,128)(2,1)} %bitcast.5), channel_id=1, source_target_pairs={{0,4},{4,0},{8,12},{12,8},{16,20},{20,16},{24,28},{28,24},{1,5},{5... | collective-permute-start | bytes 2580488 | tf_op jit(solution)/shard_map/ppermute | solution.py:225
  1.1 23.1 %collective-permute-start.1 = (bf16[210,16,128]{2,1,0:T(8,128)(2,1)}, bf16[210,16,128]{2,1,0:T(8,128)(2,1)S(1)}, u32[]{:S(2)}, u32[]{:S(2)}) collective-permute-start(bf16[210,16,128]{2,1,0:T(8,128)(2,1)} %bitcast.6), channel_id=1, source_target_pairs={{0,16},{4,20},{8,24},{12,28},{16,0},{20,4},{24,8},{28,12},{1,17},{... | collective-permute-start | bytes 2580488 | tf_op jit(solution)/shard_map/ppermute | solution.py:228
  3.7 21.4 %collective-permute-start = (bf16[210,16,128]{2,1,0:T(8,128)(2,1)}, bf16[210,16,128]{2,1,0:T(8,128)(2,1)S(1)}, u32[]{:S(2)}, u32[]{:S(2)}) collective-permute-start(bf16[210,16,128]{2,1,0:T(8,128)(2,1)} %bitcast.7), channel_id=1, source_target_pairs={{0,8},{4,12},{8,0},{12,4},{16,24},{20,28},{24,16},{28,20},{1,9},{5... | collective-permute-start | bytes 2580488 | tf_op jit(solution)/shard_map/ppermute | solution.py:228
  5.2 0.9 %copy-start.4 = (bf16[16,5120]{1,0:T(8,128)(2,1)S(1)}, bf16[16,5120]{1,0:T(8,128)(2,1)}, u32[]{:S(2)}) copy-start(bf16[16,5120]{1,0:T(8,128)(2,1)} %tokens_ref.1) | copy-start | bytes 491524
  6.8 1.4 %copy-start = (bf16[1024,1024]{1,0:T(8,128)(2,1)}, bf16[1024,1024]{1,0:T(8,128)(2,1)S(1)}, u32[]{:S(2)}) copy-start(bf16[1024,1024]{1,0:T(8,128)(2,1)S(1)} %get-tuple-element.41.onehot_ref) | copy-start | bytes 6291460
  8.2 10.5 %collective-permute-start.3 = (bf16[8,16,640]{2,1,0:T(8,128)(2,1)S(1)}, bf16[8,16,640]{2,1,0:T(8,128)(2,1)S(1)}, u32[]{:S(2)}, u32[]{:S(2)}) collective-permute-start(bf16[8,16,640]{2,1,0:T(8,128)(2,1)S(1)} %get-tuple-element.31.refs_0_), channel_id=1, source_target_pairs={{0,2},{1,3},{2,0},{3,1},{4,6},{5,7},{6,4},{7,5},{8,10},{9,11},{10,... | collective-permute-start | bytes 491528 | tf_op jit(solution)/shard_map/ppermute | solution.py:232
  10.8 13.5 %collective-permute-start.2 = (bf16[8,16,640]{2,1,0:T(8,128)(2,1)S(1)}, bf16[8,16,640]{2,1,0:T(8,128)(2,1)S(1)}, u32[]{:S(2)}, u32[]{:S(2)}) collective-permute-start(bf16[8,16,640]{2,1,0:T(8,128)(2,1)S(1)} %get-tuple-element.31.refs_0_), channel_id=1, source_target_pairs={{0,1},{1,0},{2,3},{3,2},{4,5},{5,4},{6,7},{7,6},{8,9},{9,8},{10,11... | collective-permute-start | bytes 491528 | tf_op jit(solution)/shard_map/ppermute | solution.py:232
  18.7 5.6 %collective-permute-start.4 = (bf16[8,16,640]{2,1,0:T(8,128)(2,1)S(1)}, bf16[8,16,640]{2,1,0:T(8,128)(2,1)S(1)}, u32[]{:S(2)}, u32[]{:S(2)}) collective-permute-start(bf16[8,16,640]{2,1,0:T(8,128)(2,1)S(1)} %collective-permute-done.3.refs_2_), channel_id=1, source_target_pairs={{0,1},{1,0},{2,3},{3,2},{4,5},{5,4},{6,7},{7,6},{8,9},{9,8},{10,11... | collective-permute-start | bytes 491528 | tf_op jit(solution)/shard_map/ppermute | solution.py:232
  19.3 1.2 %copy-start.2 = (bf16[16,210,128]{2,0,1:T(8,128)(2,1)S(1)}, bf16[16,210,128]{2,0,1:T(8,128)(2,1)}, u32[]{:S(2)}) copy-start(bf16[16,210,128]{2,0,1:T(8,128)(2,1)} %param.6) | copy-start | bytes 2580484
  20.4 0.7 copy-start.5
  21.1 0.7 copy-start.7
  25.1 4.0 %collective-permute-start.8 = (bf16[210,16,128]{2,1,0:T(8,128)(2,1)S(1)}, bf16[210,16,128]{2,1,0:T(8,128)(2,1)S(1)}, u32[]{:S(2)}, u32[]{:S(2)}) collective-permute-start(bf16[210,16,128]{2,1,0:T(8,128)(2,1)S(1)} %collective-permute-done.first_ref.own_ref), channel_id=1, source_target_pairs={{0,4},{4,0},{8,12},{12,8},{16,20},{20,16},{24,28},{28,24},{1,5},{5... | collective-permute-start | bytes 2580488 | tf_op jit(solution)/shard_map/ppermute | solution.py:225
  25.1 7.8 %collective-permute-start.9 = (bf16[210,16,128]{2,1,0:T(8,128)(2,1)S(1)}, bf16[210,16,128]{2,1,0:T(8,128)(2,1)S(1)}, u32[]{:S(2)}, u32[]{:S(2)}) collective-permute-start(bf16[210,16,128]{2,1,0:T(8,128)(2,1)S(1)} %collective-permute-done.1.second_ref.own_ref), channel_id=1, source_target_pairs={{0,4},{4,0},{8,12},{12,8},{16,20},{20,16},{24,28},{28,24},{1,5},{5... | collective-permute-start | bytes 2580488 | tf_op jit(solution)/shard_map/ppermute | solution.py:225
  25.7 11.9 %collective-permute-start.6 = (bf16[105,16,128]{2,1,0:T(8,128)(2,1)S(1)}, bf16[105,16,128]{2,1,0:T(8,128)(2,1)S(1)}, u32[]{:S(2)}, u32[]{:S(2)}) collective-permute-start(bf16[105,16,128]{2,1,0:T(8,128)(2,1)S(1)} %get-tuple-element.34), channel_id=1, source_target_pairs={{0,16},{4,20},{8,24},{12,28},{16,0},{20,4},{24,8},{28,12},{1,17},{... | collective-permute-start | bytes 1290248 | tf_op jit(solution)/shard_map/ppermute | solution.py:228
  26.1 3.0 %copy-start.6 = (s32[1,210]{1,0:T(1,128)S(1)}, s32[1,210]{1,0:T(1,128)}, u32[]{:S(2)}) copy-start(s32[1,210]{1,0:T(1,128)} %row_ref.11) | copy-start | bytes 2524
  26.1 3.1 %copy-start.8 = (s32[1,210]{1,0:T(1,128)S(1)}, s32[1,210]{1,0:T(1,128)}, u32[]{:S(2)}) copy-start(s32[1,210]{1,0:T(1,128)} %col_ref.11) | copy-start | bytes 2524
  26.1 11.6 %collective-permute-start.7 = (bf16[105,16,128]{2,1,0:T(8,128)(2,1)S(1)}, bf16[105,16,128]{2,1,0:T(8,128)(2,1)S(1)}, u32[]{:S(2)}, u32[]{:S(2)}) collective-permute-start(bf16[105,16,128]{2,1,0:T(8,128)(2,1)S(1)} %get-tuple-element.35), channel_id=1, source_target_pairs={{0,8},{4,12},{8,0},{12,4},{16,24},{20,28},{24,16},{28,20},{1,9},{5... | collective-permute-start | bytes 1290248 | tf_op jit(solution)/shard_map/ppermute | solution.py:228
  36.8 3.3 %copy-start.3 = (bf16[64,2688]{1,0:T(8,128)(2,1)S(1)}, bf16[64,2688]{1,0:T(8,128)(2,1)}, u32[]{:S(2)}) copy-start(bf16[64,2688]{1,0:T(8,128)(2,1)} %cotangent_ref.1) | copy-start | bytes 1032196
  37.7 2.3 %collective-permute-start.10 = (bf16[105,16,128]{2,1,0:T(8,128)(2,1)S(1)}, bf16[105,16,128]{2,1,0:T(8,128)(2,1)S(1)}, u32[]{:S(2)}, u32[]{:S(2)}) collective-permute-start(bf16[105,16,128]{2,1,0:T(8,128)(2,1)S(1)} %collective-permute-done.6.lower_ref), channel_id=1, source_target_pairs={{0,4},{4,0},{8,12},{12,8},{16,20},{20,16},{24,28},{28,24},{1,5},{5... | collective-permute-start | bytes 1290248 | tf_op jit(solution)/shard_map/ppermute | solution.py:225
  37.7 2.4 %collective-permute-start.11 = (bf16[105,16,128]{2,1,0:T(8,128)(2,1)S(1)}, bf16[105,16,128]{2,1,0:T(8,128)(2,1)S(1)}, u32[]{:S(2)}, u32[]{:S(2)}) collective-permute-start(bf16[105,16,128]{2,1,0:T(8,128)(2,1)S(1)} %collective-permute-done.7.upper_ref), channel_id=1, source_target_pairs={{0,4},{4,0},{8,12},{12,8},{16,20},{20,16},{24,28},{28,24},{1,5},{5... | collective-permute-start | bytes 1290248 | tf_op jit(solution)/shard_map/ppermute | solution.py:225
  43.9 26.7 %collective-permute-start.15 = (bf16[64,3968]{1,0:T(8,128)(2,1)S(1)}, bf16[64,3968]{1,0:T(8,128)(2,1)S(1)}, u32[]{:S(2)}, u32[]{:S(2)}) collective-permute-start(bf16[64,3968]{1,0:T(8,128)(2,1)S(1)} %get-tuple-element.54), channel_id=1, source_target_pairs={{0,8},{4,12},{8,0},{12,4},{16,24},{20,28},{24,16},{28,20},{1,9},{5... | collective-permute-start | bytes 1523720 | tf_op jit(solution)/shard_map/ppermute | solution.py:228
  45.5 25.1 %collective-permute-start.16 = (bf16[64,3968]{1,0:T(8,128)(2,1)S(1)}, bf16[64,3968]{1,0:T(8,128)(2,1)S(1)}, u32[]{:S(2)}, u32[]{:S(2)}) collective-permute-start(bf16[64,3968]{1,0:T(8,128)(2,1)S(1)} %get-tuple-element.55), channel_id=1, source_target_pairs={{0,16},{4,20},{8,24},{12,28},{16,0},{20,4},{24,8},{28,12},{1,17},{... | collective-permute-start | bytes 1523720 | tf_op jit(solution)/shard_map/ppermute | solution.py:228
  47.0 23.6 %collective-permute-start.17 = (bf16[64,3968]{1,0:T(8,128)(2,1)S(1)}, bf16[64,3968]{1,0:T(8,128)(2,1)S(1)}, u32[]{:S(2)}, u32[]{:S(2)}) collective-permute-start(bf16[64,3968]{1,0:T(8,128)(2,1)S(1)} %get-tuple-element.56), channel_id=1, source_target_pairs={{0,24},{4,28},{8,16},{12,20},{16,8},{20,12},{24,0},{28,4},{1,25},{... | collective-permute-start | bytes 1523720 | tf_op jit(solution)/shard_map/ppermute | solution.py:228
  51.2 23.3 %copy-start.1 = (bf16[1024,1024]{1,0:T(8,128)(2,1)S(1)}, bf16[1024,1024]{1,0:T(8,128)(2,1)}, u32[]{:S(2)}) copy-start(bf16[1024,1024]{1,0:T(8,128)(2,1)} %copy-done) | copy-start | bytes 6291460
  55.1 8.2 %collective-permute-start.12 = (bf16[4,16,1280]{2,1,0:T(8,128)(2,1)S(1)}, bf16[4,16,1280]{2,1,0:T(8,128)(2,1)S(1)}, u32[]{:S(2)}, u32[]{:S(2)}) collective-permute-start(bf16[4,16,1280]{2,1,0:T(8,128)(2,1)S(1)} %get-tuple-element.49), channel_id=1, source_target_pairs={{0,1},{1,0},{2,3},{3,2},{4,5},{5,4},{6,7},{7,6},{8,9},{9,8},{10,11... | collective-permute-start | bytes 491528 | tf_op jit(solution)/shard_map/ppermute | solution.py:232
  56.8 13.8 %collective-permute-start.13 = (bf16[4,16,1280]{2,1,0:T(8,128)(2,1)S(1)}, bf16[4,16,1280]{2,1,0:T(8,128)(2,1)S(1)}, u32[]{:S(2)}, u32[]{:S(2)}) collective-permute-start(bf16[4,16,1280]{2,1,0:T(8,128)(2,1)S(1)} %get-tuple-element.50), channel_id=1, source_target_pairs={{0,2},{1,3},{2,0},{3,1},{4,6},{5,7},{6,4},{7,5},{8,10},{9,11},{10,... | collective-permute-start | bytes 491528 | tf_op jit(solution)/shard_map/ppermute | solution.py:232
  63.3 7.3 %collective-permute-start.14 = (bf16[4,16,1280]{2,1,0:T(8,128)(2,1)S(1)}, bf16[4,16,1280]{2,1,0:T(8,128)(2,1)S(1)}, u32[]{:S(2)}, u32[]{:S(2)}) collective-permute-start(bf16[4,16,1280]{2,1,0:T(8,128)(2,1)S(1)} %get-tuple-element.51), channel_id=1, source_target_pairs={{0,3},{1,2},{2,1},{3,0},{4,7},{5,6},{6,5},{7,4},{8,11},{9,10},{10,... | collective-permute-start | bytes 491528 | tf_op jit(solution)/shard_map/ppermute | solution.py:232
  74.4 2.5 %collective-permute-start.18 = (bf16[210,16,128]{2,1,0:T(8,128)(2,1)S(1)}, bf16[210,16,128]{2,1,0:T(8,128)(2,1)S(1)}, u32[]{:S(2)}, u32[]{:S(2)}) collective-permute-start(bf16[210,16,128]{2,1,0:T(8,128)(2,1)S(1)} %get-tuple-element.58), channel_id=1, source_target_pairs={{0,4},{4,0},{8,12},{12,8},{16,20},{20,16},{24,28},{28,24},{1,5},{5... | collective-permute-start | bytes 2580488 | tf_op jit(solution)/shard_map/ppermute | solution.py:225

commit v4 on v3

--- a/solution.py
+++ b/solution.py
@@ -114,11 +114,21 @@
     upper_ref[...] = second_ref[lower_ref.shape[0] :]
 
 
-def half_weight_kernel(half, order_ref, row_ref, col_ref, lower_ref, upper_ref, out_ref):
+def blank_kernel(order_ref, out_ref):
+    out_ref[...] = jnp.zeros_like(out_ref)
+
+
+def half_weight_kernel(n_tp, step, half, order_ref, row_ref, col_ref, lower_ref, upper_ref, blank_ref, early_ref, *refs):
+    x_refs = refs[:n_tp]
+    out_ref, sum_ref = refs[n_tp:]
     slots = row_ref.shape[1]
-    out_ref[...] = jnp.zeros_like(out_ref)
+    rows = out_ref.shape[0] // 2
     place_tiles(0, row_ref, col_ref, lower_ref, out_ref, 0, half)
     place_tiles(0, row_ref, col_ref, upper_ref, out_ref, half, slots - half)
+    lhs = jnp.concatenate([x_ref[2 * step] for x_ref in x_refs], axis=0)
+    sum_ref[...] = early_ref[...] + jnp.dot(
+        lhs, out_ref[:rows, :], preferred_element_type=F32
+    )
 
 
 def slice_rows(x_refs, step):
@@ -134,10 +144,11 @@
     rows = x_refs[0].shape[1]
     place_tiles(1, row_ref, col_ref, lower_ref, w_ref, 0, half)
     place_tiles(1, row_ref, col_ref, upper_ref, w_ref, half, row_ref.shape[1] - half)
-    lhs = slice_rows(x_refs, step)
+    half_rows = w_ref.shape[0] // 2
+    lhs = jnp.concatenate([x_ref[2 * step + 1] for x_ref in x_refs], axis=0)
     for left, right in column_blocks(w_ref.shape[1]):
         hidden = early_ref[:, left:right] + jnp.dot(
-            lhs, w_ref[:, left:right], preferred_element_type=F32
+            lhs, w_ref[half_rows:, left:right], preferred_element_type=F32
         )
         act_value, act_slope = gelu_pair(hidden)
         act_value = act_value.astype(BF16)
@@ -287,8 +298,16 @@
         token_parts = along_z(split)
         tiles += [to_chip(tiles[0], 1), to_chip(tiles[0], 2)]
         weights = [make_weight(0, z_index)]
-        tiles[1], tiles[2], *_ = lax.optimization_barrier(
-            (tiles[1], tiles[2], *token_parts[1:], weights[0])
+        blank = pl.pallas_call(
+            blank_kernel,
+            out_shape=jax.ShapeDtypeStruct((depth, columns), BF16),
+            in_specs=[spec(SMEM)],
+            out_specs=spec(),
+            compiler_params=params(10),
+            cost_estimate=cost(0, 2 * depth * columns),
+        )(after(z_index, weights[0]))
+        tiles[1], tiles[2], blank, *_ = lax.optimization_barrier(
+            (tiles[1], tiles[2], blank, *token_parts[1:], weights[0])
         )
         half = slots // 2
         relay = pl.pallas_call(
@@ -302,7 +321,7 @@
             compiler_params=params(8),
         )(tiles[1], tiles[2])
         relayed = [to_chip(relay[0], 2), to_chip(relay[1], 1)]
-        others += [to_core(part) for part in tiles[1:]]
+        others += [to_core(after(part, *relay)) for part in tiles[1:]]
         for step in range(1, chips - 1):
             weights.append(make_weight(step, after(z_index, weights[-1], *relay)))
         early = add_hidden(0)
@@ -322,14 +341,18 @@
         slice_parts = along_z(jnp.stack(pieces))
 
     if fast:
-        half_weight = pl.pallas_call(
-            functools.partial(half_weight_kernel, half),
-            out_shape=jax.ShapeDtypeStruct((depth, columns), BF16),
-            in_specs=[spec(SMEM)] * 3 + [spec()] * 2,
-            out_specs=spec(),
-            compiler_params=params(10),
-            cost_estimate=cost(0, 2 * 2 * depth * columns),
-        )(z_index, tile_row, tile_col, *relayed)
+        half_weight, early = pl.pallas_call(
+            functools.partial(half_weight_kernel, n_tp, chips - 1, half),
+            out_shape=[
+                jax.ShapeDtypeStruct((depth, columns), BF16),
+                jax.ShapeDtypeStruct((block, columns), F32),
+            ],
+            in_specs=[spec(SMEM)] * 3 + [spec()] * (4 + n_tp),
+            out_specs=[spec()] * 2,
+            input_output_aliases={5: 0, 6: 1},
+            compiler_params=params(20),
+            cost_estimate=cost(block * depth * columns, 2 * depth * columns),
+        )(z_index, tile_row, tile_col, *relayed, blank, early, *token_parts)
         last_weight, act, hidden_grad, *packs = pl.pallas_call(
             functools.partial(hidden_kernel, n_tp, chips - 1, half),
             out_shape=[
@@ -393,7 +416,10 @@
                 compiler_params=params(18),
                 cost_estimate=cost(4 * block * depth * columns, 4 * depth * columns),
             )(hidden_grad, *weights[first : first + 2], *backs)
-        returned = [backs[0]] + [to_z(backs[j], j) for j in range(1, n_tp)]
+        near = after(backs[1], packs[1])
+        returned = [backs[0]] + [
+            to_z(near if j == 1 else backs[j], j) for j in range(1, n_tp)
+        ]
         mine, theirs = pl.pallas_call(
             functools.partial(tile_grad_kernel, chips, grad_scale),
             out_shape=[

time: 79.1 us -> 78.4 us (level)
  starting transfers between devices: 23.5 us -> 21 us
  waiting for transfers between devices: 17.4 us -> 19 us
    ppermute x6, starting transfers between devices: 12.2 us -> 9.75 us  [to_z(): return lax.ppermute(value, 'tp', [(i, i ^ step) for i in range(n_tp)])]
    ppermute x6, waiting for transfers between devices: 14.4 us -> 16.6 us  [to_z(): return lax.ppermute(value, 'tp', [(i, i ^ step) for i in range(n_tp)])]
    pallas_call x1 -> x2, Pallas kernels: 1.75 us -> 2.48 us  [the longest x1 2.01 us: local(): pl.pallas_call(functools.partial(half_weight_kernel, n_tp, chips - 1, hal...]
  transfers between devices with their start and end apart: 19 -> 19, of which waited for: 8 -> 6; matrix products, arithmetic and copies ran while one was open for 0% -> 0% of each run, Pallas kernels for 29% -> 30%
where the time goes in v4:
time: 78.4 us; the launch traced here: 77.5 us
  Pallas kernels  30.5 us (39%)
  starting transfers between devices  21 us (27%)
  waiting for transfers between devices  19 us (24%)
  local copies, waits for them, and re-layouts  4.8 us (6%)
  other arithmetic  1.36 us (2%)
  between operations  0.88 us (1%)
    ppermute x6, waiting for transfers between devices, to_z(): return lax.ppermute(value, 'tp', [(i, i ^ step) for i in range(n_tp)])  16.6 us
    ppermute x6, starting transfers between devices, to_z(): return lax.ppermute(value, 'tp', [(i, i ^ step) for i in range(n_tp)])  9.75 us
    ppermute x7, starting transfers between devices, to_chip(): return lax.ppermute(value, 'fsdp', [(f, f ^ 2 * step) for f in range(fsdp)])  9.57 us
    pallas_call x2, Pallas kernels, local(): pl.pallas_call(functools.partial(back_kernel, n_tp, first, 2), out_shape=...  7.69 us
    pallas_call x3, Pallas kernels, make_weight(): pl.pallas_call(weight_kernel, out_shape=jax.ShapeDtypeStruct((depth, colu...  7.44 us
    unnamed x18, local copies, waits for them, and re-layouts  4.8 us
    pallas_call x3, Pallas kernels, add_hidden(): pl.pallas_call(functools.partial(early_kernel, n_tp, step), out_shape=jax...  3.92 us
    pallas_call x1, Pallas kernels, local(): pl.pallas_call(functools.partial(tile_grad_kernel, chips, grad_scale), ou...  3.75 us
  transfers between devices with their start and end apart: 19, of which 6 were waited for; matrix products, arithmetic and copies ran while one was open for 0% of the time, Pallas kernels for 30%

profile of v4, /device:TPU:0, one launch (start us, length us, event | category | flops | bytes accessed | tf_op | source)
XLA Modules:
  0.0 77.5 jit_solution(6427118779603107603)
XLA Ops:
  1.1 2.6 %collective-permute-start.1 = (bf16[210,16,128]{2,1,0:T(8,128)(2,1)}, bf16[210,16,128]{2,1,0:T(8,128)(2,1)S(1)}, u32[]{:S(2)}, u32[]{:S(2)}) collective-permute-start(bf16[210,16,128]{2,1,0:T(8,128)(2,1)} %bitcast.6), channel_id=1, source_target_pairs={{0,16},{4,20},{8,24},{12,28},{16,0},{20,4},{24,8},{28,12},{1,17},{... | collective-permute-start | bytes 2580488 | tf_op jit(solution)/shard_map/ppermute | solution.py:239
  3.7 1.5 %collective-permute-start = (bf16[210,16,128]{2,1,0:T(8,128)(2,1)}, bf16[210,16,128]{2,1,0:T(8,128)(2,1)S(1)}, u32[]{:S(2)}, u32[]{:S(2)}) collective-permute-start(bf16[210,16,128]{2,1,0:T(8,128)(2,1)} %bitcast.7), channel_id=1, source_target_pairs={{0,8},{4,12},{8,0},{12,4},{16,24},{20,28},{24,16},{28,20},{1,9},{5... | collective-permute-start | bytes 2580488 | tf_op jit(solution)/shard_map/ppermute | solution.py:239
  5.2 0.9 %copy-done.4 = bf16[16,5120]{1,0:T(8,128)(2,1)S(1)} copy-done((bf16[16,5120]{1,0:T(8,128)(2,1)S(1)}, bf16[16,5120]{1,0:T(8,128)(2,1)}, u32[]{:S(2)}) %copy-start.4) | copy-done | bytes 163864
  6.8 1.3 %copy-done = bf16[1024,1024]{1,0:T(8,128)(2,1)} copy-done((bf16[1024,1024]{1,0:T(8,128)(2,1)}, bf16[1024,1024]{1,0:T(8,128)(2,1)S(1)}, u32[]{:S(2)}) %copy-start) | copy-done | bytes 2097176
  8.2 2.6 %collective-permute-start.4 = (bf16[8,16,640]{2,1,0:T(8,128)(2,1)S(1)}, bf16[8,16,640]{2,1,0:T(8,128)(2,1)S(1)}, u32[]{:S(2)}, u32[]{:S(2)}) collective-permute-start(bf16[8,16,640]{2,1,0:T(8,128)(2,1)S(1)} %get-tuple-element.39.refs_0_), channel_id=1, source_target_pairs={{0,2},{1,3},{2,0},{3,1},{4,6},{5,7},{6,4},{7,5},{8,10},{9,11},{10,... | collective-permute-start | bytes 491528 | tf_op jit(solution)/shard_map/ppermute | solution.py:243
  10.8 1.6 %collective-permute-start.3 = (bf16[8,16,640]{2,1,0:T(8,128)(2,1)S(1)}, bf16[8,16,640]{2,1,0:T(8,128)(2,1)S(1)}, u32[]{:S(2)}, u32[]{:S(2)}) collective-permute-start(bf16[8,16,640]{2,1,0:T(8,128)(2,1)S(1)} %get-tuple-element.39.refs_0_), channel_id=1, source_target_pairs={{0,1},{1,0},{2,3},{3,2},{4,5},{5,4},{6,7},{7,6},{8,9},{9,8},{10,11... | collective-permute-start | bytes 491528 | tf_op jit(solution)/shard_map/ppermute | solution.py:243
  12.4 6.3 %collective-permute-done.4.refs_2_ = bf16[8,16,640]{2,1,0:T(8,128)(2,1)S(1)} collective-permute-done((bf16[8,16,640]{2,1,0:T(8,128)(2,1)S(1)}, bf16[8,16,640]{2,1,0:T(8,128)(2,1)S(1)}, u32[]{:S(2)}, u32[]{:S(2)}) %collective-permute-start.4) | collective-permute-done | bytes 163872 | tf_op jit(solution)/shard_map/ppermute | solution.py:243
  19.3 1.2 %copy-done.2 = bf16[16,210,128]{2,0,1:T(8,128)(2,1)S(1)} copy-done((bf16[16,210,128]{2,0,1:T(8,128)(2,1)S(1)}, bf16[16,210,128]{2,0,1:T(8,128)(2,1)}, u32[]{:S(2)}) %copy-start.2) | copy-done | bytes 860184
  20.4 0.7 copy-done.5
  21.1 0.7 copy-done.7
  21.8 2.5 %shard_map.76.w_ref.refs_0_ = bf16[1280,2688]{1,0:T(8,128)(2,1)S(1)} custom-call(s32[1]{0:T(128)} %bitcast.order_ref.z_ref, s32[1,210]{1,0:T(1,128)S(1)} %copy-done.5, s32[1,210]{1,0:T(1,128)S(1)} %copy-done.7, bf16[210,16,128]{2,1,0:T(8,128)(2,1)S(1)} %bitcast.8, bf16[210,16,128]{2,1,0:T(8,128)(2,1)S(1)} %collective-permute-done.2.other_ref), custom_call_target="tpu_custom_call" | custom-call | bytes 3360 | tf_op jit(solution)/shard_map/pallas_call | solution.py:268
  26.1 1.7 %collective-permute-start.7 = (bf16[105,16,128]{2,1,0:T(8,128)(2,1)S(1)}, bf16[105,16,128]{2,1,0:T(8,128)(2,1)S(1)}, u32[]{:S(2)}, u32[]{:S(2)}) collective-permute-start(bf16[105,16,128]{2,1,0:T(8,128)(2,1)S(1)} %get-tuple-element.43), channel_id=1, source_target_pairs={{0,8},{4,12},{8,0},{12,4},{16,24},{20,28},{24,16},{28,20},{1,9},{5... | collective-permute-start | bytes 1290248 | tf_op jit(solution)/shard_map/ppermute | solution.py:239
  27.8 1.3 %shard_map.82.refs_4_ = f32[64,2688]{1,0:T(8,128)S(1)} custom-call(bf16[1280,2688]{1,0:T(8,128)(2,1)S(1)} %shard_map.76.w_ref.refs_0_, bf16[8,16,640]{2,1,0:T(8,128)(2,1)S(1)} %get-tuple-element.39.refs_0_, bf16[8,16,640]{2,1,0:T(8,128)(2,1)S(1)} %collective-permute-done.3.refs_1_, bf16[8,16,640]{2,1,0:T(8,128)(2,1)S(1)} %collective-permute-done.4.refs_2_, ...), custom_call_target="tpu_custom_call" | custom-call | flops 107520 | bytes 1680 | tf_op jit(solution)/shard_map/pallas_call | solution.py:278
  29.1 2.5 %shard_map.80.w_ref.refs_1_ = bf16[1280,2688]{1,0:T(8,128)(2,1)S(1)} custom-call(s32[1]{0:T(128)} %bitcast.order_ref.z_ref, s32[1,210]{1,0:T(1,128)S(1)} %copy-done.6, s32[1,210]{1,0:T(1,128)S(1)} %copy-done.8, bf16[210,16,128]{2,1,0:T(8,128)(2,1)S(1)} %collective-permute-done.first_ref.own_ref, bf16[210,16,128]{2,1,0:T(8,128)(2,1)S(1)} %collective-permute-done.8.other_ref), custom_call_target="tpu_custom_call" | custom-call | bytes 3360 | tf_op jit(solution)/shard_map/pallas_call | solution.py:268
  31.6 1.3 %shard_map.83.refs_4_ = f32[64,2688]{1,0:T(8,128)S(1)} custom-call(bf16[1280,2688]{1,0:T(8,128)(2,1)S(1)} %shard_map.80.w_ref.refs_1_, bf16[8,16,640]{2,1,0:T(8,128)(2,1)S(1)} %get-tuple-element.39.refs_0_, bf16[8,16,640]{2,1,0:T(8,128)(2,1)S(1)} %collective-permute-done.3.refs_1_, bf16[8,16,640]{2,1,0:T(8,128)(2,1)S(1)} %collective-permute-done.4.refs_2_, ...), custom_call_target="tpu_custom_call" | custom-call | flops 107520 | bytes 1680 | tf_op jit(solution)/shard_map/pallas_call | solution.py:278
  32.9 2.5 %shard_map.81.w_ref.refs_0_ = bf16[1280,2688]{1,0:T(8,128)(2,1)S(1)} custom-call(s32[1]{0:T(128)} %bitcast.order_ref.z_ref, s32[1,210]{1,0:T(1,128)S(1)} %copy-done.6, s32[1,210]{1,0:T(1,128)S(1)} %copy-done.8, bf16[210,16,128]{2,1,0:T(8,128)(2,1)S(1)} %collective-permute-done.1.second_ref.own_ref, bf16[210,16,128]{2,1,0:T(8,128)(2,1)S(1)} %collective-permute-done.9.other_ref), custom_call_target="tpu_custom_call" | custom-call | bytes 3360 | tf_op jit(solution)/shard_map/pallas_call | solution.py:268
  35.4 1.3 %shard_map.84.early_ref = f32[64,2688]{1,0:T(8,128)S(1)} custom-call(bf16[1280,2688]{1,0:T(8,128)(2,1)S(1)} %shard_map.81.w_ref.refs_0_, bf16[8,16,640]{2,1,0:T(8,128)(2,1)S(1)} %get-tuple-element.39.refs_0_, bf16[8,16,640]{2,1,0:T(8,128)(2,1)S(1)} %collective-permute-done.3.refs_1_, bf16[8,16,640]{2,1,0:T(8,128)(2,1)S(1)} %collective-permute-done.4.refs_2_, ...), custom_call_target="tpu_custom_call" | custom-call | flops 107520 | bytes 1680 | tf_op jit(solution)/shard_map/pallas_call | solution.py:278
  36.8 0.9 %collective-permute-done.6.lower_ref = bf16[105,16,128]{2,1,0:T(8,128)(2,1)S(1)} collective-permute-done((bf16[105,16,128]{2,1,0:T(8,128)(2,1)S(1)}, bf16[105,16,128]{2,1,0:T(8,128)(2,1)S(1)}, u32[]{:S(2)}, u32[]{:S(2)}) %collective-permute-start.6) | collective-permute-done | bytes 430112 | tf_op jit(solution)/shard_map/ppermute | solution.py:239
  38.2 2.0 %shard_map.85 = (bf16[1280,2688]{1,0:T(8,128)(2,1)S(1)}, f32[64,2688]{1,0:T(8,128)S(1)}) custom-call(s32[1]{0:T(128)} %bitcast.order_ref.z_ref, s32[1,210]{1,0:T(1,128)S(1)} %copy-done.6, s32[1,210]{1,0:T(1,128)S(1)} %copy-done.8, bf16[105,16,128]{2,1,0:T(8,128)(2,1)S(1)} %collective-permute-done.6.lower_ref, ...), custom_call_target="tpu_custom_call", output_to_operand_aliasing={{0}: (5, {}), {1}: (6, {})} | custom-call | flops 53760 | bytes 1680 | tf_op jit(solution)/shard_map/pallas_call | solution.py:344
  40.2 3.2 %shard_map.86 = (bf16[1280,2688]{1,0:T(8,128)(2,1)S(1)}, bf16[64,2688]{1,0:T(8,128)(2,1)}, bf16[64,2688]{1,0:T(8,128)(2,1)S(1)}, bf16[64,3968]{1,0:T(8,128)(2,1)...) custom-call(s32[1]{0:T(128)} %bitcast.order_ref.z_ref, ...), custom_call_target="tpu_custom_call", output_to_operand_aliasing={{0}: (8, {})} | custom-call | flops 107520 | bytes 1680 | tf_op jit(solution)/shard_map/pallas_call | solution.py:356
  43.4 1.7 %collective-permute-start.12 = (bf16[64,3968]{1,0:T(8,128)(2,1)S(1)}, bf16[64,3968]{1,0:T(8,128)(2,1)S(1)}, u32[]{:S(2)}, u32[]{:S(2)}) collective-permute-start(bf16[64,3968]{1,0:T(8,128)(2,1)S(1)} %get-tuple-element.63), channel_id=1, source_target_pairs={{0,8},{4,12},{8,0},{12,4},{16,24},{20,28},{24,16},{28,20},{1,9},{5... | collective-permute-start | bytes 1523720 | tf_op jit(solution)/shard_map/ppermute | solution.py:239
  45.2 1.5 %collective-permute-start.16 = (bf16[64,3968]{1,0:T(8,128)(2,1)S(1)}, bf16[64,3968]{1,0:T(8,128)(2,1)S(1)}, u32[]{:S(2)}, u32[]{:S(2)}) collective-permute-start(bf16[64,3968]{1,0:T(8,128)(2,1)S(1)} %get-tuple-element.69), channel_id=1, source_target_pairs={{0,16},{4,20},{8,24},{12,28},{16,0},{20,4},{24,8},{28,12},{1,17},{... | collective-permute-start | bytes 1523720 | tf_op jit(solution)/shard_map/ppermute | solution.py:239
  46.9 3.8 %shard_map.87 = (f32[4,16,1280]{2,1,0:T(8,128)S(1)}, bf16[4,16,1280]{2,1,0:T(8,128)(2,1)S(1)}, bf16[4,16,1280]{2,1,0:T(8,128)(2,1)S(1)}, bf16[4,16,1280]{2,1,0:T(8,128)(2,1)S(1)}) custom-call(bf16[64,2688]{1,0:T(8,128)(2,1)S(1)} %get-tuple-element.55.g_ref, bf16[1280,2688]{1,0:T(8,128)(2,1)S(1)} %shard_map.76.w_ref.refs_0_, ...), custom_call_target="tpu_custom_call" | custom-call | flops 215040 | bytes 3360 | tf_op jit(solution)/shard_map/pallas_call | solution.py:407
  50.8 3.8 %shard_map.88 = (f32[4,16,1280]{2,1,0:T(8,128)S(1)}, bf16[4,16,1280]{2,1,0:T(8,128)(2,1)S(1)}, bf16[4,16,1280]{2,1,0:T(8,128)(2,1)S(1)}, bf16[4,16,1280]{2,1,0:T(8,128)(2,1)S(1)}) custom-call(bf16[64,2688]{1,0:T(8,128)(2,1)S(1)} %get-tuple-element.55.g_ref, ...), custom_call_target="tpu_custom_call", output_to_operand_aliasing={{0}: (3, {}), {1}: (4, {}), {2}: (5, {}), {3}: (6, {})} | custom-call | flops 215040 | bytes 3360 | tf_op jit(solution)/shard_map/pallas_call | solution.py:407
  54.7 3.3 %collective-permute-start.14 = (bf16[4,16,1280]{2,1,0:T(8,128)(2,1)S(1)}, bf16[4,16,1280]{2,1,0:T(8,128)(2,1)S(1)}, u32[]{:S(2)}, u32[]{:S(2)}) collective-permute-start(bf16[4,16,1280]{2,1,0:T(8,128)(2,1)S(1)} %get-tuple-element.65), channel_id=1, source_target_pairs={{0,2},{1,3},{2,0},{3,1},{4,6},{5,7},{6,4},{7,5},{8,10},{9,11},{10,... | collective-permute-start | bytes 491528 | tf_op jit(solution)/shard_map/ppermute | solution.py:243
  58.0 0.9 %collective-permute-start.15 = (bf16[4,16,1280]{2,1,0:T(8,128)(2,1)S(1)}, bf16[4,16,1280]{2,1,0:T(8,128)(2,1)S(1)}, u32[]{:S(2)}, u32[]{:S(2)}) collective-permute-start(bf16[4,16,1280]{2,1,0:T(8,128)(2,1)S(1)} %get-tuple-element.66), channel_id=1, source_target_pairs={{0,3},{1,2},{2,1},{3,0},{4,7},{5,6},{6,5},{7,4},{8,11},{9,10},{10,... | collective-permute-start | bytes 491528 | tf_op jit(solution)/shard_map/ppermute | solution.py:243
  58.9 0.8 %collective-permute-start.13 = (bf16[4,16,1280]{2,1,0:T(8,128)(2,1)S(1)}, bf16[4,16,1280]{2,1,0:T(8,128)(2,1)S(1)}, u32[]{:S(2)}, u32[]{:S(2)}) collective-permute-start(bf16[4,16,1280]{2,1,0:T(8,128)(2,1)S(1)} %get-tuple-element.64), channel_id=1, source_target_pairs={{0,1},{1,0},{2,3},{3,2},{4,5},{5,4},{6,7},{7,6},{8,9},{9,8},{10,11... | collective-permute-start | bytes 491528 | tf_op jit(solution)/shard_map/ppermute | solution.py:243
  59.7 9.6 %collective-permute-done.14.refs_2_ = bf16[4,16,1280]{2,1,0:T(8,128)(2,1)S(1)} collective-permute-done((bf16[4,16,1280]{2,1,0:T(8,128)(2,1)S(1)}, bf16[4,16,1280]{2,1,0:T(8,128)(2,1)S(1)}, u32[]{:S(2)}, u32[]{:S(2)}) %collective-permute-start.14) | collective-permute-done | bytes 163872 | tf_op jit(solution)/shard_map/ppermute | solution.py:243
  69.9 3.8 %shard_map.90 = (f32[210,16,128]{2,1,0:T(8,128)S(1)}, bf16[210,16,128]{2,1,0:T(8,128)(2,1)S(1)}) custom-call(s32[1]{0:T(128)} %bitcast.order_ref.z_ref, s32[1,210]{1,0:T(1,128)S(1)} %copy-done.6, s32[1,210]{1,0:T(1,128)S(1)} %copy-done.8, bf16[64,3968]{1,0:T(8,128)(2,1)S(1)} %get-tuple-element.68.refs_0_, ...), custom_call_target="tpu_custom_call" | custom-call | flops 430080 | bytes 3360 | tf_op jit(solution)/shard_map/pallas_call | solution.py:423
  73.8 1.2 %shard_map.89 = bf16[16,5120]{1,0:T(8,128)(2,1)} custom-call(s32[1]{0:T(128)} %bitcast.2.place_ref, bf16[1024,1024]{1,0:T(8,128)(2,1)S(1)} %copy-done.1, f32[4,16,1280]{2,1,0:T(8,128)S(1)} %get-tuple-element.61.refs_0_, bf16[4,16,1280]{2,1,0:T(8,128)(2,1)S(1)} %collective-permute-done.13.refs_1_, bf16[4,16,1280]{2,1,0:T(8,128)(2,1)S(1)} %collective-permute-done.14.refs_2_, ...), custom_call_target="tpu_custom_call" | custom-call | tf_op jit(solution)/shard_map/pallas_call | solution.py:436
  75.0 1.1 %collective-permute-done.18 = bf16[210,16,128]{2,1,0:T(8,128)(2,1)S(1)} collective-permute-done((bf16[210,16,128]{2,1,0:T(8,128)(2,1)S(1)}, bf16[210,16,128]{2,1,0:T(8,128)(2,1)S(1)}, u32[]{:S(2)}, u32[]{:S(2)}) %collective-permute-start.18) | collective-permute-done | bytes 860192 | tf_op jit(solution)/shard_map/ppermute | solution.py:236
  76.2 1.4 %add_bitcast_fusion = f32[16,210,128]{2,0,1:T(8,128)} fusion(f32[210,16,128]{2,1,0:T(8,128)S(1)} %get-tuple-element.71, bf16[210,16,128]{2,1,0:T(8,128)(2,1)S(1)} %collective-permute-done.18), kind=kLoop, calls=%fused_computation | loop fusion | flops 860160 | bytes 4300800 | tf_op jit(solution)/shard_map/transpose | solution.py:469
  (40 shorter events, 5.0 us)
Async XLA Ops:
  0.6 18.6 %collective-permute-start.2 = (bf16[210,16,128]{2,1,0:T(8,128)(2,1)}, bf16[210,16,128]{2,1,0:T(8,128)(2,1)S(1)}, u32[]{:S(2)}, u32[]{:S(2)}) collective-permute-start(bf16[210,16,128]{2,1,0:T(8,128)(2,1)} %bitcast.5), channel_id=1, source_target_pairs={{0,4},{4,0},{8,12},{12,8},{16,20},{20,16},{24,28},{28,24},{1,5},{5... | collective-permute-start | bytes 2580488 | tf_op jit(solution)/shard_map/ppermute | solution.py:236
  1.1 23.6 %collective-permute-start.1 = (bf16[210,16,128]{2,1,0:T(8,128)(2,1)}, bf16[210,16,128]{2,1,0:T(8,128)(2,1)S(1)}, u32[]{:S(2)}, u32[]{:S(2)}) collective-permute-start(bf16[210,16,128]{2,1,0:T(8,128)(2,1)} %bitcast.6), channel_id=1, source_target_pairs={{0,16},{4,20},{8,24},{12,28},{16,0},{20,4},{24,8},{28,12},{1,17},{... | collective-permute-start | bytes 2580488 | tf_op jit(solution)/shard_map/ppermute | solution.py:239
  3.7 21.4 %collective-permute-start = (bf16[210,16,128]{2,1,0:T(8,128)(2,1)}, bf16[210,16,128]{2,1,0:T(8,128)(2,1)S(1)}, u32[]{:S(2)}, u32[]{:S(2)}) collective-permute-start(bf16[210,16,128]{2,1,0:T(8,128)(2,1)} %bitcast.7), channel_id=1, source_target_pairs={{0,8},{4,12},{8,0},{12,4},{16,24},{20,28},{24,16},{28,20},{1,9},{5... | collective-permute-start | bytes 2580488 | tf_op jit(solution)/shard_map/ppermute | solution.py:239
  5.2 0.9 %copy-start.4 = (bf16[16,5120]{1,0:T(8,128)(2,1)S(1)}, bf16[16,5120]{1,0:T(8,128)(2,1)}, u32[]{:S(2)}) copy-start(bf16[16,5120]{1,0:T(8,128)(2,1)} %tokens_ref.1) | copy-start | bytes 491524
  6.8 1.4 %copy-start = (bf16[1024,1024]{1,0:T(8,128)(2,1)}, bf16[1024,1024]{1,0:T(8,128)(2,1)S(1)}, u32[]{:S(2)}) copy-start(bf16[1024,1024]{1,0:T(8,128)(2,1)S(1)} %get-tuple-element.54.onehot_ref) | copy-start | bytes 6291460
  8.2 10.5 %collective-permute-start.4 = (bf16[8,16,640]{2,1,0:T(8,128)(2,1)S(1)}, bf16[8,16,640]{2,1,0:T(8,128)(2,1)S(1)}, u32[]{:S(2)}, u32[]{:S(2)}) collective-permute-start(bf16[8,16,640]{2,1,0:T(8,128)(2,1)S(1)} %get-tuple-element.39.refs_0_), channel_id=1, source_target_pairs={{0,2},{1,3},{2,0},{3,1},{4,6},{5,7},{6,4},{7,5},{8,10},{9,11},{10,... | collective-permute-start | bytes 491528 | tf_op jit(solution)/shard_map/ppermute | solution.py:243
  10.8 14.0 %collective-permute-start.3 = (bf16[8,16,640]{2,1,0:T(8,128)(2,1)S(1)}, bf16[8,16,640]{2,1,0:T(8,128)(2,1)S(1)}, u32[]{:S(2)}, u32[]{:S(2)}) collective-permute-start(bf16[8,16,640]{2,1,0:T(8,128)(2,1)S(1)} %get-tuple-element.39.refs_0_), channel_id=1, source_target_pairs={{0,1},{1,0},{2,3},{3,2},{4,5},{5,4},{6,7},{7,6},{8,9},{9,8},{10,11... | collective-permute-start | bytes 491528 | tf_op jit(solution)/shard_map/ppermute | solution.py:243
  18.7 6.1 %collective-permute-start.5 = (bf16[8,16,640]{2,1,0:T(8,128)(2,1)S(1)}, bf16[8,16,640]{2,1,0:T(8,128)(2,1)S(1)}, u32[]{:S(2)}, u32[]{:S(2)}) collective-permute-start(bf16[8,16,640]{2,1,0:T(8,128)(2,1)S(1)} %collective-permute-done.4.refs_2_), channel_id=1, source_target_pairs={{0,1},{1,0},{2,3},{3,2},{4,5},{5,4},{6,7},{7,6},{8,9},{9,8},{10,11... | collective-permute-start | bytes 491528 | tf_op jit(solution)/shard_map/ppermute | solution.py:243
  19.3 1.2 %copy-start.2 = (bf16[16,210,128]{2,0,1:T(8,128)(2,1)S(1)}, bf16[16,210,128]{2,0,1:T(8,128)(2,1)}, u32[]{:S(2)}) copy-start(bf16[16,210,128]{2,0,1:T(8,128)(2,1)} %param.6) | copy-start | bytes 2580484
  20.4 0.7 copy-start.5
  21.1 0.7 copy-start.7
  24.3 4.8 %copy-start.6 = (s32[1,210]{1,0:T(1,128)S(1)}, s32[1,210]{1,0:T(1,128)}, u32[]{:S(2)}) copy-start(s32[1,210]{1,0:T(1,128)} %row_ref.11) | copy-start | bytes 2524
  24.3 4.8 %copy-start.8 = (s32[1,210]{1,0:T(1,128)S(1)}, s32[1,210]{1,0:T(1,128)}, u32[]{:S(2)}) copy-start(s32[1,210]{1,0:T(1,128)} %col_ref.11) | copy-start | bytes 2524
  25.2 3.9 %collective-permute-start.8 = (bf16[210,16,128]{2,1,0:T(8,128)(2,1)S(1)}, bf16[210,16,128]{2,1,0:T(8,128)(2,1)S(1)}, u32[]{:S(2)}, u32[]{:S(2)}) collective-permute-start(bf16[210,16,128]{2,1,0:T(8,128)(2,1)S(1)} %collective-permute-done.first_ref.own_ref), channel_id=1, source_target_pairs={{0,4},{4,0},{8,12},{12,8},{16,20},{20,16},{24,28},{28,24},{1,5},{5... | collective-permute-start | bytes 2580488 | tf_op jit(solution)/shard_map/ppermute | solution.py:236
  25.3 7.6 %collective-permute-start.9 = (bf16[210,16,128]{2,1,0:T(8,128)(2,1)S(1)}, bf16[210,16,128]{2,1,0:T(8,128)(2,1)S(1)}, u32[]{:S(2)}, u32[]{:S(2)}) collective-permute-start(bf16[210,16,128]{2,1,0:T(8,128)(2,1)S(1)} %collective-permute-done.1.second_ref.own_ref), channel_id=1, source_target_pairs={{0,4},{4,0},{8,12},{12,8},{16,20},{20,16},{24,28},{28,24},{1,5},{5... | collective-permute-start | bytes 2580488 | tf_op jit(solution)/shard_map/ppermute | solution.py:236
  25.8 11.9 %collective-permute-start.6 = (bf16[105,16,128]{2,1,0:T(8,128)(2,1)S(1)}, bf16[105,16,128]{2,1,0:T(8,128)(2,1)S(1)}, u32[]{:S(2)}, u32[]{:S(2)}) collective-permute-start(bf16[105,16,128]{2,1,0:T(8,128)(2,1)S(1)} %get-tuple-element.42), channel_id=1, source_target_pairs={{0,16},{4,20},{8,24},{12,28},{16,0},{20,4},{24,8},{28,12},{1,17},{... | collective-permute-start | bytes 1290248 | tf_op jit(solution)/shard_map/ppermute | solution.py:239
  26.1 11.6 %collective-permute-start.7 = (bf16[105,16,128]{2,1,0:T(8,128)(2,1)S(1)}, bf16[105,16,128]{2,1,0:T(8,128)(2,1)S(1)}, u32[]{:S(2)}, u32[]{:S(2)}) collective-permute-start(bf16[105,16,128]{2,1,0:T(8,128)(2,1)S(1)} %get-tuple-element.43), channel_id=1, source_target_pairs={{0,8},{4,12},{8,0},{12,4},{16,24},{20,28},{24,16},{28,20},{1,9},{5... | collective-permute-start | bytes 1290248 | tf_op jit(solution)/shard_map/ppermute | solution.py:239
  35.4 4.8 %copy-start.3 = (bf16[64,2688]{1,0:T(8,128)(2,1)S(1)}, bf16[64,2688]{1,0:T(8,128)(2,1)}, u32[]{:S(2)}) copy-start(bf16[64,2688]{1,0:T(8,128)(2,1)} %cotangent_ref.1) | copy-start | bytes 1032196
  37.7 2.5 %collective-permute-start.10 = (bf16[105,16,128]{2,1,0:T(8,128)(2,1)S(1)}, bf16[105,16,128]{2,1,0:T(8,128)(2,1)S(1)}, u32[]{:S(2)}, u32[]{:S(2)}) collective-permute-start(bf16[105,16,128]{2,1,0:T(8,128)(2,1)S(1)} %collective-permute-done.6.lower_ref), channel_id=1, source_target_pairs={{0,4},{4,0},{8,12},{12,8},{16,20},{20,16},{24,28},{28,24},{1,5},{5... | collective-permute-start | bytes 1290248 | tf_op jit(solution)/shard_map/ppermute | solution.py:236
  37.7 2.5 %collective-permute-start.11 = (bf16[105,16,128]{2,1,0:T(8,128)(2,1)S(1)}, bf16[105,16,128]{2,1,0:T(8,128)(2,1)S(1)}, u32[]{:S(2)}, u32[]{:S(2)}) collective-permute-start(bf16[105,16,128]{2,1,0:T(8,128)(2,1)S(1)} %collective-permute-done.7.upper_ref), channel_id=1, source_target_pairs={{0,4},{4,0},{8,12},{12,8},{16,20},{20,16},{24,28},{28,24},{1,5},{5... | collective-permute-start | bytes 1290248 | tf_op jit(solution)/shard_map/ppermute | solution.py:236
  43.4 15.4 %collective-permute-start.12 = (bf16[64,3968]{1,0:T(8,128)(2,1)S(1)}, bf16[64,3968]{1,0:T(8,128)(2,1)S(1)}, u32[]{:S(2)}, u32[]{:S(2)}) collective-permute-start(bf16[64,3968]{1,0:T(8,128)(2,1)S(1)} %get-tuple-element.63), channel_id=1, source_target_pairs={{0,8},{4,12},{8,0},{12,4},{16,24},{20,28},{24,16},{28,20},{1,9},{5... | collective-permute-start | bytes 1523720 | tf_op jit(solution)/shard_map/ppermute | solution.py:239
  45.2 24.8 %collective-permute-start.16 = (bf16[64,3968]{1,0:T(8,128)(2,1)S(1)}, bf16[64,3968]{1,0:T(8,128)(2,1)S(1)}, u32[]{:S(2)}, u32[]{:S(2)}) collective-permute-start(bf16[64,3968]{1,0:T(8,128)(2,1)S(1)} %get-tuple-element.69), channel_id=1, source_target_pairs={{0,16},{4,20},{8,24},{12,28},{16,0},{20,4},{24,8},{28,12},{1,17},{... | collective-permute-start | bytes 1523720 | tf_op jit(solution)/shard_map/ppermute | solution.py:239
  46.7 23.3 %collective-permute-start.17 = (bf16[64,3968]{1,0:T(8,128)(2,1)S(1)}, bf16[64,3968]{1,0:T(8,128)(2,1)S(1)}, u32[]{:S(2)}, u32[]{:S(2)}) collective-permute-start(bf16[64,3968]{1,0:T(8,128)(2,1)S(1)} %get-tuple-element.70), channel_id=1, source_target_pairs={{0,24},{4,28},{8,16},{12,20},{16,8},{20,12},{24,0},{28,4},{1,25},{... | collective-permute-start | bytes 1523720 | tf_op jit(solution)/shard_map/ppermute | solution.py:239
  50.8 23.0 %copy-start.1 = (bf16[1024,1024]{1,0:T(8,128)(2,1)S(1)}, bf16[1024,1024]{1,0:T(8,128)(2,1)}, u32[]{:S(2)}) copy-start(bf16[1024,1024]{1,0:T(8,128)(2,1)} %copy-done) | copy-start | bytes 6291460
  54.7 14.6 %collective-permute-start.14 = (bf16[4,16,1280]{2,1,0:T(8,128)(2,1)S(1)}, bf16[4,16,1280]{2,1,0:T(8,128)(2,1)S(1)}, u32[]{:S(2)}, u32[]{:S(2)}) collective-permute-start(bf16[4,16,1280]{2,1,0:T(8,128)(2,1)S(1)} %get-tuple-element.65), channel_id=1, source_target_pairs={{0,2},{1,3},{2,0},{3,1},{4,6},{5,7},{6,4},{7,5},{8,10},{9,11},{10,... | collective-permute-start | bytes 491528 | tf_op jit(solution)/shard_map/ppermute | solution.py:243
  58.0 11.3 %collective-permute-start.15 = (bf16[4,16,1280]{2,1,0:T(8,128)(2,1)S(1)}, bf16[4,16,1280]{2,1,0:T(8,128)(2,1)S(1)}, u32[]{:S(2)}, u32[]{:S(2)}) collective-permute-start(bf16[4,16,1280]{2,1,0:T(8,128)(2,1)S(1)} %get-tuple-element.66), channel_id=1, source_target_pairs={{0,3},{1,2},{2,1},{3,0},{4,7},{5,6},{6,5},{7,4},{8,11},{9,10},{10,... | collective-permute-start | bytes 491528 | tf_op jit(solution)/shard_map/ppermute | solution.py:243
  58.9 11.1 %collective-permute-start.13 = (bf16[4,16,1280]{2,1,0:T(8,128)(2,1)S(1)}, bf16[4,16,1280]{2,1,0:T(8,128)(2,1)S(1)}, u32[]{:S(2)}, u32[]{:S(2)}) collective-permute-start(bf16[4,16,1280]{2,1,0:T(8,128)(2,1)S(1)} %get-tuple-element.64), channel_id=1, source_target_pairs={{0,1},{1,0},{2,3},{3,2},{4,5},{5,4},{6,7},{7,6},{8,9},{9,8},{10,11... | collective-permute-start | bytes 491528 | tf_op jit(solution)/shard_map/ppermute | solution.py:243
  73.7 2.5 %collective-permute-start.18 = (bf16[210,16,128]{2,1,0:T(8,128)(2,1)S(1)}, bf16[210,16,128]{2,1,0:T(8,128)(2,1)S(1)}, u32[]{:S(2)}, u32[]{:S(2)}) collective-permute-start(bf16[210,16,128]{2,1,0:T(8,128)(2,1)S(1)} %get-tuple-element.72), channel_id=1, source_target_pairs={{0,4},{4,0},{8,12},{12,8},{16,20},{20,16},{24,28},{28,24},{1,5},{5... | collective-permute-start | bytes 2580488 | tf_op jit(solution)/shard_map/ppermute | solution.py:236

commit v5 on v4

--- a/solution.py
+++ b/solution.py
@@ -93,7 +93,7 @@
         out_ref[pl.ds(top, rows), pl.ds(left, width)] = tiles_ref[slot]
         return carry
 
-    lax.fori_loop(0, slots, place, 0, unroll=15)
+    lax.fori_loop(0, slots, place, 0, unroll=35)
 
 
 def weight_kernel(order_ref, row_ref, col_ref, own_ref, other_ref, w_ref):
@@ -200,7 +200,7 @@
         )
         return carry
 
-    lax.fori_loop(0, slots, place_tile, 0, unroll=15)
+    lax.fori_loop(0, slots, place_tile, 0, unroll=35)
 
 
 def params(limit):
@@ -305,7 +305,7 @@
             out_specs=spec(),
             compiler_params=params(10),
             cost_estimate=cost(0, 2 * depth * columns),
-        )(after(z_index, weights[0]))
+        )(after(z_index, token_parts[2]))
         tiles[1], tiles[2], blank, *_ = lax.optimization_barrier(
             (tiles[1], tiles[2], blank, *token_parts[1:], weights[0])
         )

time: 78.4 us -> 78.1 us (level)
  local copies, waits for them, and re-layouts: 4.8 us -> 2.29 us
  waiting for transfers between devices: 19 us -> 20.8 us
    unnamed x18 -> x14, local copies, waits for them, and re-layouts: 4.8 us -> 2.29 us
    ppermute x7, waiting for transfers between devices: 1.28 us -> 2.32 us  [to_chip(): return lax.ppermute(value, 'fsdp', [(f, f ^ 2 * step) for f in range(fsdp)])]
  transfers between devices with their start and end apart: 19 -> 19, of which waited for: 6 -> 7; matrix products, arithmetic and copies ran while one was open for 0% -> 0% of each run, Pallas kernels for 30% -> 31%
where the time goes in v5:
time: 78.1 us; the launch traced here: 76.9 us
  Pallas kernels  30.5 us (39%)
  starting transfers between devices  21 us (27%)
  waiting for transfers between devices  20.8 us (27%)
  local copies, waits for them, and re-layouts  2.29 us (3%)
  other arithmetic  1.36 us (2%)
  between operations  0.87 us (1%)
    ppermute x6, waiting for transfers between devices, to_z(): return lax.ppermute(value, 'tp', [(i, i ^ step) for i in range(n_tp)])  17.4 us
    ppermute x6, starting transfers between devices, to_z(): return lax.ppermute(value, 'tp', [(i, i ^ step) for i in range(n_tp)])  9.76 us
    ppermute x7, starting transfers between devices, to_chip(): return lax.ppermute(value, 'fsdp', [(f, f ^ 2 * step) for f in range(fsdp)])  9.57 us
    pallas_call x2, Pallas kernels, local(): pl.pallas_call(functools.partial(back_kernel, n_tp, first, 2), out_shape=...  7.7 us
    pallas_call x3, Pallas kernels, make_weight(): pl.pallas_call(weight_kernel, out_shape=jax.ShapeDtypeStruct((depth, colu...  7.69 us
    pallas_call x3, Pallas kernels, add_hidden(): pl.pallas_call(functools.partial(early_kernel, n_tp, step), out_shape=jax...  3.92 us
    pallas_call x1, Pallas kernels, local(): pl.pallas_call(functools.partial(tile_grad_kernel, chips, grad_scale), ou...  3.71 us
    pallas_call x1, Pallas kernels, local(): pl.pallas_call(functools.partial(hidden_kernel, n_tp, chips - 1, half), o...  3.14 us
  transfers between devices with their start and end apart: 19, of which 7 were waited for; matrix products, arithmetic and copies ran while one was open for 0% of the time, Pallas kernels for 31%

profile of v5, /device:TPU:0, one launch (start us, length us, event | category | flops | bytes accessed | tf_op | source)
XLA Modules:
  0.0 76.9 jit_solution(8762352614281150000)
XLA Ops:
  1.2 2.6 %collective-permute-start.1 = (bf16[210,16,128]{2,1,0:T(8,128)(2,1)}, bf16[210,16,128]{2,1,0:T(8,128)(2,1)S(1)}, u32[]{:S(2)}, u32[]{:S(2)}) collective-permute-start(bf16[210,16,128]{2,1,0:T(8,128)(2,1)} %bitcast.6), channel_id=1, source_target_pairs={{0,16},{4,20},{8,24},{12,28},{16,0},{20,4},{24,8},{28,12},{1,17},{... | collective-permute-start | bytes 2580488 | tf_op jit(solution)/shard_map/ppermute | solution.py:239
  3.8 1.5 %collective-permute-start = (bf16[210,16,128]{2,1,0:T(8,128)(2,1)}, bf16[210,16,128]{2,1,0:T(8,128)(2,1)S(1)}, u32[]{:S(2)}, u32[]{:S(2)}) collective-permute-start(bf16[210,16,128]{2,1,0:T(8,128)(2,1)} %bitcast.7), channel_id=1, source_target_pairs={{0,8},{4,12},{8,0},{12,4},{16,24},{20,28},{24,16},{28,20},{1,9},{5... | collective-permute-start | bytes 2580488 | tf_op jit(solution)/shard_map/ppermute | solution.py:239
  5.2 0.9 %copy-done.4 = bf16[16,5120]{1,0:T(8,128)(2,1)S(1)} copy-done((bf16[16,5120]{1,0:T(8,128)(2,1)S(1)}, bf16[16,5120]{1,0:T(8,128)(2,1)}, u32[]{:S(2)}) %copy-start.4) | copy-done | bytes 163864
  6.2 0.7 shard_map.76
  6.9 1.4 %copy-done = bf16[1024,1024]{1,0:T(8,128)(2,1)} copy-done((bf16[1024,1024]{1,0:T(8,128)(2,1)}, bf16[1024,1024]{1,0:T(8,128)(2,1)S(1)}, u32[]{:S(2)}) %copy-start) | copy-done | bytes 2097176
  8.2 2.6 %collective-permute-start.2 = (bf16[8,16,640]{2,1,0:T(8,128)(2,1)S(1)}, bf16[8,16,640]{2,1,0:T(8,128)(2,1)S(1)}, u32[]{:S(2)}, u32[]{:S(2)}) collective-permute-start(bf16[8,16,640]{2,1,0:T(8,128)(2,1)S(1)} %get-tuple-element.38.refs_0_), channel_id=1, source_target_pairs={{0,2},{1,3},{2,0},{3,1},{4,6},{5,7},{6,4},{7,5},{8,10},{9,11},{10,... | collective-permute-start | bytes 491528 | tf_op jit(solution)/shard_map/ppermute | solution.py:243
  10.8 1.6 %collective-permute-start.3 = (bf16[8,16,640]{2,1,0:T(8,128)(2,1)S(1)}, bf16[8,16,640]{2,1,0:T(8,128)(2,1)S(1)}, u32[]{:S(2)}, u32[]{:S(2)}) collective-permute-start(bf16[8,16,640]{2,1,0:T(8,128)(2,1)S(1)} %get-tuple-element.38.refs_0_), channel_id=1, source_target_pairs={{0,1},{1,0},{2,3},{3,2},{4,5},{5,4},{6,7},{7,6},{8,9},{9,8},{10,11... | collective-permute-start | bytes 491528 | tf_op jit(solution)/shard_map/ppermute | solution.py:243
  12.4 6.3 %collective-permute-done.2.refs_2_ = bf16[8,16,640]{2,1,0:T(8,128)(2,1)S(1)} collective-permute-done((bf16[8,16,640]{2,1,0:T(8,128)(2,1)S(1)}, bf16[8,16,640]{2,1,0:T(8,128)(2,1)S(1)}, u32[]{:S(2)}, u32[]{:S(2)}) %collective-permute-start.2) | collective-permute-done | bytes 163872 | tf_op jit(solution)/shard_map/ppermute | solution.py:243
  19.8 3.0 %shard_map.78.w_ref.refs_0_ = bf16[1280,2688]{1,0:T(8,128)(2,1)S(1)} custom-call(s32[1]{0:T(128)} %bitcast.order_ref.z_ref, s32[1,210]{1,0:T(1,128)S(1)} %copy-done.5, s32[1,210]{1,0:T(1,128)S(1)} %copy-done.6, bf16[210,16,128]{2,1,0:T(8,128)(2,1)S(1)} %bitcast.8, bf16[210,16,128]{2,1,0:T(8,128)(2,1)} %collective-permute-done.5.other_ref), custom_call_target="tpu_custom_call" | custom-call | bytes 3360 | tf_op jit(solution)/shard_map/pallas_call | solution.py:268
  22.8 1.3 %collective-permute-done.4.refs_3_ = bf16[8,16,640]{2,1,0:T(8,128)(2,1)S(1)} collective-permute-done((bf16[8,16,640]{2,1,0:T(8,128)(2,1)S(1)}, bf16[8,16,640]{2,1,0:T(8,128)(2,1)S(1)}, u32[]{:S(2)}, u32[]{:S(2)}) %collective-permute-start.4) | collective-permute-done | bytes 163872 | tf_op jit(solution)/shard_map/ppermute | solution.py:243
  24.0 1.1 %collective-permute-done.first_ref.own_ref = bf16[210,16,128]{2,1,0:T(8,128)(2,1)S(1)} collective-permute-done((bf16[210,16,128]{2,1,0:T(8,128)(2,1)}, bf16[210,16,128]{2,1,0:T(8,128)(2,1)S(1)}, u32[]{:S(2)}, u32[]{:S(2)}) %collective-permute-start) | collective-permute-done | bytes 860192 | tf_op jit(solution)/shard_map/ppermute | solution.py:239
  26.1 1.7 %collective-permute-start.7 = (bf16[105,16,128]{2,1,0:T(8,128)(2,1)S(1)}, bf16[105,16,128]{2,1,0:T(8,128)(2,1)S(1)}, u32[]{:S(2)}, u32[]{:S(2)}) collective-permute-start(bf16[105,16,128]{2,1,0:T(8,128)(2,1)S(1)} %get-tuple-element.43), channel_id=1, source_target_pairs={{0,8},{4,12},{8,0},{12,4},{16,24},{20,28},{24,16},{28,20},{1,9},{5... | collective-permute-start | bytes 1290248 | tf_op jit(solution)/shard_map/ppermute | solution.py:239
  27.8 1.3 %shard_map.82.refs_4_ = f32[64,2688]{1,0:T(8,128)S(1)} custom-call(bf16[1280,2688]{1,0:T(8,128)(2,1)S(1)} %shard_map.78.w_ref.refs_0_, bf16[8,16,640]{2,1,0:T(8,128)(2,1)S(1)} %get-tuple-element.38.refs_0_, bf16[8,16,640]{2,1,0:T(8,128)(2,1)S(1)} %collective-permute-done.3.refs_1_, bf16[8,16,640]{2,1,0:T(8,128)(2,1)S(1)} %collective-permute-done.2.refs_2_, ...), custom_call_target="tpu_custom_call" | custom-call | flops 107520 | bytes 1680 | tf_op jit(solution)/shard_map/pallas_call | solution.py:278
  29.1 2.4 %shard_map.80.w_ref.refs_1_ = bf16[1280,2688]{1,0:T(8,128)(2,1)S(1)} custom-call(s32[1]{0:T(128)} %bitcast.order_ref.z_ref, s32[1,210]{1,0:T(1,128)S(1)} %copy-done.5, s32[1,210]{1,0:T(1,128)S(1)} %copy-done.6, bf16[210,16,128]{2,1,0:T(8,128)(2,1)S(1)} %collective-permute-done.first_ref.own_ref, bf16[210,16,128]{2,1,0:T(8,128)(2,1)S(1)} %collective-permute-done.8.other_ref), custom_call_target="tpu_custom_call" | custom-call | bytes 3360 | tf_op jit(solution)/shard_map/pallas_call | solution.py:268
  31.5 1.3 %shard_map.83.refs_4_ = f32[64,2688]{1,0:T(8,128)S(1)} custom-call(bf16[1280,2688]{1,0:T(8,128)(2,1)S(1)} %shard_map.80.w_ref.refs_1_, bf16[8,16,640]{2,1,0:T(8,128)(2,1)S(1)} %get-tuple-element.38.refs_0_, bf16[8,16,640]{2,1,0:T(8,128)(2,1)S(1)} %collective-permute-done.3.refs_1_, bf16[8,16,640]{2,1,0:T(8,128)(2,1)S(1)} %collective-permute-done.2.refs_2_, ...), custom_call_target="tpu_custom_call" | custom-call | flops 107520 | bytes 1680 | tf_op jit(solution)/shard_map/pallas_call | solution.py:278
  32.8 2.4 %shard_map.81.w_ref.refs_0_ = bf16[1280,2688]{1,0:T(8,128)(2,1)S(1)} custom-call(s32[1]{0:T(128)} %bitcast.order_ref.z_ref, s32[1,210]{1,0:T(1,128)S(1)} %copy-done.5, s32[1,210]{1,0:T(1,128)S(1)} %copy-done.6, bf16[210,16,128]{2,1,0:T(8,128)(2,1)S(1)} %collective-permute-done.1.second_ref.own_ref, bf16[210,16,128]{2,1,0:T(8,128)(2,1)S(1)} %collective-permute-done.9.other_ref), custom_call_target="tpu_custom_call" | custom-call | bytes 3360 | tf_op jit(solution)/shard_map/pallas_call | solution.py:268
  35.2 1.3 %shard_map.84.early_ref = f32[64,2688]{1,0:T(8,128)S(1)} custom-call(bf16[1280,2688]{1,0:T(8,128)(2,1)S(1)} %shard_map.81.w_ref.refs_0_, bf16[8,16,640]{2,1,0:T(8,128)(2,1)S(1)} %get-tuple-element.38.refs_0_, bf16[8,16,640]{2,1,0:T(8,128)(2,1)S(1)} %collective-permute-done.3.refs_1_, bf16[8,16,640]{2,1,0:T(8,128)(2,1)S(1)} %collective-permute-done.2.refs_2_, ...), custom_call_target="tpu_custom_call" | custom-call | flops 107520 | bytes 1680 | tf_op jit(solution)/shard_map/pallas_call | solution.py:278
  36.5 1.2 %collective-permute-done.6.lower_ref = bf16[105,16,128]{2,1,0:T(8,128)(2,1)S(1)} collective-permute-done((bf16[105,16,128]{2,1,0:T(8,128)(2,1)S(1)}, bf16[105,16,128]{2,1,0:T(8,128)(2,1)S(1)}, u32[]{:S(2)}, u32[]{:S(2)}) %collective-permute-start.6) | collective-permute-done | bytes 430112 | tf_op jit(solution)/shard_map/ppermute | solution.py:239
  38.2 2.0 %shard_map.85 = (bf16[1280,2688]{1,0:T(8,128)(2,1)S(1)}, f32[64,2688]{1,0:T(8,128)S(1)}) custom-call(s32[1]{0:T(128)} %bitcast.order_ref.z_ref, s32[1,210]{1,0:T(1,128)S(1)} %copy-done.5, s32[1,210]{1,0:T(1,128)S(1)} %copy-done.6, bf16[105,16,128]{2,1,0:T(8,128)(2,1)S(1)} %collective-permute-done.6.lower_ref, ...), custom_call_target="tpu_custom_call", output_to_operand_aliasing={{0}: (5, {}), {1}: (6, {})} | custom-call | flops 53760 | bytes 1680 | tf_op jit(solution)/shard_map/pallas_call | solution.py:344
  40.2 3.1 %shard_map.86 = (bf16[1280,2688]{1,0:T(8,128)(2,1)S(1)}, bf16[64,2688]{1,0:T(8,128)(2,1)}, bf16[64,2688]{1,0:T(8,128)(2,1)S(1)}, bf16[64,3968]{1,0:T(8,128)(2,1)...) custom-call(s32[1]{0:T(128)} %bitcast.order_ref.z_ref, ...), custom_call_target="tpu_custom_call", output_to_operand_aliasing={{0}: (8, {})} | custom-call | flops 107520 | bytes 1680 | tf_op jit(solution)/shard_map/pallas_call | solution.py:356
  43.3 1.7 %collective-permute-start.12 = (bf16[64,3968]{1,0:T(8,128)(2,1)S(1)}, bf16[64,3968]{1,0:T(8,128)(2,1)S(1)}, u32[]{:S(2)}, u32[]{:S(2)}) collective-permute-start(bf16[64,3968]{1,0:T(8,128)(2,1)S(1)} %get-tuple-element.63), channel_id=1, source_target_pairs={{0,8},{4,12},{8,0},{12,4},{16,24},{20,28},{24,16},{28,20},{1,9},{5... | collective-permute-start | bytes 1523720 | tf_op jit(solution)/shard_map/ppermute | solution.py:239
  45.0 1.5 %collective-permute-start.16 = (bf16[64,3968]{1,0:T(8,128)(2,1)S(1)}, bf16[64,3968]{1,0:T(8,128)(2,1)S(1)}, u32[]{:S(2)}, u32[]{:S(2)}) collective-permute-start(bf16[64,3968]{1,0:T(8,128)(2,1)S(1)} %get-tuple-element.69), channel_id=1, source_target_pairs={{0,16},{4,20},{8,24},{12,28},{16,0},{20,4},{24,8},{28,12},{1,17},{... | collective-permute-start | bytes 1523720 | tf_op jit(solution)/shard_map/ppermute | solution.py:239
  46.8 3.8 %shard_map.87 = (f32[4,16,1280]{2,1,0:T(8,128)S(1)}, bf16[4,16,1280]{2,1,0:T(8,128)(2,1)S(1)}, bf16[4,16,1280]{2,1,0:T(8,128)(2,1)S(1)}, bf16[4,16,1280]{2,1,0:T(8,128)(2,1)S(1)}) custom-call(bf16[64,2688]{1,0:T(8,128)(2,1)S(1)} %get-tuple-element.55.g_ref, bf16[1280,2688]{1,0:T(8,128)(2,1)S(1)} %shard_map.78.w_ref.refs_0_, ...), custom_call_target="tpu_custom_call" | custom-call | flops 215040 | bytes 3360 | tf_op jit(solution)/shard_map/pallas_call | solution.py:407
  50.7 3.8 %shard_map.88 = (f32[4,16,1280]{2,1,0:T(8,128)S(1)}, bf16[4,16,1280]{2,1,0:T(8,128)(2,1)S(1)}, bf16[4,16,1280]{2,1,0:T(8,128)(2,1)S(1)}, bf16[4,16,1280]{2,1,0:T(8,128)(2,1)S(1)}) custom-call(bf16[64,2688]{1,0:T(8,128)(2,1)S(1)} %get-tuple-element.55.g_ref, ...), custom_call_target="tpu_custom_call", output_to_operand_aliasing={{0}: (3, {}), {1}: (4, {}), {2}: (5, {}), {3}: (6, {})} | custom-call | flops 215040 | bytes 3360 | tf_op jit(solution)/shard_map/pallas_call | solution.py:407
  54.5 2.9 %collective-permute-start.14 = (bf16[4,16,1280]{2,1,0:T(8,128)(2,1)S(1)}, bf16[4,16,1280]{2,1,0:T(8,128)(2,1)S(1)}, u32[]{:S(2)}, u32[]{:S(2)}) collective-permute-start(bf16[4,16,1280]{2,1,0:T(8,128)(2,1)S(1)} %get-tuple-element.65), channel_id=1, source_target_pairs={{0,2},{1,3},{2,0},{3,1},{4,6},{5,7},{6,4},{7,5},{8,10},{9,11},{10,... | collective-permute-start | bytes 491528 | tf_op jit(solution)/shard_map/ppermute | solution.py:243
  57.4 1.4 %collective-permute-start.15 = (bf16[4,16,1280]{2,1,0:T(8,128)(2,1)S(1)}, bf16[4,16,1280]{2,1,0:T(8,128)(2,1)S(1)}, u32[]{:S(2)}, u32[]{:S(2)}) collective-permute-start(bf16[4,16,1280]{2,1,0:T(8,128)(2,1)S(1)} %get-tuple-element.66), channel_id=1, source_target_pairs={{0,3},{1,2},{2,1},{3,0},{4,7},{5,6},{6,5},{7,4},{8,11},{9,10},{10,... | collective-permute-start | bytes 491528 | tf_op jit(solution)/shard_map/ppermute | solution.py:243
  58.8 0.8 %collective-permute-start.13 = (bf16[4,16,1280]{2,1,0:T(8,128)(2,1)S(1)}, bf16[4,16,1280]{2,1,0:T(8,128)(2,1)S(1)}, u32[]{:S(2)}, u32[]{:S(2)}) collective-permute-start(bf16[4,16,1280]{2,1,0:T(8,128)(2,1)S(1)} %get-tuple-element.64), channel_id=1, source_target_pairs={{0,1},{1,0},{2,3},{3,2},{4,5},{5,4},{6,7},{7,6},{8,9},{9,8},{10,11... | collective-permute-start | bytes 491528 | tf_op jit(solution)/shard_map/ppermute | solution.py:243
  59.6 9.6 %collective-permute-done.14.refs_2_ = bf16[4,16,1280]{2,1,0:T(8,128)(2,1)S(1)} collective-permute-done((bf16[4,16,1280]{2,1,0:T(8,128)(2,1)S(1)}, bf16[4,16,1280]{2,1,0:T(8,128)(2,1)S(1)}, u32[]{:S(2)}, u32[]{:S(2)}) %collective-permute-start.14) | collective-permute-done | bytes 163872 | tf_op jit(solution)/shard_map/ppermute | solution.py:243
  69.4 3.7 %shard_map.90 = (f32[210,16,128]{2,1,0:T(8,128)S(1)}, bf16[210,16,128]{2,1,0:T(8,128)(2,1)S(1)}) custom-call(s32[1]{0:T(128)} %bitcast.order_ref.z_ref, s32[1,210]{1,0:T(1,128)S(1)} %copy-done.5, s32[1,210]{1,0:T(1,128)S(1)} %copy-done.6, bf16[64,3968]{1,0:T(8,128)(2,1)S(1)} %get-tuple-element.68.refs_0_, ...), custom_call_target="tpu_custom_call" | custom-call | flops 430080 | bytes 3360 | tf_op jit(solution)/shard_map/pallas_call | solution.py:423
  73.2 1.2 %shard_map.89 = bf16[16,5120]{1,0:T(8,128)(2,1)} custom-call(s32[1]{0:T(128)} %bitcast.2.place_ref, bf16[1024,1024]{1,0:T(8,128)(2,1)S(1)} %copy-done.1, f32[4,16,1280]{2,1,0:T(8,128)S(1)} %get-tuple-element.61.refs_0_, bf16[4,16,1280]{2,1,0:T(8,128)(2,1)S(1)} %collective-permute-done.13.refs_1_, bf16[4,16,1280]{2,1,0:T(8,128)(2,1)S(1)} %collective-permute-done.14.refs_2_, ...), custom_call_target="tpu_custom_call" | custom-call | tf_op jit(solution)/shard_map/pallas_call | solution.py:436
  74.4 1.1 %collective-permute-done.18 = bf16[210,16,128]{2,1,0:T(8,128)(2,1)S(1)} collective-permute-done((bf16[210,16,128]{2,1,0:T(8,128)(2,1)S(1)}, bf16[210,16,128]{2,1,0:T(8,128)(2,1)S(1)}, u32[]{:S(2)}, u32[]{:S(2)}) %collective-permute-start.18) | collective-permute-done | bytes 860192 | tf_op jit(solution)/shard_map/ppermute | solution.py:236
  75.5 1.4 %add_bitcast_fusion = f32[16,210,128]{2,0,1:T(8,128)} fusion(f32[210,16,128]{2,1,0:T(8,128)S(1)} %get-tuple-element.71, bf16[210,16,128]{2,1,0:T(8,128)(2,1)S(1)} %collective-permute-done.18), kind=kLoop, calls=%fused_computation | loop fusion | flops 860160 | bytes 4300800 | tf_op jit(solution)/shard_map/transpose | solution.py:469
  (36 shorter events, 3.5 us)
Async XLA Ops:
  0.6 19.1 %copy-start.2 = (bf16[16,210,128]{2,0,1:T(8,128)(2,1)S(1)}, bf16[16,210,128]{2,0,1:T(8,128)(2,1)}, u32[]{:S(2)}) copy-start(bf16[16,210,128]{2,0,1:T(8,128)(2,1)} %param.6) | copy-start | bytes 2580484
  0.6 19.1 %collective-permute-start.5 = (bf16[210,16,128]{2,1,0:T(8,128)(2,1)}, bf16[210,16,128]{2,1,0:T(8,128)(2,1)}, u32[]{:S(2)}, u32[]{:S(2)}) collective-permute-start(bf16[210,16,128]{2,1,0:T(8,128)(2,1)} %bitcast.5), channel_id=1, source_target_pairs={{0,4},{4,0},{8,12},{12,8},{16,20},{20,16},{24,28},{28,24},{1,5},{5... | collective-permute-start | bytes 2580488 | tf_op jit(solution)/shard_map/ppermute | solution.py:236
  1.2 22.9 %collective-permute-start.1 = (bf16[210,16,128]{2,1,0:T(8,128)(2,1)}, bf16[210,16,128]{2,1,0:T(8,128)(2,1)S(1)}, u32[]{:S(2)}, u32[]{:S(2)}) collective-permute-start(bf16[210,16,128]{2,1,0:T(8,128)(2,1)} %bitcast.6), channel_id=1, source_target_pairs={{0,16},{4,20},{8,24},{12,28},{16,0},{20,4},{24,8},{28,12},{1,17},{... | collective-permute-start | bytes 2580488 | tf_op jit(solution)/shard_map/ppermute | solution.py:239
  3.8 21.4 %collective-permute-start = (bf16[210,16,128]{2,1,0:T(8,128)(2,1)}, bf16[210,16,128]{2,1,0:T(8,128)(2,1)S(1)}, u32[]{:S(2)}, u32[]{:S(2)}) collective-permute-start(bf16[210,16,128]{2,1,0:T(8,128)(2,1)} %bitcast.7), channel_id=1, source_target_pairs={{0,8},{4,12},{8,0},{12,4},{16,24},{20,28},{24,16},{28,20},{1,9},{5... | collective-permute-start | bytes 2580488 | tf_op jit(solution)/shard_map/ppermute | solution.py:239
  5.2 0.9 %copy-start.4 = (bf16[16,5120]{1,0:T(8,128)(2,1)S(1)}, bf16[16,5120]{1,0:T(8,128)(2,1)}, u32[]{:S(2)}) copy-start(bf16[16,5120]{1,0:T(8,128)(2,1)} %tokens_ref.1) | copy-start | bytes 491524
  6.2 13.6 %copy-start.5 = (s32[1,210]{1,0:T(1,128)S(1)}, s32[1,210]{1,0:T(1,128)}, u32[]{:S(2)}) copy-start(s32[1,210]{1,0:T(1,128)} %row_ref.11) | copy-start | bytes 2524
  6.2 13.6 %copy-start.6 = (s32[1,210]{1,0:T(1,128)S(1)}, s32[1,210]{1,0:T(1,128)}, u32[]{:S(2)}) copy-start(s32[1,210]{1,0:T(1,128)} %col_ref.11) | copy-start | bytes 2524
  6.8 1.4 %copy-start = (bf16[1024,1024]{1,0:T(8,128)(2,1)}, bf16[1024,1024]{1,0:T(8,128)(2,1)S(1)}, u32[]{:S(2)}) copy-start(bf16[1024,1024]{1,0:T(8,128)(2,1)S(1)} %get-tuple-element.54.onehot_ref) | copy-start | bytes 6291460
  8.2 10.5 %collective-permute-start.2 = (bf16[8,16,640]{2,1,0:T(8,128)(2,1)S(1)}, bf16[8,16,640]{2,1,0:T(8,128)(2,1)S(1)}, u32[]{:S(2)}, u32[]{:S(2)}) collective-permute-start(bf16[8,16,640]{2,1,0:T(8,128)(2,1)S(1)} %get-tuple-element.38.refs_0_), channel_id=1, source_target_pairs={{0,2},{1,3},{2,0},{3,1},{4,6},{5,7},{6,4},{7,5},{8,10},{9,11},{10,... | collective-permute-start | bytes 491528 | tf_op jit(solution)/shard_map/ppermute | solution.py:243
  10.8 12.0 %collective-permute-start.3 = (bf16[8,16,640]{2,1,0:T(8,128)(2,1)S(1)}, bf16[8,16,640]{2,1,0:T(8,128)(2,1)S(1)}, u32[]{:S(2)}, u32[]{:S(2)}) collective-permute-start(bf16[8,16,640]{2,1,0:T(8,128)(2,1)S(1)} %get-tuple-element.38.refs_0_), channel_id=1, source_target_pairs={{0,1},{1,0},{2,3},{3,2},{4,5},{5,4},{6,7},{7,6},{8,9},{9,8},{10,11... | collective-permute-start | bytes 491528 | tf_op jit(solution)/shard_map/ppermute | solution.py:243
  18.7 5.3 %collective-permute-start.4 = (bf16[8,16,640]{2,1,0:T(8,128)(2,1)S(1)}, bf16[8,16,640]{2,1,0:T(8,128)(2,1)S(1)}, u32[]{:S(2)}, u32[]{:S(2)}) collective-permute-start(bf16[8,16,640]{2,1,0:T(8,128)(2,1)S(1)} %collective-permute-done.2.refs_2_), channel_id=1, source_target_pairs={{0,1},{1,0},{2,3},{3,2},{4,5},{5,4},{6,7},{7,6},{8,9},{9,8},{10,11... | collective-permute-start | bytes 491528 | tf_op jit(solution)/shard_map/ppermute | solution.py:243
  25.2 3.9 %collective-permute-start.8 = (bf16[210,16,128]{2,1,0:T(8,128)(2,1)S(1)}, bf16[210,16,128]{2,1,0:T(8,128)(2,1)S(1)}, u32[]{:S(2)}, u32[]{:S(2)}) collective-permute-start(bf16[210,16,128]{2,1,0:T(8,128)(2,1)S(1)} %collective-permute-done.first_ref.own_ref), channel_id=1, source_target_pairs={{0,4},{4,0},{8,12},{12,8},{16,20},{20,16},{24,28},{28,24},{1,5},{5... | collective-permute-start | bytes 2580488 | tf_op jit(solution)/shard_map/ppermute | solution.py:236
  25.3 7.5 %collective-permute-start.9 = (bf16[210,16,128]{2,1,0:T(8,128)(2,1)S(1)}, bf16[210,16,128]{2,1,0:T(8,128)(2,1)S(1)}, u32[]{:S(2)}, u32[]{:S(2)}) collective-permute-start(bf16[210,16,128]{2,1,0:T(8,128)(2,1)S(1)} %collective-permute-done.1.second_ref.own_ref), channel_id=1, source_target_pairs={{0,4},{4,0},{8,12},{12,8},{16,20},{20,16},{24,28},{28,24},{1,5},{5... | collective-permute-start | bytes 2580488 | tf_op jit(solution)/shard_map/ppermute | solution.py:236
  25.8 11.9 %collective-permute-start.6 = (bf16[105,16,128]{2,1,0:T(8,128)(2,1)S(1)}, bf16[105,16,128]{2,1,0:T(8,128)(2,1)S(1)}, u32[]{:S(2)}, u32[]{:S(2)}) collective-permute-start(bf16[105,16,128]{2,1,0:T(8,128)(2,1)S(1)} %get-tuple-element.42), channel_id=1, source_target_pairs={{0,16},{4,20},{8,24},{12,28},{16,0},{20,4},{24,8},{28,12},{1,17},{... | collective-permute-start | bytes 1290248 | tf_op jit(solution)/shard_map/ppermute | solution.py:239
  26.1 11.6 %collective-permute-start.7 = (bf16[105,16,128]{2,1,0:T(8,128)(2,1)S(1)}, bf16[105,16,128]{2,1,0:T(8,128)(2,1)S(1)}, u32[]{:S(2)}, u32[]{:S(2)}) collective-permute-start(bf16[105,16,128]{2,1,0:T(8,128)(2,1)S(1)} %get-tuple-element.43), channel_id=1, source_target_pairs={{0,8},{4,12},{8,0},{12,4},{16,24},{20,28},{24,16},{28,20},{1,9},{5... | collective-permute-start | bytes 1290248 | tf_op jit(solution)/shard_map/ppermute | solution.py:239
  35.2 5.0 %copy-start.3 = (bf16[64,2688]{1,0:T(8,128)(2,1)S(1)}, bf16[64,2688]{1,0:T(8,128)(2,1)}, u32[]{:S(2)}) copy-start(bf16[64,2688]{1,0:T(8,128)(2,1)} %cotangent_ref.1) | copy-start | bytes 1032196
  37.7 2.5 %collective-permute-start.10 = (bf16[105,16,128]{2,1,0:T(8,128)(2,1)S(1)}, bf16[105,16,128]{2,1,0:T(8,128)(2,1)S(1)}, u32[]{:S(2)}, u32[]{:S(2)}) collective-permute-start(bf16[105,16,128]{2,1,0:T(8,128)(2,1)S(1)} %collective-permute-done.6.lower_ref), channel_id=1, source_target_pairs={{0,4},{4,0},{8,12},{12,8},{16,20},{20,16},{24,28},{28,24},{1,5},{5... | collective-permute-start | bytes 1290248 | tf_op jit(solution)/shard_map/ppermute | solution.py:236
  37.7 2.5 %collective-permute-start.11 = (bf16[105,16,128]{2,1,0:T(8,128)(2,1)S(1)}, bf16[105,16,128]{2,1,0:T(8,128)(2,1)S(1)}, u32[]{:S(2)}, u32[]{:S(2)}) collective-permute-start(bf16[105,16,128]{2,1,0:T(8,128)(2,1)S(1)} %collective-permute-done.7.upper_ref), channel_id=1, source_target_pairs={{0,4},{4,0},{8,12},{12,8},{16,20},{20,16},{24,28},{28,24},{1,5},{5... | collective-permute-start | bytes 1290248 | tf_op jit(solution)/shard_map/ppermute | solution.py:236
  43.3 15.4 %collective-permute-start.12 = (bf16[64,3968]{1,0:T(8,128)(2,1)S(1)}, bf16[64,3968]{1,0:T(8,128)(2,1)S(1)}, u32[]{:S(2)}, u32[]{:S(2)}) collective-permute-start(bf16[64,3968]{1,0:T(8,128)(2,1)S(1)} %get-tuple-element.63), channel_id=1, source_target_pairs={{0,8},{4,12},{8,0},{12,4},{16,24},{20,28},{24,16},{28,20},{1,9},{5... | collective-permute-start | bytes 1523720 | tf_op jit(solution)/shard_map/ppermute | solution.py:239
  45.0 24.3 %collective-permute-start.16 = (bf16[64,3968]{1,0:T(8,128)(2,1)S(1)}, bf16[64,3968]{1,0:T(8,128)(2,1)S(1)}, u32[]{:S(2)}, u32[]{:S(2)}) collective-permute-start(bf16[64,3968]{1,0:T(8,128)(2,1)S(1)} %get-tuple-element.69), channel_id=1, source_target_pairs={{0,16},{4,20},{8,24},{12,28},{16,0},{20,4},{24,8},{28,12},{1,17},{... | collective-permute-start | bytes 1523720 | tf_op jit(solution)/shard_map/ppermute | solution.py:239
  46.6 22.8 %collective-permute-start.17 = (bf16[64,3968]{1,0:T(8,128)(2,1)S(1)}, bf16[64,3968]{1,0:T(8,128)(2,1)S(1)}, u32[]{:S(2)}, u32[]{:S(2)}) collective-permute-start(bf16[64,3968]{1,0:T(8,128)(2,1)S(1)} %get-tuple-element.70), channel_id=1, source_target_pairs={{0,24},{4,28},{8,16},{12,20},{16,8},{20,12},{24,0},{28,4},{1,25},{... | collective-permute-start | bytes 1523720 | tf_op jit(solution)/shard_map/ppermute | solution.py:239
  50.7 22.5 %copy-start.1 = (bf16[1024,1024]{1,0:T(8,128)(2,1)S(1)}, bf16[1024,1024]{1,0:T(8,128)(2,1)}, u32[]{:S(2)}) copy-start(bf16[1024,1024]{1,0:T(8,128)(2,1)} %copy-done) | copy-start | bytes 6291460
  54.5 14.7 %collective-permute-start.14 = (bf16[4,16,1280]{2,1,0:T(8,128)(2,1)S(1)}, bf16[4,16,1280]{2,1,0:T(8,128)(2,1)S(1)}, u32[]{:S(2)}, u32[]{:S(2)}) collective-permute-start(bf16[4,16,1280]{2,1,0:T(8,128)(2,1)S(1)} %get-tuple-element.65), channel_id=1, source_target_pairs={{0,2},{1,3},{2,0},{3,1},{4,6},{5,7},{6,4},{7,5},{8,10},{9,11},{10,... | collective-permute-start | bytes 491528 | tf_op jit(solution)/shard_map/ppermute | solution.py:243
  57.4 11.8 %collective-permute-start.15 = (bf16[4,16,1280]{2,1,0:T(8,128)(2,1)S(1)}, bf16[4,16,1280]{2,1,0:T(8,128)(2,1)S(1)}, u32[]{:S(2)}, u32[]{:S(2)}) collective-permute-start(bf16[4,16,1280]{2,1,0:T(8,128)(2,1)S(1)} %get-tuple-element.66), channel_id=1, source_target_pairs={{0,3},{1,2},{2,1},{3,0},{4,7},{5,6},{6,5},{7,4},{8,11},{9,10},{10,... | collective-permute-start | bytes 491528 | tf_op jit(solution)/shard_map/ppermute | solution.py:243
  58.8 10.6 %collective-permute-start.13 = (bf16[4,16,1280]{2,1,0:T(8,128)(2,1)S(1)}, bf16[4,16,1280]{2,1,0:T(8,128)(2,1)S(1)}, u32[]{:S(2)}, u32[]{:S(2)}) collective-permute-start(bf16[4,16,1280]{2,1,0:T(8,128)(2,1)S(1)} %get-tuple-element.64), channel_id=1, source_target_pairs={{0,1},{1,0},{2,3},{3,2},{4,5},{5,4},{6,7},{7,6},{8,9},{9,8},{10,11... | collective-permute-start | bytes 491528 | tf_op jit(solution)/shard_map/ppermute | solution.py:243
  73.1 2.5 %collective-permute-start.18 = (bf16[210,16,128]{2,1,0:T(8,128)(2,1)S(1)}, bf16[210,16,128]{2,1,0:T(8,128)(2,1)S(1)}, u32[]{:S(2)}, u32[]{:S(2)}) collective-permute-start(bf16[210,16,128]{2,1,0:T(8,128)(2,1)S(1)} %get-tuple-element.72), channel_id=1, source_target_pairs={{0,4},{4,0},{8,12},{12,8},{16,20},{20,16},{24,28},{28,24},{1,5},{5... | collective-permute-start | bytes 2580488 | tf_op jit(solution)/shard_map/ppermute | solution.py:236

commit v6 on v5

--- a/solution.py
+++ b/solution.py
@@ -163,7 +163,7 @@
         pack_ref[:, w_ref.shape[1] :] = slice_rows(x_refs, chip)
 
 
-def column_blocks(columns, block=512):
+def column_blocks(columns, block=896):
     return [(left, min(left + block, columns)) for left in range(0, columns, block)]
 
 

time: 78.1 us -> 78.2 us (level)
  no operation moved by 1% of the time
where the time goes in v6:
time: 78.2 us; the launch traced here: 77 us
  Pallas kernels  30.7 us (39%)
  starting transfers between devices  21 us (27%)
  waiting for transfers between devices  20.9 us (27%)
  local copies, waits for them, and re-layouts  2.29 us (3%)
  other arithmetic  1.36 us (2%)
  between operations  0.87 us (1%)
    ppermute x6, waiting for transfers between devices, to_z(): return lax.ppermute(value, 'tp', [(i, i ^ step) for i in range(n_tp)])  17.4 us
    ppermute x6, starting transfers between devices, to_z(): return lax.ppermute(value, 'tp', [(i, i ^ step) for i in range(n_tp)])  9.76 us
    ppermute x7, starting transfers between devices, to_chip(): return lax.ppermute(value, 'fsdp', [(f, f ^ 2 * step) for f in range(fsdp)])  9.57 us
    pallas_call x2, Pallas kernels, local(): pl.pallas_call(functools.partial(back_kernel, n_tp, first, 2), out_shape=...  7.69 us
    pallas_call x3, Pallas kernels, make_weight(): pl.pallas_call(weight_kernel, out_shape=jax.ShapeDtypeStruct((depth, colu...  7.69 us
    pallas_call x3, Pallas kernels, add_hidden(): pl.pallas_call(functools.partial(early_kernel, n_tp, step), out_shape=jax...  3.92 us
    pallas_call x1, Pallas kernels, local(): pl.pallas_call(functools.partial(tile_grad_kernel, chips, grad_scale), ou...  3.88 us
    pallas_call x1, Pallas kernels, local(): pl.pallas_call(functools.partial(hidden_kernel, n_tp, chips - 1, half), o...  3.09 us
  transfers between devices with their start and end apart: 19, of which 7 were waited for; matrix products, arithmetic and copies ran while one was open for 0% of the time, Pallas kernels for 31%

profile of v6, /device:TPU:0, one launch (start us, length us, event | category | flops | bytes accessed | tf_op | source)
XLA Modules:
  0.0 77.0 jit_solution(6729521839390598965)
XLA Ops:
  1.2 2.6 %collective-permute-start.1 = (bf16[210,16,128]{2,1,0:T(8,128)(2,1)}, bf16[210,16,128]{2,1,0:T(8,128)(2,1)S(1)}, u32[]{:S(2)}, u32[]{:S(2)}) collective-permute-start(bf16[210,16,128]{2,1,0:T(8,128)(2,1)} %bitcast.6), channel_id=1, source_target_pairs={{0,16},{4,20},{8,24},{12,28},{16,0},{20,4},{24,8},{28,12},{1,17},{... | collective-permute-start | bytes 2580488 | tf_op jit(solution)/shard_map/ppermute | solution.py:239
  3.8 1.5 %collective-permute-start = (bf16[210,16,128]{2,1,0:T(8,128)(2,1)}, bf16[210,16,128]{2,1,0:T(8,128)(2,1)S(1)}, u32[]{:S(2)}, u32[]{:S(2)}) collective-permute-start(bf16[210,16,128]{2,1,0:T(8,128)(2,1)} %bitcast.7), channel_id=1, source_target_pairs={{0,8},{4,12},{8,0},{12,4},{16,24},{20,28},{24,16},{28,20},{1,9},{5... | collective-permute-start | bytes 2580488 | tf_op jit(solution)/shard_map/ppermute | solution.py:239
  5.2 0.9 %copy-done.4 = bf16[16,5120]{1,0:T(8,128)(2,1)S(1)} copy-done((bf16[16,5120]{1,0:T(8,128)(2,1)S(1)}, bf16[16,5120]{1,0:T(8,128)(2,1)}, u32[]{:S(2)}) %copy-start.4) | copy-done | bytes 163864
  6.2 0.7 shard_map.76
  6.9 1.4 %copy-done = bf16[1024,1024]{1,0:T(8,128)(2,1)} copy-done((bf16[1024,1024]{1,0:T(8,128)(2,1)}, bf16[1024,1024]{1,0:T(8,128)(2,1)S(1)}, u32[]{:S(2)}) %copy-start) | copy-done | bytes 2097176
  8.2 2.6 %collective-permute-start.2 = (bf16[8,16,640]{2,1,0:T(8,128)(2,1)S(1)}, bf16[8,16,640]{2,1,0:T(8,128)(2,1)S(1)}, u32[]{:S(2)}, u32[]{:S(2)}) collective-permute-start(bf16[8,16,640]{2,1,0:T(8,128)(2,1)S(1)} %get-tuple-element.38.refs_0_), channel_id=1, source_target_pairs={{0,2},{1,3},{2,0},{3,1},{4,6},{5,7},{6,4},{7,5},{8,10},{9,11},{10,... | collective-permute-start | bytes 491528 | tf_op jit(solution)/shard_map/ppermute | solution.py:243
  10.8 1.6 %collective-permute-start.3 = (bf16[8,16,640]{2,1,0:T(8,128)(2,1)S(1)}, bf16[8,16,640]{2,1,0:T(8,128)(2,1)S(1)}, u32[]{:S(2)}, u32[]{:S(2)}) collective-permute-start(bf16[8,16,640]{2,1,0:T(8,128)(2,1)S(1)} %get-tuple-element.38.refs_0_), channel_id=1, source_target_pairs={{0,1},{1,0},{2,3},{3,2},{4,5},{5,4},{6,7},{7,6},{8,9},{9,8},{10,11... | collective-permute-start | bytes 491528 | tf_op jit(solution)/shard_map/ppermute | solution.py:243
  12.4 6.3 %collective-permute-done.2.refs_2_ = bf16[8,16,640]{2,1,0:T(8,128)(2,1)S(1)} collective-permute-done((bf16[8,16,640]{2,1,0:T(8,128)(2,1)S(1)}, bf16[8,16,640]{2,1,0:T(8,128)(2,1)S(1)}, u32[]{:S(2)}, u32[]{:S(2)}) %collective-permute-start.2) | collective-permute-done | bytes 163872 | tf_op jit(solution)/shard_map/ppermute | solution.py:243
  19.8 3.0 %shard_map.78.w_ref.refs_0_ = bf16[1280,2688]{1,0:T(8,128)(2,1)S(1)} custom-call(s32[1]{0:T(128)} %bitcast.order_ref.z_ref, s32[1,210]{1,0:T(1,128)S(1)} %copy-done.5, s32[1,210]{1,0:T(1,128)S(1)} %copy-done.6, bf16[210,16,128]{2,1,0:T(8,128)(2,1)S(1)} %bitcast.8, bf16[210,16,128]{2,1,0:T(8,128)(2,1)} %collective-permute-done.5.other_ref), custom_call_target="tpu_custom_call" | custom-call | bytes 3360 | tf_op jit(solution)/shard_map/pallas_call | solution.py:268
  22.8 1.3 %collective-permute-done.4.refs_3_ = bf16[8,16,640]{2,1,0:T(8,128)(2,1)S(1)} collective-permute-done((bf16[8,16,640]{2,1,0:T(8,128)(2,1)S(1)}, bf16[8,16,640]{2,1,0:T(8,128)(2,1)S(1)}, u32[]{:S(2)}, u32[]{:S(2)}) %collective-permute-start.4) | collective-permute-done | bytes 163872 | tf_op jit(solution)/shard_map/ppermute | solution.py:243
  24.0 1.1 %collective-permute-done.first_ref.own_ref = bf16[210,16,128]{2,1,0:T(8,128)(2,1)S(1)} collective-permute-done((bf16[210,16,128]{2,1,0:T(8,128)(2,1)}, bf16[210,16,128]{2,1,0:T(8,128)(2,1)S(1)}, u32[]{:S(2)}, u32[]{:S(2)}) %collective-permute-start) | collective-permute-done | bytes 860192 | tf_op jit(solution)/shard_map/ppermute | solution.py:239
  26.1 1.7 %collective-permute-start.7 = (bf16[105,16,128]{2,1,0:T(8,128)(2,1)S(1)}, bf16[105,16,128]{2,1,0:T(8,128)(2,1)S(1)}, u32[]{:S(2)}, u32[]{:S(2)}) collective-permute-start(bf16[105,16,128]{2,1,0:T(8,128)(2,1)S(1)} %get-tuple-element.43), channel_id=1, source_target_pairs={{0,8},{4,12},{8,0},{12,4},{16,24},{20,28},{24,16},{28,20},{1,9},{5... | collective-permute-start | bytes 1290248 | tf_op jit(solution)/shard_map/ppermute | solution.py:239
  27.8 1.3 %shard_map.82.refs_4_ = f32[64,2688]{1,0:T(8,128)S(1)} custom-call(bf16[1280,2688]{1,0:T(8,128)(2,1)S(1)} %shard_map.78.w_ref.refs_0_, bf16[8,16,640]{2,1,0:T(8,128)(2,1)S(1)} %get-tuple-element.38.refs_0_, bf16[8,16,640]{2,1,0:T(8,128)(2,1)S(1)} %collective-permute-done.3.refs_1_, bf16[8,16,640]{2,1,0:T(8,128)(2,1)S(1)} %collective-permute-done.2.refs_2_, ...), custom_call_target="tpu_custom_call" | custom-call | flops 107520 | bytes 1680 | tf_op jit(solution)/shard_map/pallas_call | solution.py:278
  29.1 2.4 %shard_map.80.w_ref.refs_1_ = bf16[1280,2688]{1,0:T(8,128)(2,1)S(1)} custom-call(s32[1]{0:T(128)} %bitcast.order_ref.z_ref, s32[1,210]{1,0:T(1,128)S(1)} %copy-done.5, s32[1,210]{1,0:T(1,128)S(1)} %copy-done.6, bf16[210,16,128]{2,1,0:T(8,128)(2,1)S(1)} %collective-permute-done.first_ref.own_ref, bf16[210,16,128]{2,1,0:T(8,128)(2,1)S(1)} %collective-permute-done.8.other_ref), custom_call_target="tpu_custom_call" | custom-call | bytes 3360 | tf_op jit(solution)/shard_map/pallas_call | solution.py:268
  31.5 1.3 %shard_map.83.refs_4_ = f32[64,2688]{1,0:T(8,128)S(1)} custom-call(bf16[1280,2688]{1,0:T(8,128)(2,1)S(1)} %shard_map.80.w_ref.refs_1_, bf16[8,16,640]{2,1,0:T(8,128)(2,1)S(1)} %get-tuple-element.38.refs_0_, bf16[8,16,640]{2,1,0:T(8,128)(2,1)S(1)} %collective-permute-done.3.refs_1_, bf16[8,16,640]{2,1,0:T(8,128)(2,1)S(1)} %collective-permute-done.2.refs_2_, ...), custom_call_target="tpu_custom_call" | custom-call | flops 107520 | bytes 1680 | tf_op jit(solution)/shard_map/pallas_call | solution.py:278
  32.8 2.4 %shard_map.81.w_ref.refs_0_ = bf16[1280,2688]{1,0:T(8,128)(2,1)S(1)} custom-call(s32[1]{0:T(128)} %bitcast.order_ref.z_ref, s32[1,210]{1,0:T(1,128)S(1)} %copy-done.5, s32[1,210]{1,0:T(1,128)S(1)} %copy-done.6, bf16[210,16,128]{2,1,0:T(8,128)(2,1)S(1)} %collective-permute-done.1.second_ref.own_ref, bf16[210,16,128]{2,1,0:T(8,128)(2,1)S(1)} %collective-permute-done.9.other_ref), custom_call_target="tpu_custom_call" | custom-call | bytes 3360 | tf_op jit(solution)/shard_map/pallas_call | solution.py:268
  35.2 1.3 %shard_map.84.early_ref = f32[64,2688]{1,0:T(8,128)S(1)} custom-call(bf16[1280,2688]{1,0:T(8,128)(2,1)S(1)} %shard_map.81.w_ref.refs_0_, bf16[8,16,640]{2,1,0:T(8,128)(2,1)S(1)} %get-tuple-element.38.refs_0_, bf16[8,16,640]{2,1,0:T(8,128)(2,1)S(1)} %collective-permute-done.3.refs_1_, bf16[8,16,640]{2,1,0:T(8,128)(2,1)S(1)} %collective-permute-done.2.refs_2_, ...), custom_call_target="tpu_custom_call" | custom-call | flops 107520 | bytes 1680 | tf_op jit(solution)/shard_map/pallas_call | solution.py:278
  36.5 1.2 %collective-permute-done.6.lower_ref = bf16[105,16,128]{2,1,0:T(8,128)(2,1)S(1)} collective-permute-done((bf16[105,16,128]{2,1,0:T(8,128)(2,1)S(1)}, bf16[105,16,128]{2,1,0:T(8,128)(2,1)S(1)}, u32[]{:S(2)}, u32[]{:S(2)}) %collective-permute-start.6) | collective-permute-done | bytes 430112 | tf_op jit(solution)/shard_map/ppermute | solution.py:239
  38.2 2.0 %shard_map.85 = (bf16[1280,2688]{1,0:T(8,128)(2,1)S(1)}, f32[64,2688]{1,0:T(8,128)S(1)}) custom-call(s32[1]{0:T(128)} %bitcast.order_ref.z_ref, s32[1,210]{1,0:T(1,128)S(1)} %copy-done.5, s32[1,210]{1,0:T(1,128)S(1)} %copy-done.6, bf16[105,16,128]{2,1,0:T(8,128)(2,1)S(1)} %collective-permute-done.6.lower_ref, ...), custom_call_target="tpu_custom_call", output_to_operand_aliasing={{0}: (5, {}), {1}: (6, {})} | custom-call | flops 53760 | bytes 1680 | tf_op jit(solution)/shard_map/pallas_call | solution.py:344
  40.2 3.1 %shard_map.86 = (bf16[1280,2688]{1,0:T(8,128)(2,1)S(1)}, bf16[64,2688]{1,0:T(8,128)(2,1)}, bf16[64,2688]{1,0:T(8,128)(2,1)S(1)}, bf16[64,3968]{1,0:T(8,128)(2,1)...) custom-call(s32[1]{0:T(128)} %bitcast.order_ref.z_ref, ...), custom_call_target="tpu_custom_call", output_to_operand_aliasing={{0}: (8, {})} | custom-call | flops 107520 | bytes 1680 | tf_op jit(solution)/shard_map/pallas_call | solution.py:356
  43.3 1.7 %collective-permute-start.12 = (bf16[64,3968]{1,0:T(8,128)(2,1)S(1)}, bf16[64,3968]{1,0:T(8,128)(2,1)S(1)}, u32[]{:S(2)}, u32[]{:S(2)}) collective-permute-start(bf16[64,3968]{1,0:T(8,128)(2,1)S(1)} %get-tuple-element.63), channel_id=1, source_target_pairs={{0,8},{4,12},{8,0},{12,4},{16,24},{20,28},{24,16},{28,20},{1,9},{5... | collective-permute-start | bytes 1523720 | tf_op jit(solution)/shard_map/ppermute | solution.py:239
  45.0 1.5 %collective-permute-start.16 = (bf16[64,3968]{1,0:T(8,128)(2,1)S(1)}, bf16[64,3968]{1,0:T(8,128)(2,1)S(1)}, u32[]{:S(2)}, u32[]{:S(2)}) collective-permute-start(bf16[64,3968]{1,0:T(8,128)(2,1)S(1)} %get-tuple-element.69), channel_id=1, source_target_pairs={{0,16},{4,20},{8,24},{12,28},{16,0},{20,4},{24,8},{28,12},{1,17},{... | collective-permute-start | bytes 1523720 | tf_op jit(solution)/shard_map/ppermute | solution.py:239
  46.8 3.8 %shard_map.87 = (f32[4,16,1280]{2,1,0:T(8,128)S(1)}, bf16[4,16,1280]{2,1,0:T(8,128)(2,1)S(1)}, bf16[4,16,1280]{2,1,0:T(8,128)(2,1)S(1)}, bf16[4,16,1280]{2,1,0:T(8,128)(2,1)S(1)}) custom-call(bf16[64,2688]{1,0:T(8,128)(2,1)S(1)} %get-tuple-element.55.g_ref, bf16[1280,2688]{1,0:T(8,128)(2,1)S(1)} %shard_map.78.w_ref.refs_0_, ...), custom_call_target="tpu_custom_call" | custom-call | flops 215040 | bytes 3360 | tf_op jit(solution)/shard_map/pallas_call | solution.py:407
  50.6 3.8 %shard_map.88 = (f32[4,16,1280]{2,1,0:T(8,128)S(1)}, bf16[4,16,1280]{2,1,0:T(8,128)(2,1)S(1)}, bf16[4,16,1280]{2,1,0:T(8,128)(2,1)S(1)}, bf16[4,16,1280]{2,1,0:T(8,128)(2,1)S(1)}) custom-call(bf16[64,2688]{1,0:T(8,128)(2,1)S(1)} %get-tuple-element.55.g_ref, ...), custom_call_target="tpu_custom_call", output_to_operand_aliasing={{0}: (3, {}), {1}: (4, {}), {2}: (5, {}), {3}: (6, {})} | custom-call | flops 215040 | bytes 3360 | tf_op jit(solution)/shard_map/pallas_call | solution.py:407
  54.5 2.9 %collective-permute-start.14 = (bf16[4,16,1280]{2,1,0:T(8,128)(2,1)S(1)}, bf16[4,16,1280]{2,1,0:T(8,128)(2,1)S(1)}, u32[]{:S(2)}, u32[]{:S(2)}) collective-permute-start(bf16[4,16,1280]{2,1,0:T(8,128)(2,1)S(1)} %get-tuple-element.65), channel_id=1, source_target_pairs={{0,2},{1,3},{2,0},{3,1},{4,6},{5,7},{6,4},{7,5},{8,10},{9,11},{10,... | collective-permute-start | bytes 491528 | tf_op jit(solution)/shard_map/ppermute | solution.py:243
  57.4 1.3 %collective-permute-start.15 = (bf16[4,16,1280]{2,1,0:T(8,128)(2,1)S(1)}, bf16[4,16,1280]{2,1,0:T(8,128)(2,1)S(1)}, u32[]{:S(2)}, u32[]{:S(2)}) collective-permute-start(bf16[4,16,1280]{2,1,0:T(8,128)(2,1)S(1)} %get-tuple-element.66), channel_id=1, source_target_pairs={{0,3},{1,2},{2,1},{3,0},{4,7},{5,6},{6,5},{7,4},{8,11},{9,10},{10,... | collective-permute-start | bytes 491528 | tf_op jit(solution)/shard_map/ppermute | solution.py:243
  58.7 0.8 %collective-permute-start.13 = (bf16[4,16,1280]{2,1,0:T(8,128)(2,1)S(1)}, bf16[4,16,1280]{2,1,0:T(8,128)(2,1)S(1)}, u32[]{:S(2)}, u32[]{:S(2)}) collective-permute-start(bf16[4,16,1280]{2,1,0:T(8,128)(2,1)S(1)} %get-tuple-element.64), channel_id=1, source_target_pairs={{0,1},{1,0},{2,3},{3,2},{4,5},{5,4},{6,7},{7,6},{8,9},{9,8},{10,11... | collective-permute-start | bytes 491528 | tf_op jit(solution)/shard_map/ppermute | solution.py:243
  59.5 9.6 %collective-permute-done.14.refs_2_ = bf16[4,16,1280]{2,1,0:T(8,128)(2,1)S(1)} collective-permute-done((bf16[4,16,1280]{2,1,0:T(8,128)(2,1)S(1)}, bf16[4,16,1280]{2,1,0:T(8,128)(2,1)S(1)}, u32[]{:S(2)}, u32[]{:S(2)}) %collective-permute-start.14) | collective-permute-done | bytes 163872 | tf_op jit(solution)/shard_map/ppermute | solution.py:243
  69.3 3.9 %shard_map.90 = (f32[210,16,128]{2,1,0:T(8,128)S(1)}, bf16[210,16,128]{2,1,0:T(8,128)(2,1)S(1)}) custom-call(s32[1]{0:T(128)} %bitcast.order_ref.z_ref, s32[1,210]{1,0:T(1,128)S(1)} %copy-done.5, s32[1,210]{1,0:T(1,128)S(1)} %copy-done.6, bf16[64,3968]{1,0:T(8,128)(2,1)S(1)} %get-tuple-element.68.refs_0_, ...), custom_call_target="tpu_custom_call" | custom-call | flops 430080 | bytes 3360 | tf_op jit(solution)/shard_map/pallas_call | solution.py:423
  73.3 1.2 %shard_map.89 = bf16[16,5120]{1,0:T(8,128)(2,1)} custom-call(s32[1]{0:T(128)} %bitcast.2.place_ref, bf16[1024,1024]{1,0:T(8,128)(2,1)S(1)} %copy-done.1, f32[4,16,1280]{2,1,0:T(8,128)S(1)} %get-tuple-element.61.refs_0_, bf16[4,16,1280]{2,1,0:T(8,128)(2,1)S(1)} %collective-permute-done.13.refs_1_, bf16[4,16,1280]{2,1,0:T(8,128)(2,1)S(1)} %collective-permute-done.14.refs_2_, ...), custom_call_target="tpu_custom_call" | custom-call | tf_op jit(solution)/shard_map/pallas_call | solution.py:436
  74.5 1.1 %collective-permute-done.18 = bf16[210,16,128]{2,1,0:T(8,128)(2,1)S(1)} collective-permute-done((bf16[210,16,128]{2,1,0:T(8,128)(2,1)S(1)}, bf16[210,16,128]{2,1,0:T(8,128)(2,1)S(1)}, u32[]{:S(2)}, u32[]{:S(2)}) %collective-permute-start.18) | collective-permute-done | bytes 860192 | tf_op jit(solution)/shard_map/ppermute | solution.py:236
  75.7 1.4 %add_bitcast_fusion = f32[16,210,128]{2,0,1:T(8,128)} fusion(f32[210,16,128]{2,1,0:T(8,128)S(1)} %get-tuple-element.71, bf16[210,16,128]{2,1,0:T(8,128)(2,1)S(1)} %collective-permute-done.18), kind=kLoop, calls=%fused_computation | loop fusion | flops 860160 | bytes 4300800 | tf_op jit(solution)/shard_map/transpose | solution.py:469
  (36 shorter events, 3.5 us)
Async XLA Ops:
  0.6 19.1 %copy-start.2 = (bf16[16,210,128]{2,0,1:T(8,128)(2,1)S(1)}, bf16[16,210,128]{2,0,1:T(8,128)(2,1)}, u32[]{:S(2)}) copy-start(bf16[16,210,128]{2,0,1:T(8,128)(2,1)} %param.6) | copy-start | bytes 2580484
  0.6 19.1 %collective-permute-start.5 = (bf16[210,16,128]{2,1,0:T(8,128)(2,1)}, bf16[210,16,128]{2,1,0:T(8,128)(2,1)}, u32[]{:S(2)}, u32[]{:S(2)}) collective-permute-start(bf16[210,16,128]{2,1,0:T(8,128)(2,1)} %bitcast.5), channel_id=1, source_target_pairs={{0,4},{4,0},{8,12},{12,8},{16,20},{20,16},{24,28},{28,24},{1,5},{5... | collective-permute-start | bytes 2580488 | tf_op jit(solution)/shard_map/ppermute | solution.py:236
  1.2 22.9 %collective-permute-start.1 = (bf16[210,16,128]{2,1,0:T(8,128)(2,1)}, bf16[210,16,128]{2,1,0:T(8,128)(2,1)S(1)}, u32[]{:S(2)}, u32[]{:S(2)}) collective-permute-start(bf16[210,16,128]{2,1,0:T(8,128)(2,1)} %bitcast.6), channel_id=1, source_target_pairs={{0,16},{4,20},{8,24},{12,28},{16,0},{20,4},{24,8},{28,12},{1,17},{... | collective-permute-start | bytes 2580488 | tf_op jit(solution)/shard_map/ppermute | solution.py:239
  3.8 21.4 %collective-permute-start = (bf16[210,16,128]{2,1,0:T(8,128)(2,1)}, bf16[210,16,128]{2,1,0:T(8,128)(2,1)S(1)}, u32[]{:S(2)}, u32[]{:S(2)}) collective-permute-start(bf16[210,16,128]{2,1,0:T(8,128)(2,1)} %bitcast.7), channel_id=1, source_target_pairs={{0,8},{4,12},{8,0},{12,4},{16,24},{20,28},{24,16},{28,20},{1,9},{5... | collective-permute-start | bytes 2580488 | tf_op jit(solution)/shard_map/ppermute | solution.py:239
  5.2 0.9 %copy-start.4 = (bf16[16,5120]{1,0:T(8,128)(2,1)S(1)}, bf16[16,5120]{1,0:T(8,128)(2,1)}, u32[]{:S(2)}) copy-start(bf16[16,5120]{1,0:T(8,128)(2,1)} %tokens_ref.1) | copy-start | bytes 491524
  6.2 13.6 %copy-start.5 = (s32[1,210]{1,0:T(1,128)S(1)}, s32[1,210]{1,0:T(1,128)}, u32[]{:S(2)}) copy-start(s32[1,210]{1,0:T(1,128)} %row_ref.11) | copy-start | bytes 2524
  6.2 13.6 %copy-start.6 = (s32[1,210]{1,0:T(1,128)S(1)}, s32[1,210]{1,0:T(1,128)}, u32[]{:S(2)}) copy-start(s32[1,210]{1,0:T(1,128)} %col_ref.11) | copy-start | bytes 2524
  6.8 1.4 %copy-start = (bf16[1024,1024]{1,0:T(8,128)(2,1)}, bf16[1024,1024]{1,0:T(8,128)(2,1)S(1)}, u32[]{:S(2)}) copy-start(bf16[1024,1024]{1,0:T(8,128)(2,1)S(1)} %get-tuple-element.54.onehot_ref) | copy-start | bytes 6291460
  8.2 10.5 %collective-permute-start.2 = (bf16[8,16,640]{2,1,0:T(8,128)(2,1)S(1)}, bf16[8,16,640]{2,1,0:T(8,128)(2,1)S(1)}, u32[]{:S(2)}, u32[]{:S(2)}) collective-permute-start(bf16[8,16,640]{2,1,0:T(8,128)(2,1)S(1)} %get-tuple-element.38.refs_0_), channel_id=1, source_target_pairs={{0,2},{1,3},{2,0},{3,1},{4,6},{5,7},{6,4},{7,5},{8,10},{9,11},{10,... | collective-permute-start | bytes 491528 | tf_op jit(solution)/shard_map/ppermute | solution.py:243
  10.8 12.0 %collective-permute-start.3 = (bf16[8,16,640]{2,1,0:T(8,128)(2,1)S(1)}, bf16[8,16,640]{2,1,0:T(8,128)(2,1)S(1)}, u32[]{:S(2)}, u32[]{:S(2)}) collective-permute-start(bf16[8,16,640]{2,1,0:T(8,128)(2,1)S(1)} %get-tuple-element.38.refs_0_), channel_id=1, source_target_pairs={{0,1},{1,0},{2,3},{3,2},{4,5},{5,4},{6,7},{7,6},{8,9},{9,8},{10,11... | collective-permute-start | bytes 491528 | tf_op jit(solution)/shard_map/ppermute | solution.py:243
  18.7 5.3 %collective-permute-start.4 = (bf16[8,16,640]{2,1,0:T(8,128)(2,1)S(1)}, bf16[8,16,640]{2,1,0:T(8,128)(2,1)S(1)}, u32[]{:S(2)}, u32[]{:S(2)}) collective-permute-start(bf16[8,16,640]{2,1,0:T(8,128)(2,1)S(1)} %collective-permute-done.2.refs_2_), channel_id=1, source_target_pairs={{0,1},{1,0},{2,3},{3,2},{4,5},{5,4},{6,7},{7,6},{8,9},{9,8},{10,11... | collective-permute-start | bytes 491528 | tf_op jit(solution)/shard_map/ppermute | solution.py:243
  25.2 3.9 %collective-permute-start.8 = (bf16[210,16,128]{2,1,0:T(8,128)(2,1)S(1)}, bf16[210,16,128]{2,1,0:T(8,128)(2,1)S(1)}, u32[]{:S(2)}, u32[]{:S(2)}) collective-permute-start(bf16[210,16,128]{2,1,0:T(8,128)(2,1)S(1)} %collective-permute-done.first_ref.own_ref), channel_id=1, source_target_pairs={{0,4},{4,0},{8,12},{12,8},{16,20},{20,16},{24,28},{28,24},{1,5},{5... | collective-permute-start | bytes 2580488 | tf_op jit(solution)/shard_map/ppermute | solution.py:236
  25.3 7.5 %collective-permute-start.9 = (bf16[210,16,128]{2,1,0:T(8,128)(2,1)S(1)}, bf16[210,16,128]{2,1,0:T(8,128)(2,1)S(1)}, u32[]{:S(2)}, u32[]{:S(2)}) collective-permute-start(bf16[210,16,128]{2,1,0:T(8,128)(2,1)S(1)} %collective-permute-done.1.second_ref.own_ref), channel_id=1, source_target_pairs={{0,4},{4,0},{8,12},{12,8},{16,20},{20,16},{24,28},{28,24},{1,5},{5... | collective-permute-start | bytes 2580488 | tf_op jit(solution)/shard_map/ppermute | solution.py:236
  25.8 11.9 %collective-permute-start.6 = (bf16[105,16,128]{2,1,0:T(8,128)(2,1)S(1)}, bf16[105,16,128]{2,1,0:T(8,128)(2,1)S(1)}, u32[]{:S(2)}, u32[]{:S(2)}) collective-permute-start(bf16[105,16,128]{2,1,0:T(8,128)(2,1)S(1)} %get-tuple-element.42), channel_id=1, source_target_pairs={{0,16},{4,20},{8,24},{12,28},{16,0},{20,4},{24,8},{28,12},{1,17},{... | collective-permute-start | bytes 1290248 | tf_op jit(solution)/shard_map/ppermute | solution.py:239
  26.1 11.6 %collective-permute-start.7 = (bf16[105,16,128]{2,1,0:T(8,128)(2,1)S(1)}, bf16[105,16,128]{2,1,0:T(8,128)(2,1)S(1)}, u32[]{:S(2)}, u32[]{:S(2)}) collective-permute-start(bf16[105,16,128]{2,1,0:T(8,128)(2,1)S(1)} %get-tuple-element.43), channel_id=1, source_target_pairs={{0,8},{4,12},{8,0},{12,4},{16,24},{20,28},{24,16},{28,20},{1,9},{5... | collective-permute-start | bytes 1290248 | tf_op jit(solution)/shard_map/ppermute | solution.py:239
  35.2 5.0 %copy-start.3 = (bf16[64,2688]{1,0:T(8,128)(2,1)S(1)}, bf16[64,2688]{1,0:T(8,128)(2,1)}, u32[]{:S(2)}) copy-start(bf16[64,2688]{1,0:T(8,128)(2,1)} %cotangent_ref.1) | copy-start | bytes 1032196
  37.7 2.5 %collective-permute-start.10 = (bf16[105,16,128]{2,1,0:T(8,128)(2,1)S(1)}, bf16[105,16,128]{2,1,0:T(8,128)(2,1)S(1)}, u32[]{:S(2)}, u32[]{:S(2)}) collective-permute-start(bf16[105,16,128]{2,1,0:T(8,128)(2,1)S(1)} %collective-permute-done.6.lower_ref), channel_id=1, source_target_pairs={{0,4},{4,0},{8,12},{12,8},{16,20},{20,16},{24,28},{28,24},{1,5},{5... | collective-permute-start | bytes 1290248 | tf_op jit(solution)/shard_map/ppermute | solution.py:236
  37.7 2.5 %collective-permute-start.11 = (bf16[105,16,128]{2,1,0:T(8,128)(2,1)S(1)}, bf16[105,16,128]{2,1,0:T(8,128)(2,1)S(1)}, u32[]{:S(2)}, u32[]{:S(2)}) collective-permute-start(bf16[105,16,128]{2,1,0:T(8,128)(2,1)S(1)} %collective-permute-done.7.upper_ref), channel_id=1, source_target_pairs={{0,4},{4,0},{8,12},{12,8},{16,20},{20,16},{24,28},{28,24},{1,5},{5... | collective-permute-start | bytes 1290248 | tf_op jit(solution)/shard_map/ppermute | solution.py:236
  43.3 15.4 %collective-permute-start.12 = (bf16[64,3968]{1,0:T(8,128)(2,1)S(1)}, bf16[64,3968]{1,0:T(8,128)(2,1)S(1)}, u32[]{:S(2)}, u32[]{:S(2)}) collective-permute-start(bf16[64,3968]{1,0:T(8,128)(2,1)S(1)} %get-tuple-element.63), channel_id=1, source_target_pairs={{0,8},{4,12},{8,0},{12,4},{16,24},{20,28},{24,16},{28,20},{1,9},{5... | collective-permute-start | bytes 1523720 | tf_op jit(solution)/shard_map/ppermute | solution.py:239
  45.0 24.3 %collective-permute-start.16 = (bf16[64,3968]{1,0:T(8,128)(2,1)S(1)}, bf16[64,3968]{1,0:T(8,128)(2,1)S(1)}, u32[]{:S(2)}, u32[]{:S(2)}) collective-permute-start(bf16[64,3968]{1,0:T(8,128)(2,1)S(1)} %get-tuple-element.69), channel_id=1, source_target_pairs={{0,16},{4,20},{8,24},{12,28},{16,0},{20,4},{24,8},{28,12},{1,17},{... | collective-permute-start | bytes 1523720 | tf_op jit(solution)/shard_map/ppermute | solution.py:239
  46.5 22.8 %collective-permute-start.17 = (bf16[64,3968]{1,0:T(8,128)(2,1)S(1)}, bf16[64,3968]{1,0:T(8,128)(2,1)S(1)}, u32[]{:S(2)}, u32[]{:S(2)}) collective-permute-start(bf16[64,3968]{1,0:T(8,128)(2,1)S(1)} %get-tuple-element.70), channel_id=1, source_target_pairs={{0,24},{4,28},{8,16},{12,20},{16,8},{20,12},{24,0},{28,4},{1,25},{... | collective-permute-start | bytes 1523720 | tf_op jit(solution)/shard_map/ppermute | solution.py:239
  50.6 22.7 %copy-start.1 = (bf16[1024,1024]{1,0:T(8,128)(2,1)S(1)}, bf16[1024,1024]{1,0:T(8,128)(2,1)}, u32[]{:S(2)}) copy-start(bf16[1024,1024]{1,0:T(8,128)(2,1)} %copy-done) | copy-start | bytes 6291460
  54.5 14.6 %collective-permute-start.14 = (bf16[4,16,1280]{2,1,0:T(8,128)(2,1)S(1)}, bf16[4,16,1280]{2,1,0:T(8,128)(2,1)S(1)}, u32[]{:S(2)}, u32[]{:S(2)}) collective-permute-start(bf16[4,16,1280]{2,1,0:T(8,128)(2,1)S(1)} %get-tuple-element.65), channel_id=1, source_target_pairs={{0,2},{1,3},{2,0},{3,1},{4,6},{5,7},{6,4},{7,5},{8,10},{9,11},{10,... | collective-permute-start | bytes 491528 | tf_op jit(solution)/shard_map/ppermute | solution.py:243
  57.4 11.8 %collective-permute-start.15 = (bf16[4,16,1280]{2,1,0:T(8,128)(2,1)S(1)}, bf16[4,16,1280]{2,1,0:T(8,128)(2,1)S(1)}, u32[]{:S(2)}, u32[]{:S(2)}) collective-permute-start(bf16[4,16,1280]{2,1,0:T(8,128)(2,1)S(1)} %get-tuple-element.66), channel_id=1, source_target_pairs={{0,3},{1,2},{2,1},{3,0},{4,7},{5,6},{6,5},{7,4},{8,11},{9,10},{10,... | collective-permute-start | bytes 491528 | tf_op jit(solution)/shard_map/ppermute | solution.py:243
  58.7 10.6 %collective-permute-start.13 = (bf16[4,16,1280]{2,1,0:T(8,128)(2,1)S(1)}, bf16[4,16,1280]{2,1,0:T(8,128)(2,1)S(1)}, u32[]{:S(2)}, u32[]{:S(2)}) collective-permute-start(bf16[4,16,1280]{2,1,0:T(8,128)(2,1)S(1)} %get-tuple-element.64), channel_id=1, source_target_pairs={{0,1},{1,0},{2,3},{3,2},{4,5},{5,4},{6,7},{7,6},{8,9},{9,8},{10,11... | collective-permute-start | bytes 491528 | tf_op jit(solution)/shard_map/ppermute | solution.py:243
  73.2 2.5 %collective-permute-start.18 = (bf16[210,16,128]{2,1,0:T(8,128)(2,1)S(1)}, bf16[210,16,128]{2,1,0:T(8,128)(2,1)S(1)}, u32[]{:S(2)}, u32[]{:S(2)}) collective-permute-start(bf16[210,16,128]{2,1,0:T(8,128)(2,1)S(1)} %get-tuple-element.72), channel_id=1, source_target_pairs={{0,4},{4,0},{8,12},{12,8},{16,20},{20,16},{24,28},{28,24},{1,5},{5... | collective-permute-start | bytes 2580488 | tf_op jit(solution)/shard_map/ppermute | solution.py:236
